TPU v7x, 32 devices: a whole 2x2x4 slice. The times are simulated.
32 devices in a mesh: ctx: 16 (over z, y, x), mp: 2 (over core).
Axes of the slice: x: 2, y: 2, z: 4, core: 2. Of those that a mesh axis runs over, the one named last changes fastest.
Arguments:
- seq_in: bfloat16 [2048, 8192], P('ctx', 'mp'), may hold values from -6 to 6
- gate_in: bfloat16 [2048, 8192], P('ctx', 'mp'), may hold values from -6 to 6
- upstream: bfloat16 [2048, 8192], P('ctx', 'mp'), may hold values from -6 to 6
- forget_flags: int32 [2048], P('ctx'), may hold values 0 or 1
- conv_weight: float32 [4, 8192], P(None, 'mp'), may hold values from -3 to 3
- conv_bias: float32 [8192], P('mp'), may hold values from -3 to 3
- proj_weight: bfloat16 [8192, 544], P(('mp', 'ctx')), may hold values from -0.0625 to 0.0625
- dt_weight: bfloat16 [512, 8192], P('ctx', 'mp'), may hold values from -0.25 to 0.25
- dt_bias: float32 [8192], P('mp'), may hold values from -10 to -3
- a_log: float32 [16, 8192], P(None, 'mp'), may hold values from 0 to 2.77
- skip_gain: float32 [8192], P('mp'), may hold values from 0.5 to 1.5
Outputs:
- grad_seq: bfloat16 [2048, 8192], P('ctx', 'mp')
- grad_gate: bfloat16 [2048, 8192], P('ctx', 'mp')
- grad_dt_weight: float32 [512, 8192], P('ctx', 'mp')
- grad_conv_weight: float32 [4, 8192], P(None, ('mp', 'ctx'))
- grad_conv_bias: float32 [8192], P(('mp', 'ctx'))
- grad_dt_bias: float32 [8192], P(('mp', 'ctx'))
- grad_a_log: float32 [16, 8192], P(None, ('mp', 'ctx'))
- grad_skip: float32 [8192], P(('mp', 'ctx'))
All inputs are finite; a program needn't handle non-finite values. No bound on the sum of `forget_flags` on one device may be relied on, other than what follows from the above.
Results may differ from a plain program's by a relative error of at most 0.017.
Values may be sent and summed in bfloat16 or wider, within the bound.
No kernel may reach another device: no remote copies, remote signals or barrier semaphores. Data moves between devices by JAX's collectives and lax.ppermute only.
A program may use at most 128 MiB of HBM per device.

v0:
```python
import jax
import jax.numpy as jnp
from jax import lax
from jax.sharding import PartitionSpec as P

STATE = 16
RANK = 512
CONV = 4


def shifted(block, axis, distance):
    devices = range(lax.axis_size(axis))
    route = [(i - distance, i) for i in devices if i - distance in devices]
    return lax.ppermute(block, axis, route)


def prefix(x, axis, combine, identity, reverse):
    count, mine = (lax.axis_size(axis), lax.axis_index(axis))
    everything = jax.tree.map(lambda part: lax.all_gather(part, axis), x)
    start = jax.tree.map(
        lambda part, zero: jnp.broadcast_to(jnp.asarray(zero, part.dtype), part.shape), x, identity
    )

    def step(k, before):
        at = count - 1 - k if reverse else k
        reached = at > mine if reverse else at < mine
        new = combine(before, jax.tree.map(lambda part: part[at], everything))
        return jax.tree.map(lambda a, b: jnp.where(reached, a, b), new, before)

    return lax.fori_loop(0, count, step, start)


def to_blocks(arrays):
    return tuple((a.reshape((a.shape[0] // 16, 16) + a.shape[1:]) for a in arrays))


def block_closed(carry, inputs):
    state, a_matrix = carry
    act_blk, step_blk, b_blk, c_blk = inputs
    rows = step_blk.shape[0]
    cumul = jnp.cumsum(step_blk[:, None, :] * a_matrix[None], axis=0)
    later_rows = lax.broadcasted_iota(jnp.int32, (rows, rows), 0)
    early_rows = lax.broadcasted_iota(jnp.int32, (rows, rows), 1)
    lower = (later_rows >= early_rows)[:, :, None, None]
    gaps = jnp.where(lower, cumul[:, None] - cumul[None, :], 0.0)
    weights = jnp.where(lower, jnp.exp(gaps), 0.0)
    inflow = b_blk[:, :, None] * (step_blk * act_blk)[:, None, :]
    states = jnp.exp(cumul) * state[None] + jnp.sum(weights * inflow[None], axis=1)
    outputs = jnp.sum(c_blk[:, :, None] * states, axis=1)
    return ((states[-1], a_matrix), outputs)


def scan_tokens(act_full, step_size, b_matrix, c_matrix, log_rates, skip):
    a_matrix = -jnp.exp(log_rates)
    length = act_full.shape[0]
    start_state = jnp.zeros(log_rates.shape, jnp.float32)
    carry, outputs = lax.scan(
        jax.checkpoint(block_closed),
        (start_state, a_matrix),
        to_blocks((act_full, step_size, b_matrix, c_matrix)),
    )
    return (outputs.reshape(length, -1) + skip[None, :] * act_full, carry[0])


def carry_block(carry, inputs):
    state, a_matrix = carry
    step_blk, c_blk = inputs
    cumul = jnp.cumsum(step_blk[:, None, :] * a_matrix[None], axis=0)
    states = jnp.exp(cumul) * state[None]
    return ((states[-1], a_matrix), jnp.sum(c_blk[:, :, None] * states, axis=1))


def carry_in(step_size, c_matrix, log_rates, state_in):
    a_matrix = -jnp.exp(log_rates)
    length = step_size.shape[0]
    carry, outputs = lax.scan(
        jax.checkpoint(carry_block), (state_in, a_matrix), to_blocks((step_size, c_matrix))
    )
    return (outputs.reshape(length, -1), carry[0])


def compose(earlier, later):
    return (earlier[0] * later[0], later[0] * earlier[1] + later[1])


def body(
    seq_in,
    gate_in,
    upstream,
    forget_flags,
    conv_weight,
    conv_bias,
    proj_weight,
    dt_weight,
    dt_bias,
    a_log,
    skip_gain,
):
    length = seq_in.shape[0]
    rim_rows = CONV - 1
    from_left = shifted(seq_in[length - rim_rows :], "ctx", 1)
    padded = jnp.concatenate([from_left, seq_in], axis=0)
    pre_act = jnp.zeros(seq_in.shape, jnp.float32) + conv_bias[None, :]
    for k in range(CONV):
        pre_act = pre_act + conv_weight[k][None, :] * padded[k : k + length]
    act_half = jax.nn.silu(pre_act).astype(jnp.bfloat16)
    rows_proj, rows_dt = (
        lax.all_gather(proj_weight, "ctx", axis=0, tiled=True),
        lax.all_gather(dt_weight, "ctx", axis=0, tiled=True),
    )
    partial_proj = jnp.dot(act_half, rows_proj, preferred_element_type=jnp.float32)
    projected = lax.psum(partial_proj, "mp")
    dt_low = projected[:, :RANK].astype(jnp.bfloat16)
    b_matrix = projected[:, RANK : RANK + STATE]
    c_matrix = projected[:, RANK + STATE :]
    dt_pre = jnp.dot(dt_low, rows_dt, preferred_element_type=jnp.float32) + dt_bias[None, :]
    step_size = jax.nn.softplus(dt_pre)
    a_matrix = -jnp.exp(a_log)
    act_full = act_half.astype(jnp.float32)
    (mixed_local, state_end), pull_local = jax.vjp(
        scan_tokens, act_full, step_size, b_matrix, c_matrix, a_log, skip_gain
    )
    zeros_state = jnp.zeros_like(state_end)
    step_totals = jnp.sum(step_size, axis=0)
    decays = jnp.exp(a_matrix * step_totals[None, :])
    state_in = prefix(
        (decays, state_end), "ctx", compose, (jnp.ones_like(decays), zeros_state), False
    )[1]
    (mixed_carry, unused_end), pull_carry = jax.vjp(carry_in, step_size, c_matrix, a_log, state_in)
    mixed = mixed_local + mixed_carry
    flag_values = forget_flags.astype(jnp.float32)
    grad_out = -flag_values[:, None] * upstream.astype(jnp.float32)
    gate_full = gate_in.astype(jnp.float32)
    gate_sigmoid = jax.nn.sigmoid(gate_full)
    grad_mixed = grad_out * (gate_full * gate_sigmoid)
    grad_gate = (
        grad_out * mixed * (gate_sigmoid * (1.0 + gate_full * (1.0 - gate_sigmoid)))
    ).astype(jnp.bfloat16)
    local_adjoint = pull_carry((grad_mixed, zeros_state))[3]
    adjoint_out = prefix(
        (decays, local_adjoint), "ctx", compose, (jnp.ones_like(decays), zeros_state), True
    )[1]
    grad_act_scan, grad_step, grad_bmat, grad_cmat, grad_rate, grad_skip = pull_local(
        (grad_mixed, adjoint_out)
    )
    extra_step, extra_cmat, extra_rate, unused_in = pull_carry((grad_mixed, adjoint_out))
    grad_step = grad_step + extra_step
    grad_cmat = grad_cmat + extra_cmat
    grad_rate = grad_rate + extra_rate
    grad_pre = grad_step * jax.nn.sigmoid(dt_pre)
    grad_pre_half = grad_pre.astype(jnp.bfloat16)
    grad_dtw = lax.dot_general(
        dt_low, grad_pre_half, (((0,), (0,)), ((), ())), preferred_element_type=jnp.float32
    )
    grad_low = lax.dot_general(
        grad_pre_half, rows_dt, (((1,), (1,)), ((), ())), preferred_element_type=jnp.float32
    )
    grad_proj = lax.psum(
        jnp.concatenate([grad_low, grad_bmat, grad_cmat], axis=1).astype(jnp.bfloat16), "mp"
    )
    grad_from_proj = lax.dot_general(
        grad_proj, rows_proj, (((1,), (1,)), ((), ())), preferred_element_type=jnp.float32
    )
    act_sigmoid = jax.nn.sigmoid(pre_act)
    grad_pre_act = (grad_act_scan + grad_from_proj) * (
        act_sigmoid * (1.0 + pre_act * (1.0 - act_sigmoid))
    )
    from_next = shifted(grad_pre_act[:rim_rows], "ctx", -1)
    grad_padded = jnp.concatenate([grad_pre_act, from_next], axis=0)
    grad_seq = jnp.zeros(seq_in.shape, jnp.float32)
    for k in range(CONV):
        grad_seq = (
            grad_seq + conv_weight[k][None, :] * grad_padded[rim_rows - k : rim_rows - k + length]
        )
    grad_conv_w = jnp.stack(
        [jnp.sum(grad_pre_act * padded[k : k + length], axis=0) for k in range(CONV)]
    )
    grad_conv_b = jnp.sum(grad_pre_act, axis=0)
    grad_dt_b = jnp.sum(grad_pre, axis=0)
    summed_grads = (
        lax.psum_scatter(grad_dtw, "ctx", scatter_dimension=0, tiled=True),
        lax.psum_scatter(grad_conv_w, "ctx", scatter_dimension=1, tiled=True),
        lax.psum_scatter(grad_conv_b, "ctx", scatter_dimension=0, tiled=True),
        lax.psum_scatter(grad_dt_b, "ctx", scatter_dimension=0, tiled=True),
        lax.psum_scatter(grad_rate, "ctx", scatter_dimension=1, tiled=True),
        lax.psum_scatter(grad_skip, "ctx", scatter_dimension=0, tiled=True),
    )
    return (grad_seq.astype(jnp.bfloat16), grad_gate) + tuple(summed_grads)


def solution(mesh):
    return jax.shard_map(
        body,
        mesh=mesh,
        in_specs=(
            P("ctx", "mp"),
            P("ctx", "mp"),
            P("ctx", "mp"),
            P("ctx"),
            P(None, "mp"),
            P("mp"),
            P(("mp", "ctx"), None),
            P("ctx", "mp"),
            P("mp"),
            P(None, "mp"),
            P("mp"),
        ),
        out_specs=(
            P("ctx", "mp"),
            P("ctx", "mp"),
            P("ctx", "mp"),
            P(None, ("mp", "ctx")),
            P(("mp", "ctx")),
            P(("mp", "ctx")),
            P(None, ("mp", "ctx")),
            P(("mp", "ctx")),
        ),
        check_vma=False,
    )
```

profile of v0, /device:TPU:14, one launch (start us, length us, event | category | flops | bytes accessed | tf_op | source)
XLA Modules:
  0.0 1859.0 jit_solution(5645868681700251075)
XLA Ops:
  21.0 78.1 %all-gather.9.cloned.1.call-done = bf16[4096,544]{0,1:T(8,128)(2,1)} async-done(((bf16[256,544]{0,1:T(8,128)(2,1)}), bf16[4096,544]{0,1:T(8,128)(2,1)}) %all-gather.9.cloned.1.call-update) | async-done | bytes 4456464 | tf_op jit(solution)/shard_map/all_gather | solution.py:108
  124.3 78.3 %all-gather.11.cloned.1.call-done = bf16[512,4096]{1,0:T(8,128)(2,1)} async-done(((bf16[32,4096]{1,0:T(8,128)(2,1)}), bf16[512,4096]{1,0:T(8,128)(2,1)}) %all-gather.11.cloned.1.call-update) | async-done | bytes 4194320 | tf_op jit(solution)/shard_map/all_gather | solution.py:109
  214.2 304.1 %while.128 = (s32[]{:T(128)}, f32[16,4096]{1,0:T(8,128)S(1)}, f32[8,16,4096]{2,1,0:T(8,128)}, f32[8,16,4096]{2,1,0:T(8,128)}, f32[8,16,4096]{2,1,0:T(8,128)}, /*...) while((s32[]{:T(128)}, f32[16,4096]{1,0:T(8,128)S(1)}, ...), condition=%wide.region_6.7_spmd.clone.clone, body=%wide.region_2.6_spmd.clone.clone.sunk | while | flops 104857600 | bytes 38280576 | solution.py:57
  221.0 24.7 %multiply_reduce_fusion.25 = f32[16,16,4096]{2,1,0:T(8,128)} fusion(f32[16,16,4096]{2,1,0:T(8,128)} %broadcast_multiply_fusion.4, f32[16,16,4096]{2,1,0:T(8,128)} %fusion.101, pred[16,16]{1,0:T(8,128)(4,1)S(1)} %get-tuple-element.2082), kind=kLoop, calls=%fused_computation.22.clone.1 | loop fusion | flops 82837504 | bytes 12583168 | tf_op jit(solution)/shard_map/jvp()/while/body/eval_jaxpr/reduce_sum | solution.py:48
  259.0 24.7 %multiply_reduce_fusion.25 = f32[16,16,4096]{2,1,0:T(8,128)} fusion(f32[16,16,4096]{2,1,0:T(8,128)} %broadcast_multiply_fusion.4, f32[16,16,4096]{2,1,0:T(8,128)} %fusion.101, pred[16,16]{1,0:T(8,128)(4,1)S(1)} %get-tuple-element.2082), kind=kLoop, calls=%fused_computation.22.clone.1 | loop fusion | flops 82837504 | bytes 12583168 | tf_op jit(solution)/shard_map/jvp()/while/body/eval_jaxpr/reduce_sum | solution.py:48
  297.0 24.7 %multiply_reduce_fusion.25 = f32[16,16,4096]{2,1,0:T(8,128)} fusion(f32[16,16,4096]{2,1,0:T(8,128)} %broadcast_multiply_fusion.4, f32[16,16,4096]{2,1,0:T(8,128)} %fusion.101, pred[16,16]{1,0:T(8,128)(4,1)S(1)} %get-tuple-element.2082), kind=kLoop, calls=%fused_computation.22.clone.1 | loop fusion | flops 82837504 | bytes 12583168 | tf_op jit(solution)/shard_map/jvp()/while/body/eval_jaxpr/reduce_sum | solution.py:48
  335.1 24.7 %multiply_reduce_fusion.25 = f32[16,16,4096]{2,1,0:T(8,128)} fusion(f32[16,16,4096]{2,1,0:T(8,128)} %broadcast_multiply_fusion.4, f32[16,16,4096]{2,1,0:T(8,128)} %fusion.101, pred[16,16]{1,0:T(8,128)(4,1)S(1)} %get-tuple-element.2082), kind=kLoop, calls=%fused_computation.22.clone.1 | loop fusion | flops 82837504 | bytes 12583168 | tf_op jit(solution)/shard_map/jvp()/while/body/eval_jaxpr/reduce_sum | solution.py:48
  519.9 74.0 %all-gather.15.cloned.1.call-done = f32[256,4096]{1,0:T(8,128)} async-done(((f32[16,4096]{1,0:T(8,128)}), f32[256,4096]{1,0:T(8,128)}) %all-gather.15.cloned.1.call-update) | async-done | bytes 4194320 | tf_op jit(solution)/shard_map/all_gather | solution.py:19
  593.9 78.3 %all-gather.13.cloned.1.call-done = f32[256,4096]{1,0:T(8,128)} async-done(((f32[16,4096]{1,0:T(8,128)}), f32[256,4096]{1,0:T(8,128)}) %all-gather.13.cloned.1.call-update) | async-done | bytes 4194320 | tf_op jit(solution)/shard_map/all_gather | solution.py:19
  697.2 32.9 %while.126 = (s32[]{:T(128)}, f32[16,4096]{1,0:T(8,128)S(1)}, f32[8,16,4096]{2,1,0:T(8,128)}, f32[8,16,4096]{2,1,0:T(8,128)}, f32[8,16,4096]{2,1,0:T(8,128)}, /*...) while((s32[]{:T(128)}, f32[16,4096]{1,0:T(8,128)S(1)}, ...), condition=%wide.region_12.13_spmd, body=%wide.region_9.12_spmd.sunk | while | flops 19857408 | bytes 7868517 | solution.py:76
  756.6 73.5 %all-gather.17.cloned.1.call-done = f32[256,4096]{1,0:T(8,128)} async-done(((f32[16,4096]{1,0:T(8,128)}), f32[256,4096]{1,0:T(8,128)}) %all-gather.17.cloned.1.call-update) | async-done | bytes 4194320 | tf_op jit(solution)/shard_map/all_gather | solution.py:19
  852.3 65.9 %while.132 = (s32[]{:T(128)}, f32[16,4096]{1,0:T(8,128)S(1)}, f32[16,4096]{1,0:T(8,128)S(1)}, f32[8,16,4096]{2,1,0:T(8,128)}, f32[8,16,16]{2,1,0:T(8,128)S(1)}, ...) while((s32[]{:T(128)}, f32[16,4096]{1,0:T(8,128)S(1)}, ...), condition=%wide.region_40.41_spmd.clone, body=%wide.region_33.40_spmd.clone.sunk | while | flops 48168708 | bytes 16274599 | solution.py:76
  922.0 547.9 %while.131 = (s32[]{:T(128)}, f32[16,4096]{1,0:T(8,128)S(1)}, f32[16,4096]{1,0:T(8,128)S(1)}, f32[8,16,4096]{2,1,0:T(8,128)}, f32[8,16,4096]{2,1,0:T(8,128)}, /*...) while((s32[]{:T(128)}, f32[16,4096]{1,0:T(8,128)S(1)}, ...), condition=%wide.region_32.33_spmd.clone, body=%wide.region_19.32_spmd.clone.sunk | while | flops 273809152 | bytes 79717088 | solution.py:57
  927.5 46.5 %fusion.106 = (f32[16,16,4096]{2,1,0:T(8,128)}, f32[16,16,4096]{2,1,0:T(8,128)}, f32[16,16,4096]{2,1,0:T(8,128)}, f32[16,16,4096]{2,1,0:T(8,128)S(1)}) fusion(f32[16,16,4096]{2,1,0:T(8,128)S(1)} %fusion.105, f32[16,16,4096]{2,1,0:T(8,128)S(1)} %broadcast_multiply_fusion.5, f32[16,16,4096]{2,1,0:T(8,128)S(1)} %multiply_add_fusion.5, ...), kind=kLoop, calls=%fused_computation.50.clone.1 | loop fusion | flops 213909504 | bytes 29360384 | tf_op jit(solution)/shard_map/transpose(jvp())/while/body/eval_jaxpr/checkpoint/reduce_sum | solution.py:45
  996.0 46.5 %fusion.106 = (f32[16,16,4096]{2,1,0:T(8,128)}, f32[16,16,4096]{2,1,0:T(8,128)}, f32[16,16,4096]{2,1,0:T(8,128)}, f32[16,16,4096]{2,1,0:T(8,128)S(1)}) fusion(f32[16,16,4096]{2,1,0:T(8,128)S(1)} %fusion.105, f32[16,16,4096]{2,1,0:T(8,128)S(1)} %broadcast_multiply_fusion.5, f32[16,16,4096]{2,1,0:T(8,128)S(1)} %multiply_add_fusion.5, ...), kind=kLoop, calls=%fused_computation.50.clone.1 | loop fusion | flops 213909504 | bytes 29360384 | tf_op jit(solution)/shard_map/transpose(jvp())/while/body/eval_jaxpr/checkpoint/reduce_sum | solution.py:45
  1064.4 46.5 %fusion.106 = (f32[16,16,4096]{2,1,0:T(8,128)}, f32[16,16,4096]{2,1,0:T(8,128)}, f32[16,16,4096]{2,1,0:T(8,128)}, f32[16,16,4096]{2,1,0:T(8,128)S(1)}) fusion(f32[16,16,4096]{2,1,0:T(8,128)S(1)} %fusion.105, f32[16,16,4096]{2,1,0:T(8,128)S(1)} %broadcast_multiply_fusion.5, f32[16,16,4096]{2,1,0:T(8,128)S(1)} %multiply_add_fusion.5, ...), kind=kLoop, calls=%fused_computation.50.clone.1 | loop fusion | flops 213909504 | bytes 29360384 | tf_op jit(solution)/shard_map/transpose(jvp())/while/body/eval_jaxpr/checkpoint/reduce_sum | solution.py:45
  1132.8 46.5 %fusion.106 = (f32[16,16,4096]{2,1,0:T(8,128)}, f32[16,16,4096]{2,1,0:T(8,128)}, f32[16,16,4096]{2,1,0:T(8,128)}, f32[16,16,4096]{2,1,0:T(8,128)S(1)}) fusion(f32[16,16,4096]{2,1,0:T(8,128)S(1)} %fusion.105, f32[16,16,4096]{2,1,0:T(8,128)S(1)} %broadcast_multiply_fusion.5, f32[16,16,4096]{2,1,0:T(8,128)S(1)} %multiply_add_fusion.5, ...), kind=kLoop, calls=%fused_computation.50.clone.1 | loop fusion | flops 213909504 | bytes 29360384 | tf_op jit(solution)/shard_map/transpose(jvp())/while/body/eval_jaxpr/checkpoint/reduce_sum | solution.py:45
  1201.3 46.5 %fusion.106 = (f32[16,16,4096]{2,1,0:T(8,128)}, f32[16,16,4096]{2,1,0:T(8,128)}, f32[16,16,4096]{2,1,0:T(8,128)}, f32[16,16,4096]{2,1,0:T(8,128)S(1)}) fusion(f32[16,16,4096]{2,1,0:T(8,128)S(1)} %fusion.105, f32[16,16,4096]{2,1,0:T(8,128)S(1)} %broadcast_multiply_fusion.5, f32[16,16,4096]{2,1,0:T(8,128)S(1)} %multiply_add_fusion.5, ...), kind=kLoop, calls=%fused_computation.50.clone.1 | loop fusion | flops 213909504 | bytes 29360384 | tf_op jit(solution)/shard_map/transpose(jvp())/while/body/eval_jaxpr/checkpoint/reduce_sum | solution.py:45
  1269.7 46.5 %fusion.106 = (f32[16,16,4096]{2,1,0:T(8,128)}, f32[16,16,4096]{2,1,0:T(8,128)}, f32[16,16,4096]{2,1,0:T(8,128)}, f32[16,16,4096]{2,1,0:T(8,128)S(1)}) fusion(f32[16,16,4096]{2,1,0:T(8,128)S(1)} %fusion.105, f32[16,16,4096]{2,1,0:T(8,128)S(1)} %broadcast_multiply_fusion.5, f32[16,16,4096]{2,1,0:T(8,128)S(1)} %multiply_add_fusion.5, ...), kind=kLoop, calls=%fused_computation.50.clone.1 | loop fusion | flops 213909504 | bytes 29360384 | tf_op jit(solution)/shard_map/transpose(jvp())/while/body/eval_jaxpr/checkpoint/reduce_sum | solution.py:45
  1338.2 46.5 %fusion.106 = (f32[16,16,4096]{2,1,0:T(8,128)}, f32[16,16,4096]{2,1,0:T(8,128)}, f32[16,16,4096]{2,1,0:T(8,128)}, f32[16,16,4096]{2,1,0:T(8,128)S(1)}) fusion(f32[16,16,4096]{2,1,0:T(8,128)S(1)} %fusion.105, f32[16,16,4096]{2,1,0:T(8,128)S(1)} %broadcast_multiply_fusion.5, f32[16,16,4096]{2,1,0:T(8,128)S(1)} %multiply_add_fusion.5, ...), kind=kLoop, calls=%fused_computation.50.clone.1 | loop fusion | flops 213909504 | bytes 29360384 | tf_op jit(solution)/shard_map/transpose(jvp())/while/body/eval_jaxpr/checkpoint/reduce_sum | solution.py:45
  1406.6 46.5 %fusion.106 = (f32[16,16,4096]{2,1,0:T(8,128)}, f32[16,16,4096]{2,1,0:T(8,128)}, f32[16,16,4096]{2,1,0:T(8,128)}, f32[16,16,4096]{2,1,0:T(8,128)S(1)}) fusion(f32[16,16,4096]{2,1,0:T(8,128)S(1)} %fusion.105, f32[16,16,4096]{2,1,0:T(8,128)S(1)} %broadcast_multiply_fusion.5, f32[16,16,4096]{2,1,0:T(8,128)S(1)} %multiply_add_fusion.5, ...), kind=kLoop, calls=%fused_computation.50.clone.1 | loop fusion | flops 213909504 | bytes 29360384 | tf_op jit(solution)/shard_map/transpose(jvp())/while/body/eval_jaxpr/checkpoint/reduce_sum | solution.py:45
  1524.3 59.1 %all-reduce.6 = (f32[4096]{0:T(1024)S(1)}, f32[4096]{0:T(1024)S(1)}, f32[4096]{0:T(1024)S(1)}) all-reduce(f32[4096]{0:T(1024)S(1)} %get-tuple-element.1399, f32[4096]{0:T(1024)S(1)} %get-tuple-element.1526, f32[4096]{0:T(1024)S(1)} %copy-done.32), channel_id=7, replica_groups=mesh['ctx'=16,'mp'=2] {'ctx'}, use_global_device_ids=true, to_apply=%region_49.50.clone | all-reduce | flops 12288 | bytes 98304
  1586.9 72.2 %reduce-scatter.8.cloned.1.call-done = f32[16,256]{1,0:T(8,128)} async-done(((f32[16,4096]{1,0:T(8,128)}), f32[16,256]{1,0:T(8,128)}) %reduce-scatter.8.cloned.1.call-update) | async-done | bytes 16400 | tf_op jit(solution)/shard_map/reduce_scatter | solution.py:185
  1659.1 192.6 %reduce-scatter.6.cloned.1.call-done = f32[32,4096]{1,0:T(8,128)} async-done(((f32[512,4096]{1,0:T(8,128)}), f32[32,4096]{1,0:T(8,128)}) %reduce-scatter.6.cloned.1.call-update) | async-done | bytes 524304 | tf_op jit(solution)/shard_map/reduce_scatter | solution.py:181
  (591 shorter events, 728.1 us)
Async XLA Ops:
  7.2 92.0 %all-gather.9.cloned.1.call-start = ((), (), s32[]{:S(2)}) async-start(), calls=%async_computation.3 | async-start | bytes 4734976 | tf_op jit(solution)/shard_map/all_gather | solution.py:108
  7.9 115.5 %all-reduce.10.cloned.1.call-start = ((), (), s32[]{:S(2)}) async-start(), calls=%async_computation.4 | async-start | bytes 557056 | tf_op jit(solution)/shard_map/psum | solution.py:112
  8.8 5.8 collective-permute-start
  103.7 98.9 %copy-start.33 = (f32[4096]{0:T(1024)S(1)}, f32[4096]{0:T(1024)}, u32[]{:S(2)}) copy-start(f32[4096]{0:T(1024)} %param.33) | copy-start | bytes 49156
  103.8 98.9 %all-gather.11.cloned.1.call-start = ((), (), s32[]{:S(2)}) async-start(), calls=%async_computation.5 | async-start | bytes 4456448 | tf_op jit(solution)/shard_map/all_gather | solution.py:109
  104.5 489.4 %all-gather.15.cloned.1.call-start = ((), (), s32[]{:S(2)}) async-start(), calls=%async_computation.10 | async-start | bytes 4456448 | tf_op jit(solution)/shard_map/all_gather | solution.py:19
  124.3 84.4 %copy-start.16 = (f32[16,4096]{1,0:T(8,128)S(1)}, f32[16,4096]{1,0:T(8,128)}, u32[]{:S(2)}) copy-start(f32[16,4096]{1,0:T(8,128)} %param.34) | copy-start | bytes 786436
  519.1 153.1 %all-gather.13.cloned.1.call-start = ((), (), s32[]{:S(2)}) async-start(), calls=%async_computation.9 | async-start | bytes 4456448 | tf_op jit(solution)/shard_map/all_gather | solution.py:19
  519.7 310.5 %all-gather.17.cloned.1.call-start = ((), (), s32[]{:S(2)}) async-start(), calls=%async_computation.11 | async-start | bytes 4456448 | tf_op jit(solution)/shard_map/all_gather | solution.py:19
  756.0 739.8 %all-reduce.12.cloned.1.call-start = ((), (), s32[]{:S(2)}) async-start(), calls=%async_computation.6 | async-start | bytes 327680 | tf_op jit(solution)/shard_map/psum | solution.py:158
  986.2 4.3 copy-start.8
  1054.7 4.3 copy-start.8
  1328.4 4.3 copy-start.8
  1477.9 107.4 %reduce-scatter.10.cloned.1.call-start = ((), (), s32[]{:S(2)}) async-start(), calls=%async_computation.12 | async-start | bytes 2228224
  1477.9 17.8 copy-start.22
  1478.0 17.8 copy-start.24
  1478.0 17.8 copy-start.26
  1478.0 17.8 copy-start.28
  1478.0 17.8 copy-start.30
  1478.0 17.8 copy-start.35
  1495.8 15.1 copy-start.14
  1502.9 8.0 collective-permute-start.1
  1516.6 142.5 %reduce-scatter.8.cloned.1.call-start = ((), (), s32[]{:S(2)}) async-start(), calls=%async_computation.8 | async-start | bytes 278528 | tf_op jit(solution)/shard_map/reduce_scatter | solution.py:185
  1517.5 334.2 %reduce-scatter.6.cloned.1.call-start = ((), (), s32[]{:S(2)}) async-start(), calls=%async_computation.7 | async-start | bytes 8912896 | tf_op jit(solution)/shard_map/reduce_scatter | solution.py:181
  (34 other events, 73.8 us)
Sparse Core Ops, SparseCore 0:
  10.7 88.3 all-gather.8
  103.9 19.4 all-reduce.9
  126.6 76.0 all-gather.10
  519.2 74.6 all-gather.14
  597.5 74.6 all-gather.12
  755.4 74.6 all-gather.16
  1478.0 17.7 all-reduce.11
  1516.7 68.5 reduce-scatter.9
  1588.2 70.8 reduce-scatter.7
  1661.8 189.8 reduce-scatter.5
where the time goes:
time: 1870 us; the launch traced here: 1860 us
  other arithmetic  923 us (49%)
  waiting for transfers between devices  682 us (36%)
  local copies, waits for them, and re-layouts  145 us (8%)
  blocking collectives  59.1 us (3%)
  matrix products  23.7 us (1%)
    reduce_sum x8, other arithmetic, block_closed(): gaps = jnp.where(lower, cumul[:, None] - cumul[None, :], 0.0)  372 us
    all_gather x3, waiting for transfers between devices, prefix(): everything = jax.tree.map(lambda part: lax.all_gather(part, axis), x)  226 us
    reduce_sum x8, other arithmetic, block_closed(): jnp.sum(weights * inflow[None], axis=1)  197 us
    reduce_scatter x1, waiting for transfers between devices, body(): lax.psum_scatter(grad_dtw, 'ctx', scatter_dimension=0, tiled=True)  193 us
    another operation x24, other arithmetic, block_closed(): cumul = jnp.cumsum(step_blk[:, None, :] * a_matrix[None], axis=0)  83.7 us
    all_gather x1, waiting for transfers between devices, body(): lax.all_gather(dt_weight, 'ctx', axis=0, tiled=True)  78.3 us
    all_gather x1, waiting for transfers between devices, body(): lax.all_gather(proj_weight, 'ctx', axis=0, tiled=True)  78.1 us
    reduce_scatter x1, waiting for transfers between devices, body(): lax.psum_scatter(grad_rate, 'ctx', scatter_dimension=1, tiled=True)  72.2 us
  transfers between devices with their start and end apart: 12, of which 11 were waited for; matrix products, arithmetic and copies ran while one was open for 2% of the time, Pallas kernels for 0%

commit v1 on v0

v1 whole, which is shorter than its diff:
```python
import functools
import jax
import jax.numpy as jnp
from jax import lax
from jax.experimental import pallas as pl
from jax.experimental.pallas import tpu as pltpu
from jax.sharding import PartitionSpec as P

STATE = 16
RANK = 512
CONV = 4
PLANE = 4
LANES = 128
GROUP = 8
UNROLL = 4
BLOCK = 32
LOG2E = 1.4426950408889634
LN2 = 0.6931471805599453
VMEM_LIMIT = 58 * 1024 * 1024
F32 = jnp.float32
BF16 = jnp.bfloat16


def row_sums(parts):
    parts = [
        functools.reduce(jnp.add, [p[r : r + 8] for r in range(0, p.shape[0], 8)]) for p in parts
    ]
    row = lax.broadcasted_iota(jnp.int32, (8, LANES), 0)
    low = row < 4
    halves = [
        jnp.where(low, parts[k], parts[k + 4])
        + pltpu.roll(jnp.where(low, parts[k + 4], parts[k]), 4, 0)
        for k in range(4)
    ]
    second = (row & 2) == 0
    quarters = [
        jnp.where(
            second,
            halves[k] + pltpu.roll(halves[k], 6, 0),
            halves[k + 2] + pltpu.roll(halves[k + 2], 2, 0),
        )
        for k in range(2)
    ]
    return jnp.where(
        (row & 1) == 0,
        quarters[0] + pltpu.roll(quarters[0], 7, 0),
        quarters[1] + pltpu.roll(quarters[1], 1, 0),
    )


def local_kernel(b, c, low, dtw, dtb, act, g, alog, step_out, sig_out, ends_out, a2, us, gs):
    tokens, width = act.shape
    rows = width // LANES
    block = min(tokens, BLOCK)
    a2[...] = (-LOG2E * jnp.exp(alog[...])).reshape(STATE, rows, LANES)

    for column in range(0, width, 256):
        columns = slice(column, column + 256)
        sig_out[:, columns] = jnp.dot(low[...], dtw[:, columns], preferred_element_type=F32)

    def prepare(i, total):
        at = pl.ds(pl.multiple_of(i * block, block), block)
        pre = sig_out[at, :] + dtb[...]
        tail = jnp.exp(-jnp.abs(pre))
        step = jnp.maximum(pre, 0.0) + jnp.log1p(tail)
        sig_out[at, :] = jnp.where(pre >= 0.0, 1.0, tail) / (1.0 + tail)
        step_out[at] = step.reshape(block, rows, LANES)
        us[at] = (step * act[at, :].astype(F32)).reshape(block, rows, LANES)
        gs[at] = g[at, :].astype(F32).reshape(block, rows, LANES)
        return total + jnp.sum(step, axis=0, keepdims=True)

    ends_out[2 * STATE : 2 * STATE + 1, :] = lax.fori_loop(
        0, tokens // block, prepare, jnp.zeros((1, width), F32)
    )
    zeros = jnp.zeros((8, LANES), F32)
    ones = jnp.ones((8, LANES), F32)
    for r in range(0, rows, 8):
        part = slice(r, r + 8)
        for base in range(0, STATE, GROUP):

            def move(t, carry):
                h, p, lam = carry
                s, u, g_now = step_out[t, part, :], us[t, part, :], gs[t, part, :]
                h, p, lam = list(h), list(p), list(lam)
                for k in range(GROUP):
                    n = base + k
                    d = jnp.exp2(s * a2[n, part, :])
                    h[k] = d * h[k] + b[t, n : n + 1, :] * u
                    p[k] = d * p[k]
                    lam[k] = lam[k] + (c[t, n : n + 1, :] * g_now) * p[k]
                return tuple(h), tuple(p), tuple(lam)

            h, _, lam = lax.fori_loop(
                0, tokens, move, ((zeros,) * GROUP, (ones,) * GROUP, (zeros,) * GROUP),
                unroll=UNROLL,
            )
            columns = slice(r * LANES, (r + 8) * LANES)
            for k in range(GROUP):
                n = base + k
                ends_out[n : n + 1, columns] = h[k].reshape(1, 8 * LANES)
                ends_out[STATE + n : STATE + n + 1, columns] = lam[k].reshape(1, 8 * LANES)


def full_kernel(
    b, c, step, sig, act, g, alog, carries, skip,
    mixed_out, pre_out, act_out, rate_out, vec_out, bc_out,
    a2, acts, gs, hist, mixed, s1, s2, gb, gc,
):
    tokens, rows, _ = step.shape
    width = rows * LANES
    block = min(tokens, BLOCK)
    dense, flat = (block, rows, LANES), (block, width)
    a2[...] = (-LOG2E * jnp.exp(alog[...])).reshape(STATE, rows, LANES)

    @pl.loop(0, tokens // block)
    def _(i):
        at = pl.ds(pl.multiple_of(i * block, block), block)
        acts[at] = act[at, :].astype(F32).reshape(dense)
        gs[at] = g[at, :].astype(F32).reshape(dense)

    carry_dense = carries[...].reshape(2 * STATE, rows, LANES)
    skip_dense = skip[...].reshape(rows, LANES)
    zero = jnp.zeros((rows, LANES), F32)

    for base in range(0, STATE, GROUP):
        group = slice(base, base + GROUP)

        def forward(t, h):
            s = step[t]
            u = s * acts[t]
            g_now = gs[t]
            h = list(h)
            total = skip_dense * acts[t] if base == 0 else mixed[t]
            for k in range(GROUP):
                n = base + k
                d = jnp.exp2(s * a2[n])
                h[k] = d * h[k] + b[t, n : n + 1, :] * u
                hist[t + 1, k] = h[k]
                total = total + c[t, n : n + 1, :] * h[k]
            mixed[t] = total
            gc[t, group, :] = row_sums([g_now * part for part in h])
            return tuple(h)

        hist[0] = carry_dense[group]
        lax.fori_loop(
            0, tokens, forward, tuple(carry_dense[base + k] for k in range(GROUP)), unroll=UNROLL
        )

        def backward(i, carry):
            m, ga = carry
            m, ga = list(m), list(ga)
            t = tokens - 1 - i
            s = step[t]
            u = s * acts[t]
            g_now = gs[t]
            total1 = zero if base == 0 else s1[t]
            total2 = zero if base == 0 else s2[t]
            products = []
            for k in range(GROUP):
                n = base + k
                lam = c[t, n : n + 1, :] * g_now + m[k]
                total1 = total1 + b[t, n : n + 1, :] * lam
                products.append(lam * u)
                m[k] = jnp.exp2(s * a2[n]) * lam
                q = m[k] * hist[t, k]
                total2 = total2 + q * a2[n]
                ga[k] = ga[k] + q * s
            gb[t, group, :] = row_sums(products)
            s1[t] = total1
            s2[t] = total2
            return tuple(m), tuple(ga)

        _, ga = lax.fori_loop(
            0, tokens, backward,
            (tuple(carry_dense[STATE + base + k] for k in range(GROUP)), (zero,) * GROUP),
            unroll=UNROLL,
        )
        for k in range(GROUP):
            n = base + k
            rate_out[n : n + 1, :] = (LN2 * a2[n] * ga[k]).reshape(1, width)

    lane = lax.broadcasted_iota(jnp.int32, (1, STATE, LANES), 2)
    state = lax.broadcasted_iota(jnp.int32, (1, STATE, LANES), 1)
    ones = jnp.ones((LANES, LANES), BF16)

    def finish(i, totals):
        at = pl.ds(pl.multiple_of(i * block, block), block)
        first, act_now, g_now = s1[at], acts[at], gs[at]
        mixed_out[at, :] = mixed[at].reshape(flat).astype(BF16)
        grad_pre = (LN2 * s2[at] + first * act_now).reshape(flat) * sig[at, :]
        pre_out[at, :] = grad_pre.astype(BF16)
        act_out[at, :] = (first * step[at] + skip_dense[None] * g_now).reshape(flat)
        both = jnp.zeros((block, LANES), F32)
        for offset, ref in ((0, gb), (STATE, gc)):
            sums = jnp.dot(
                ref[at].reshape(block * STATE, LANES).astype(BF16), ones,
                preferred_element_type=F32,
            ).reshape(block, STATE, LANES)
            both = both + jnp.sum(jnp.where(lane == state + offset, sums, 0.0), axis=1)
        bc_out[at, :] = both
        return (
            totals[0] + jnp.sum(grad_pre, axis=0, keepdims=True),
            totals[1] + jnp.sum(g_now * act_now, axis=0),
        )

    bias, gain = lax.fori_loop(
        0, tokens // block, finish, (jnp.zeros((1, width), F32), zero)
    )
    vec_out[0:1, :] = bias
    vec_out[1:2, :] = gain.reshape(1, width)


def scan_local(b, c, low, dtw, dtb, act, g, alog):
    tokens, channels = act.shape
    dense = (tokens, channels // LANES, LANES)
    operands = (b, c, low, dtw, dtb, act, g, alog)
    return pl.pallas_call(
        local_kernel,
        in_specs=[pl.BlockSpec(memory_space=pltpu.VMEM)] * len(operands),
        out_shape=[
            jax.ShapeDtypeStruct(dense, F32),
            jax.ShapeDtypeStruct((tokens, channels), F32),
            jax.ShapeDtypeStruct((2 * STATE + 1, channels), F32),
        ],
        scratch_shapes=[
            pltpu.VMEM((STATE,) + dense[1:], F32), pltpu.VMEM(dense, F32), pltpu.VMEM(dense, F32),
        ],
        compiler_params=pltpu.CompilerParams(vmem_limit_bytes=VMEM_LIMIT),
        name="scan_local",
    )(*operands)


def scan_full(b, c, step, sig, act, g, alog, carries, skip):
    tokens, channels = act.shape
    dense = (tokens, channels // LANES, LANES)
    flat = (tokens, channels)
    operands = (b, c, step, sig, act, g, alog, carries, skip)
    small = pltpu.VMEM((tokens, STATE, LANES), F32)
    return pl.pallas_call(
        full_kernel,
        in_specs=[pl.BlockSpec(memory_space=pltpu.VMEM)] * len(operands),
        out_shape=[
            jax.ShapeDtypeStruct(flat, BF16),
            jax.ShapeDtypeStruct(flat, BF16),
            jax.ShapeDtypeStruct(flat, F32),
            jax.ShapeDtypeStruct((STATE, channels), F32),
            jax.ShapeDtypeStruct((2, channels), F32),
            jax.ShapeDtypeStruct((tokens, LANES), F32),
        ],
        scratch_shapes=[
            pltpu.VMEM((STATE,) + dense[1:], F32),
            pltpu.VMEM(dense, F32),
            pltpu.VMEM(dense, F32),
            pltpu.VMEM((tokens + 1, GROUP) + dense[1:], F32),
            pltpu.VMEM(dense, F32),
            pltpu.VMEM(dense, F32),
            pltpu.VMEM(dense, F32),
            small,
            small,
        ],
        compiler_params=pltpu.CompilerParams(vmem_limit_bytes=VMEM_LIMIT),
        name="scan_full",
    )(*operands)


def carry_kernel(ends, alog, out):
    count = ends.shape[0]
    a2 = -LOG2E * jnp.exp(alog[...])
    h = jnp.zeros(a2.shape, F32)
    for j in range(count):
        out[j, :STATE, :] = h
        decay = jnp.exp2(a2 * ends[j, 2 * STATE : 2 * STATE + 1, :])
        h = decay * h + ends[j, :STATE, :]
    lam = jnp.zeros(a2.shape, F32)
    for j in reversed(range(count)):
        out[j, STATE:, :] = lam
        decay = jnp.exp2(a2 * ends[j, 2 * STATE : 2 * STATE + 1, :])
        lam = decay * lam + ends[j, STATE : 2 * STATE, :]


def exchange_carries(ends, a_log):
    count, mine = lax.axis_size("ctx"), lax.axis_index("ctx")
    rows, channels = ends.shape
    width = channels // count
    parts = lax.all_to_all(
        ends.reshape(rows, count, width).transpose(1, 0, 2), "ctx", 0, 0, tiled=True
    )
    own_rates = lax.dynamic_slice_in_dim(a_log, mine * width, width, axis=1)
    carried = pl.pallas_call(
        carry_kernel,
        out_shape=jax.ShapeDtypeStruct((count, 2 * STATE, width), F32),
        name="carry",
    )(parts, own_rates)
    back = lax.all_to_all(carried, "ctx", 0, 0, tiled=True)
    return back.transpose(1, 0, 2).reshape(2 * STATE, channels)


def shifted(block, axis, distance):
    devices = range(lax.axis_size(axis))
    route = [(i - distance, i) for i in devices if i - distance in devices]
    return lax.ppermute(block, axis, route)


def send(x, route, dtype=None):
    if dtype is None:
        return lax.ppermute(x, "ctx", route)
    return lax.ppermute(x.astype(dtype), "ctx", route).astype(x.dtype)


def flip_route(bit):
    return [(i, i ^ bit) for i in range(lax.axis_size("ctx"))]


def line_route(k):
    count = lax.axis_size("ctx")
    return [(i, (i + PLANE * k) % count) for i in range(count)]


def swap_mp(x):
    return lax.ppermute(x, "mp", [(0, 1), (1, 0)])


def plane_groups():
    count = lax.axis_size("ctx")
    return [list(range(i, i + PLANE)) for i in range(0, count, PLANE)]


def in_plane(x):
    return lax.all_to_all(x, "ctx", 0, 0, axis_index_groups=plane_groups(), tiled=True)


def by_owner(x):
    count = lax.axis_size("ctx")
    rows, channels = x.shape
    x = x.reshape(rows, count // PLANE, PLANE, channels // count).transpose(2, 0, 1, 3)
    return x.reshape(PLANE, rows, channels // PLANE)


def to_channels(x):
    rows, channels = x.shape
    return in_plane(by_owner(x)).reshape(PLANE * rows, channels // PLANE)


def to_tokens(x):
    count = lax.axis_size("ctx")
    rows, channels = x.shape
    x = in_plane(x.reshape(PLANE, rows // PLANE, channels))
    x = x.reshape(PLANE, rows // PLANE, count // PLANE, PLANE * channels // count)
    return x.transpose(1, 2, 0, 3).reshape(rows // PLANE, PLANE * channels)


def own_channels(x):
    count = lax.axis_size("ctx")
    rows, channels = x.shape
    x = x.reshape(rows, count // PLANE, PLANE, channels // count)
    x = lax.dynamic_index_in_dim(x, lax.axis_index("ctx") % PLANE, 2, keepdims=False)
    return x.reshape(rows, channels // PLANE)


def gather_line(x):
    planes = lax.axis_size("ctx") // PLANE
    mine = lax.axis_index("ctx") // PLANE
    rows = x.shape[0]
    out = jnp.zeros((planes * rows, x.shape[1]), x.dtype)
    for k in range(planes):
        block = send(x, line_route(-k)) if k else x
        out = lax.dynamic_update_slice(out, block, (lax.rem(mine + k, planes) * rows, 0))
    return out


def pick(x, at, axis=0):
    return lax.dynamic_index_in_dim(x, at, axis, keepdims=False)


def sum_plane(x):
    core = lax.axis_index("mp")
    halves = x.reshape(2, x.shape[0] // 2, x.shape[1])
    mine = pick(halves, core) + swap_mp(pick(halves, 1 - core))
    middle = mine.shape[0] // 2
    a, b = mine[:middle], mine[middle:]
    a, b = a + send(a, flip_route(1), BF16), b + send(b, flip_route(2), BF16)
    a, b = a + send(a, flip_route(2), BF16), b + send(b, flip_route(1), BF16)
    mine = jnp.concatenate([a, b], axis=0)
    other = swap_mp(mine)
    return jnp.where(
        core == 0, jnp.concatenate([mine, other], axis=0), jnp.concatenate([other, mine], axis=0)
    )


def line_carries(ends, a_log):
    count = lax.axis_size("ctx")
    rates = -jnp.exp(a_log)
    state, adjoint, total = ends[:STATE], ends[STATE : 2 * STATE], ends[2 * STATE :]

    def enter(x, direction):
        x = jnp.concatenate([x, total], axis=0)
        carry = jnp.zeros((STATE, x.shape[1]), F32)
        parts = []
        for k in range(1, count // PLANE):
            step = direction * PLANE * k
            route = [(i, i + step) for i in range(count) if 0 <= i + step < count]
            parts.append(send(x, route))
        for part in reversed(parts):
            carry = jnp.exp(rates * part[STATE:]) * carry + part[:STATE]
        return carry

    return jnp.concatenate([enter(state, 1), enter(adjoint, -1)], axis=0)


def scatter_line(parts):
    planes = lax.axis_size("ctx") // PLANE
    mine = lax.axis_index("ctx") // PLANE
    total = parts(mine)
    for k in sorted(range(1, planes), key=lambda k: -min(k, planes - k)):
        total = total + send(parts(lax.rem(mine + k, planes)), line_route(k), BF16)
    return total


def sum_line(x):
    planes = lax.axis_size("ctx") // PLANE
    mine = lax.axis_index("ctx") // PLANE
    x = x.reshape(x.shape[0], planes, x.shape[1] // planes)
    total = pick(x, mine, 1)
    for k in range(1, planes):
        total = total + send(pick(x, lax.rem(mine + k, planes), 1), line_route(k))
    return total


def silu_parts(x):
    s = jax.nn.sigmoid(x)
    return x * s, s * (1.0 + x * (1.0 - s))


def conv_forward(padded, weight, bias, length):
    pre_act = jnp.zeros((length, padded.shape[1]), F32) + bias
    for k in range(CONV):
        pre_act = pre_act + weight[k][None, :] * padded[k : k + length]
    return pre_act


def conv_backward(grad_padded, weight, length):
    grad = jnp.zeros((length, grad_padded.shape[1]), F32)
    for k in range(CONV):
        grad = grad + weight[k][None, :] * grad_padded[CONV - 1 - k : CONV - 1 - k + length]
    return grad.astype(BF16)


def conv_sums(grad, padded):
    length = grad.shape[0]
    return jnp.stack(
        [jnp.sum(grad * padded[k : k + length], axis=0) for k in range(CONV)]
        + [jnp.sum(grad, axis=0)]
    )


def spread(x):
    return jnp.broadcast_to(x[:, :, None], x.shape + (LANES,))


def split_proj(projected):
    low = projected[:, :RANK].astype(BF16)
    b = spread(projected[:, RANK : RANK + STATE])
    c = spread(projected[:, RANK + STATE :])
    return low, b, c


def matmul(x, y, dims):
    return lax.dot_general(x, y, ((dims[:1], dims[1:]), ((), ())), preferred_element_type=F32)


def gate_parts(gate_in, upstream, forget_flags):
    grad_out = -forget_flags.astype(F32)[:, None] * upstream.astype(F32)
    value, slope = silu_parts(gate_in.astype(F32))
    return (grad_out * value).astype(BF16), grad_out * slope


def outputs(grad_seq, grad_gate, grad_dtw, sums):
    return (
        grad_seq, grad_gate, grad_dtw,
        sums[:CONV], sums[CONV], sums[CONV + 1], sums[CONV + 3 :], sums[CONV + 2],
    )


def plane_body(
    seq_in, gate_in, upstream, forget_flags, conv_weight, conv_bias,
    proj_weight, dt_weight, dt_bias, a_log, skip_gain,
):
    rim = CONV - 1
    seq = to_channels(seq_in)
    rows_proj = gather_line(proj_weight)
    grad_mixed, gate_factor = gate_parts(gate_in, upstream, forget_flags)
    rows_dt = gather_line(in_plane(by_owner(dt_weight)).reshape(-1, seq.shape[1]))
    grad_mixed = to_channels(grad_mixed)
    weight, bias, step_bias, rates, gain = (
        own_channels(x)
        for x in (conv_weight, conv_bias[None], dt_bias[None], a_log, skip_gain[None])
    )
    length = seq.shape[0]
    padded = jnp.concatenate([shifted(seq[length - rim :], "ctx", PLANE), seq], axis=0)
    pre_act = conv_forward(padded, weight, bias, length)
    act = jax.nn.silu(pre_act).astype(BF16)
    low, b, c = split_proj(sum_plane(matmul(act, rows_proj, (1, 0))))
    step, sig, ends = scan_local(b, c, low, rows_dt, step_bias, act, grad_mixed, rates)
    carries = line_carries(ends, rates)
    mixed, grad_pre, grad_act, grad_rate, grad_vecs, grad_bc = scan_full(
        b, c, step, sig, act, grad_mixed, rates, carries, gain
    )
    grad_low = matmul(grad_pre, rows_dt, (1, 1))
    grad_proj = sum_plane(
        jnp.concatenate([grad_low, grad_bc[:, : 2 * STATE]], axis=1)
    ).astype(BF16)
    planes = lax.axis_size("ctx") // PLANE

    def dt_part(zt):
        part = lax.dynamic_slice_in_dim(low, zt * (RANK // planes), RANK // planes, axis=1)
        return matmul(part, grad_pre, (0, 0))

    grad_dtw = to_tokens(scatter_line(dt_part).astype(BF16)).astype(F32)
    grad_gate = (gate_factor * to_tokens(mixed).astype(F32)).astype(BF16)
    grad_pre_act = (grad_act + matmul(grad_proj, rows_proj, (1, 1))) * silu_parts(pre_act)[1]
    grad_padded = jnp.concatenate(
        [grad_pre_act, shifted(grad_pre_act[:rim], "ctx", -PLANE)], axis=0
    )
    grad_seq = to_tokens(conv_backward(grad_padded, weight, length))
    sums = sum_line(
        jnp.concatenate([conv_sums(grad_pre_act, padded), grad_vecs, grad_rate], axis=0)
    )
    return outputs(grad_seq, grad_gate, grad_dtw, sums)


def block_body(
    seq_in, gate_in, upstream, forget_flags, conv_weight, conv_bias,
    proj_weight, dt_weight, dt_bias, a_log, skip_gain,
):
    length = seq_in.shape[0]
    rim = CONV - 1
    padded = jnp.concatenate([shifted(seq_in[length - rim :], "ctx", 1), seq_in], axis=0)
    pre_act = conv_forward(padded, conv_weight, conv_bias[None], length)
    act = jax.nn.silu(pre_act).astype(BF16)
    rows_proj = lax.all_gather(proj_weight, "ctx", axis=0, tiled=True)
    rows_dt = lax.all_gather(dt_weight, "ctx", axis=0, tiled=True)
    low, b, c = split_proj(lax.psum(matmul(act, rows_proj, (1, 0)), "mp"))
    grad_mixed, gate_factor = gate_parts(gate_in, upstream, forget_flags)
    step, sig, ends = scan_local(b, c, low, rows_dt, dt_bias[None], act, grad_mixed, a_log)
    carries = exchange_carries(ends, a_log)
    mixed, grad_pre, grad_act, grad_rate, grad_vecs, grad_bc = scan_full(
        b, c, step, sig, act, grad_mixed, a_log, carries, skip_gain[None]
    )
    grad_gate = (gate_factor * mixed.astype(F32)).astype(BF16)
    grad_low = matmul(grad_pre, rows_dt, (1, 1))
    grad_proj = lax.psum(
        jnp.concatenate([grad_low, grad_bc[:, : 2 * STATE]], axis=1), "mp"
    ).astype(BF16)
    grad_pre_act = (grad_act + matmul(grad_proj, rows_proj, (1, 1))) * silu_parts(pre_act)[1]
    grad_padded = jnp.concatenate([grad_pre_act, shifted(grad_pre_act[:rim], "ctx", -1)], axis=0)
    grad_seq = conv_backward(grad_padded, conv_weight, length)
    scatter = lambda x, axis: lax.psum_scatter(x, "ctx", scatter_dimension=axis, tiled=True)
    grad_dtw = scatter(matmul(low, grad_pre, (0, 0)), 0)
    sums = scatter(
        jnp.concatenate([conv_sums(grad_pre_act, padded), grad_vecs, grad_rate], axis=0), 1
    )
    return outputs(grad_seq, grad_gate, grad_dtw, sums)


def solution(mesh):
    shares = mesh.shape["mp"] == 2 and mesh.shape["ctx"] in (8, 16)
    body = plane_body if shares else block_body
    return jax.shard_map(
        body,
        mesh=mesh,
        in_specs=(
            P("ctx", "mp"),
            P("ctx", "mp"),
            P("ctx", "mp"),
            P("ctx"),
            P(None, "mp"),
            P("mp"),
            P(("mp", "ctx"), None),
            P("ctx", "mp"),
            P("mp"),
            P(None, "mp"),
            P("mp"),
        ),
        out_specs=(
            P("ctx", "mp"),
            P("ctx", "mp"),
            P("ctx", "mp"),
            P(None, ("mp", "ctx")),
            P(("mp", "ctx")),
            P(("mp", "ctx")),
            P(None, ("mp", "ctx")),
            P(("mp", "ctx")),
        ),
        check_vma=False,
    )
```

time: 1870 us -> 323 us (0.17)
  other arithmetic: 923 us -> 19.6 us
  waiting for transfers between devices: 682 us -> 79.8 us
  local copies, waits for them, and re-layouts: 145 us -> 65.8 us
  Pallas kernels: 0 us -> 72.1 us
  starting transfers between devices: 6.4 us -> 70 us
  blocking collectives: 59.1 us -> 0 us
    reduce_sum x43 -> x1, other arithmetic: 664 us -> 2.92 us  [conv_sums(): jnp.sum(grad, axis=0)]
    all_gather x5 -> x0, waiting for transfers between devices: 382 us -> none  [the longest x3 226 us: prefix(): everything = jax.tree.map(lambda part: lax.all_gather(part, axis), x)]
    reduce_scatter x2 -> x0, waiting for transfers between devices: 265 us -> none  [the longest x1 193 us: body(): lax.psum_scatter(grad_dtw, 'ctx', scatter_dimension=0, tiled=True)]
    another operation x74 -> x0, other arithmetic: 146 us -> none  [the longest x24 83.7 us: block_closed(): cumul = jnp.cumsum(step_blk[:, None, :] * a_matrix[None], axis=0)]
    pallas_call x0 -> x2, Pallas kernels: none -> 72.1 us  [the longest x1 50.6 us: scan_full(): pl.pallas_call(full_kernel, in_specs=[pl.BlockSpec(memory_space=pltpu.VME...]
    ppermute x0 -> x30, waiting for transfers between devices: none -> 61.7 us  [the longest x15 37.4 us: send(): return lax.ppermute(x, 'ctx', route)]
    unnamed x1 -> x0, blocking collectives: 59.1 us -> none
    squeeze x96 -> x0, local copies, waits for them, and re-layouts: 58.3 us -> none  [the longest x80 58 us: scan_tokens(): lax.scan(jax.checkpoint(block_closed), (start_state, a_matrix), to_blocks...]
  transfers between devices with their start and end apart: 12 -> 38, of which waited for: 11 -> 14; matrix products, arithmetic and copies ran while one was open for 2% -> 16% of each run, Pallas kernels for 0% -> 0%
where the time goes in v1:
time: 323 us; the launch traced here: 318 us
  waiting for transfers between devices  79.8 us (25%)
  Pallas kernels  72.1 us (22%)
  starting transfers between devices  70 us (22%)
  local copies, waits for them, and re-layouts  65.8 us (20%)
  other arithmetic  19.6 us (6%)
  matrix products  9.41 us (3%)
    pallas_call x1, Pallas kernels, scan_full(): pl.pallas_call(full_kernel, in_specs=[pl.BlockSpec(memory_space=pltpu.VME...  50.6 us
    ppermute x15, waiting for transfers between devices, send(): return lax.ppermute(x, 'ctx', route)  37.4 us
    ppermute x15, starting transfers between devices, send(): return lax.ppermute(x, 'ctx', route)  29.9 us
    all_to_all x6, starting transfers between devices, in_plane(): lax.all_to_all(x, 'ctx', 0, 0, axis_index_groups=plane_groups(), tiled=True)  29.2 us
    ppermute x11, waiting for transfers between devices, send(): return lax.ppermute(x.astype(dtype), 'ctx', route).astype(x.dtype)  24.2 us
    pallas_call x1, Pallas kernels, scan_local(): pl.pallas_call(local_kernel, in_specs=[pl.BlockSpec(memory_space=pltpu.VM...  21.5 us
    all_to_all x6, waiting for transfers between devices, in_plane(): lax.all_to_all(x, 'ctx', 0, 0, axis_index_groups=plane_groups(), tiled=True)  14.9 us
    dot_general x7, matrix products, matmul(): lax.dot_general(x, y, ((dims[:1], dims[1:]), ((), ())), preferred_element...  9.41 us
  transfers between devices with their start and end apart: 38, of which 14 were waited for; matrix products, arithmetic and copies ran while one was open for 16% of the time, Pallas kernels for 0%

profile of v1, /device:TPU:14, one launch (start us, length us, event | category | flops | bytes accessed | tf_op | source)
XLA Modules:
  0.0 318.4 jit_solution(17299549104220403470)
XLA Ops:
  4.5 4.3 %all-to-all-start = ((bf16[4,128,1024]{2,1,0:T(8,128)(2,1)}), bf16[4,128,1024]{2,1,0:T(8,128)(2,1)S(1)}, u32[]{:S(2)}, u32[]{:S(2)}) async-start(bf16[4,128,1024]{2,1,0:T(8,128)(2,1)} %reshape.126), calls=%async_computation | async-start | bytes 2097152 | tf_op jit(solution)/shard_map/all_to_all | solution.py:329
  10.8 4.4 %collective-permute-start.2 = (bf16[256,544]{0,1:T(8,128)(2,1)S(1)}, bf16[256,544]{0,1:T(8,128)(2,1)S(1)}, u32[]{:S(2)}, u32[]{:S(2)}) collective-permute-start(bf16[256,544]{0,1:T(8,128)(2,1)S(1)} %copy-done.17), channel_id=1, source_target_pairs={{0,16},{2,18},{4,20},{6,22},{8,24},{10,26},{12,28},{14,30},{16,0},... | collective-permute-start | bytes 835592 | tf_op jit(solution)/shard_map/ppermute | solution.py:306
  15.6 14.7 %collective-permute-done.1 = bf16[256,544]{0,1:T(8,128)(2,1)S(1)} collective-permute-done((bf16[256,544]{0,1:T(8,128)(2,1)S(1)}, bf16[256,544]{0,1:T(8,128)(2,1)S(1)}, u32[]{:S(2)}, u32[]{:S(2)}) %collective-permute-start.1) | collective-permute-done | bytes 278560 | tf_op jit(solution)/shard_map/ppermute | solution.py:306
  30.4 3.5 %collective-permute-done.2 = bf16[256,544]{0,1:T(8,128)(2,1)S(1)} collective-permute-done((bf16[256,544]{0,1:T(8,128)(2,1)S(1)}, bf16[256,544]{0,1:T(8,128)(2,1)S(1)}, u32[]{:S(2)}, u32[]{:S(2)}) %collective-permute-start.2) | collective-permute-done | bytes 278560 | tf_op jit(solution)/shard_map/ppermute | solution.py:306
  47.9 4.4 %all-to-all-start.1 = ((bf16[4,32,1024]{2,1,0:T(8,128)(2,1)}), bf16[4,32,1024]{2,1,0:T(8,128)(2,1)}, u32[]{:S(2)}, u32[]{:S(2)}) async-start(bf16[4,32,1024]{2,1,0:T(8,128)(2,1)} %reshape.130), calls=%async_computation.1 | async-start | bytes 524288 | tf_op jit(solution)/shard_map/all_to_all | solution.py:329
  55.2 5.7 %collective-permute-done.5 = bf16[128,544]{1,0:T(8,128)(2,1)S(1)} collective-permute-done((bf16[128,544]{1,0:T(8,128)(2,1)S(1)}, bf16[128,544]{1,0:T(8,128)(2,1)S(1)}, u32[]{:S(2)}, u32[]{:S(2)}) %collective-permute-start.5) | collective-permute-done | bytes 139296 | tf_op jit(solution)/shard_map/ppermute | solution.py:307
  69.0 5.0 %all-to-all-start.2 = ((bf16[4,128,1024]{2,1,0:T(8,128)(2,1)}), bf16[4,128,1024]{2,1,0:T(8,128)(2,1)S(1)}, u32[]{:S(2)}, u32[]{:S(2)}) async-start(bf16[4,128,1024]{2,1,0:T(8,128)(2,1)} %reshape.134), calls=%async_computation.2 | async-start | bytes 2097152 | tf_op jit(solution)/shard_map/all_to_all | solution.py:329
  86.0 11.6 %collective-permute-done.10 = bf16[128,1024]{1,0:T(8,128)(2,1)} collective-permute-done((bf16[128,1024]{1,0:T(8,128)(2,1)}, bf16[128,1024]{1,0:T(8,128)(2,1)}, u32[]{:S(2)}, u32[]{:S(2)}) %collective-permute-start.10) | collective-permute-done | bytes 262176 | tf_op jit(solution)/shard_map/ppermute | solution.py:306
  105.5 3.6 %broadcast_in_dim.10.c = f32[512,16,128]{2,1,0:T(8,128)} broadcast(f32[512,16]{1,0:T(8,128)} %get-tuple-element.35), dimensions={0,1} | broadcast | bytes 4227072 | tf_op jit(solution)/shard_map/broadcast_in_dim | solution.py:457
  111.7 21.5 %scan_local.1 = (f32[512,8,128]{2,1,0:T(8,128)}, f32[512,1024]{1,0:T(8,128)}, f32[33,1024]{1,0:T(8,128)}) custom-call(f32[512,16,128]{2,1,0:T(8,128)} %broadcast_in_dim.9.b, f32[512,16,128]{2,1,0:T(8,128)} %broadcast_in_dim.10.c, bf16[512,512]{1,0:T(8,128)(2,1)} %slice.305.low, bf16[512,1024]{1,0:T(8,128)(2,1)} %copy-done.6, f32[1,1024]{1,0:T(1,128)} %bitcast.110, ...), custom_call_target="tpu_custom_call" | custom-call | tf_op jit(solution)/shard_map/scan_local/pallas_call | solution.py:217
  136.5 4.0 %collective-permute-start.14 = (f32[17,1024]{1,0:T(8,128)S(1)}, f32[17,1024]{1,0:T(8,128)S(1)}, u32[]{:S(2)}, u32[]{:S(2)}) collective-permute-start(f32[17,1024]{1,0:T(8,128)S(1)} %pad_maximum_fusion.6), channel_id=1, source_target_pairs={{0,16},{2,18},{4,20},{6,22},{8,24},{10,26},{12,28},{14,30},{1,17},... | collective-permute-start | bytes 208904 | tf_op jit(solution)/shard_map/ppermute | solution.py:306
  144.4 4.5 %collective-permute-start.16 = (f32[17,1024]{1,0:T(8,128)S(1)}, f32[17,1024]{1,0:T(8,128)S(1)}, u32[]{:S(2)}, u32[]{:S(2)}) collective-permute-start(f32[17,1024]{1,0:T(8,128)S(1)} %concatenate.63), channel_id=1, source_target_pairs={{8,0},{10,2},{12,4},{14,6},{16,8},{18,10},{20,12},{22,14},{24,16},... | collective-permute-start | bytes 208904 | tf_op jit(solution)/shard_map/ppermute | solution.py:306
  149.6 4.5 %collective-permute-done.17 = f32[17,1024]{1,0:T(8,128)S(1)} collective-permute-done((f32[17,1024]{1,0:T(8,128)S(1)}, f32[17,1024]{1,0:T(8,128)S(1)}, u32[]{:S(2)}, u32[]{:S(2)}) %collective-permute-start.17) | collective-permute-done | bytes 69664 | tf_op jit(solution)/shard_map/ppermute | solution.py:306
  157.9 50.6 %scan_full.1 = (bf16[512,1024]{1,0:T(8,128)(2,1)}, bf16[512,1024]{1,0:T(8,128)(2,1)}, f32[512,1024]{1,0:T(8,128)}, f32[16,1024]{1,0:T(8,128)}, f32[2,1024]{1,0:T(2,128)}, /*index=5*/f32[512,128]{1,0:T(8,128)}) custom-call(f32[512,16,128]{2,1,0:T(8,128)} %broadcast_in_dim.9.b, f32[512,16,128]{2,1,0:T(8,128)} %broadcast_in_dim.10.c, ...), custom_call_target="tpu_custom_call" | custom-call | tf_op jit(solution)/shard_map/scan_full/pallas_call | solution.py:239
  217.4 3.6 %constant_dynamic-slice_fusion.8 = (f32[1,256,544]{1,0,2:T(1,128)}, f32[1,256,544]{1,0,2:T(1,128)S(1)}) fusion(f32[2,256,544]{1,0,2:T(2,128)} %reshape.139, s32[]{:T(128)S(6)} %select_n.104, s32[]{:T(128)S(6)} %select_n.105), kind=kLoop, calls=%fused_computation.130 | loop fusion | bytes 2228232 | tf_op jit(solution)/shard_map/jit(dynamic_index_in_dim)/dynamic_slice | solution.py:372
  231.0 5.9 %collective-permute-done.26 = bf16[128,1024]{1,0:T(8,128)(2,1)} collective-permute-done((bf16[128,1024]{1,0:T(8,128)(2,1)}, bf16[128,1024]{1,0:T(8,128)(2,1)}, u32[]{:S(2)}, u32[]{:S(2)}) %collective-permute-start.26) | collective-permute-done | bytes 262176 | tf_op jit(solution)/shard_map/ppermute | solution.py:307
  236.9 11.0 %collective-permute-done.27 = bf16[128,1024]{1,0:T(8,128)(2,1)} collective-permute-done((bf16[128,1024]{1,0:T(8,128)(2,1)S(1)}, bf16[128,1024]{1,0:T(8,128)(2,1)}, u32[]{:S(2)}, u32[]{:S(2)}) %collective-permute-start.27) | collective-permute-done | bytes 262176 | tf_op jit(solution)/shard_map/ppermute | solution.py:307
  251.2 4.2 %all-to-all-start.5 = ((bf16[4,32,1024]{2,1,0:T(8,128)(2,1)}), bf16[4,32,1024]{2,1,0:T(8,128)(2,1)S(1)}, u32[]{:S(2)}, u32[]{:S(2)}) async-start(bf16[4,32,1024]{2,1,0:T(8,128)(2,1)} %bitcast.25), calls=%async_computation.5 | async-start | bytes 524288 | tf_op jit(solution)/shard_map/all_to_all | solution.py:329
  256.2 3.7 %all-to-all-done.5 = bf16[4,32,1024]{2,1,0:T(8,128)(2,1)S(1)} async-done(((bf16[4,32,1024]{2,1,0:T(8,128)(2,1)}), bf16[4,32,1024]{2,1,0:T(8,128)(2,1)S(1)}, u32[]{:S(2)}, u32[]{:S(2)}) %all-to-all-start.5) | async-done | bytes 262176 | tf_op jit(solution)/shard_map/all_to_all | solution.py:329
  259.9 6.5 %all-to-all-start.4 = ((bf16[4,128,1024]{2,1,0:T(8,128)(2,1)}), bf16[4,128,1024]{2,1,0:T(8,128)(2,1)}, u32[]{:S(2)}, u32[]{:S(2)}) async-start(bf16[4,128,1024]{2,1,0:T(8,128)(2,1)} %bitcast.23), calls=%async_computation.4 | async-start | bytes 2097152 | tf_op jit(solution)/shard_map/all_to_all | solution.py:329
  269.7 6.6 %all-to-all-done.4 = bf16[4,128,1024]{2,1,0:T(8,128)(2,1)} async-done(((bf16[4,128,1024]{2,1,0:T(8,128)(2,1)}), bf16[4,128,1024]{2,1,0:T(8,128)(2,1)}, u32[]{:S(2)}, u32[]{:S(2)}) %all-to-all-start.4) | async-done | bytes 1048608 | tf_op jit(solution)/shard_map/all_to_all | solution.py:329
  299.2 4.9 %all-to-all-start.3 = ((bf16[4,128,1024]{2,1,0:T(8,128)(2,1)}), bf16[4,128,1024]{2,1,0:T(8,128)(2,1)S(1)}, u32[]{:S(2)}, u32[]{:S(2)}) async-start(bf16[4,128,1024]{2,1,0:T(8,128)(2,1)} %bitcast.21), calls=%async_computation.3 | async-start | bytes 2097152 | tf_op jit(solution)/shard_map/all_to_all | solution.py:329
  304.1 4.1 %fusion.25 = bf16[128,4096]{1,0:T(8,128)(2,1)} fusion(f32[128,4096]{1,0:T(8,128)} %reshape.145, bf16[128,4096]{1,0:T(8,128)(2,1)} %param.12, bf16[128,4096]{1,0:T(8,128)(2,1)} %param.13, f32[128]{0:T(128)S(1)} %copy-done.33), kind=kLoop, calls=%fused_computation.38 | loop fusion | flops 6815744 | bytes 5243392 | tf_op jit(solution)/shard_map/convert_element_type | solution.py:519
  310.0 4.6 %all-to-all-done.3 = bf16[4,128,1024]{2,1,0:T(8,128)(2,1)S(1)} async-done(((bf16[4,128,1024]{2,1,0:T(8,128)(2,1)}), bf16[4,128,1024]{2,1,0:T(8,128)(2,1)S(1)}, u32[]{:S(2)}, u32[]{:S(2)}) %all-to-all-start.3) | async-done | bytes 1048608 | tf_op jit(solution)/shard_map/all_to_all | solution.py:329
  (244 shorter events, 119.3 us)
Async XLA Ops:
  4.5 29.4 %all-to-all-start = ((bf16[4,128,1024]{2,1,0:T(8,128)(2,1)}), bf16[4,128,1024]{2,1,0:T(8,128)(2,1)S(1)}, u32[]{:S(2)}, u32[]{:S(2)}) async-start(bf16[4,128,1024]{2,1,0:T(8,128)(2,1)} %reshape.126), calls=%async_computation | async-start | bytes 2097152 | tf_op jit(solution)/shard_map/all_to_all | solution.py:329
  8.8 21.5 %collective-permute-start.1 = (bf16[256,544]{0,1:T(8,128)(2,1)S(1)}, bf16[256,544]{0,1:T(8,128)(2,1)S(1)}, u32[]{:S(2)}, u32[]{:S(2)}) collective-permute-start(bf16[256,544]{0,1:T(8,128)(2,1)S(1)} %copy-done.17), channel_id=1, source_target_pairs={{0,24},{2,26},{4,28},{6,30},{8,0},{10,2},{12,4},{14,6},{16,8},{18,... | collective-permute-start | bytes 835592 | tf_op jit(solution)/shard_map/ppermute | solution.py:306
  9.2 26.9 %collective-permute-start.3 = (bf16[256,544]{0,1:T(8,128)(2,1)S(1)}, bf16[256,544]{0,1:T(8,128)(2,1)S(1)}, u32[]{:S(2)}, u32[]{:S(2)}) collective-permute-start(bf16[256,544]{0,1:T(8,128)(2,1)S(1)} %copy-done.17), channel_id=1, source_target_pairs={{0,8},{2,10},{4,12},{6,14},{8,16},{10,18},{12,20},{14,22},{16,24},... | collective-permute-start | bytes 835592 | tf_op jit(solution)/shard_map/ppermute | solution.py:306
  10.8 23.0 %collective-permute-start.2 = (bf16[256,544]{0,1:T(8,128)(2,1)S(1)}, bf16[256,544]{0,1:T(8,128)(2,1)S(1)}, u32[]{:S(2)}, u32[]{:S(2)}) collective-permute-start(bf16[256,544]{0,1:T(8,128)(2,1)S(1)} %copy-done.17), channel_id=1, source_target_pairs={{0,16},{2,18},{4,20},{6,22},{8,24},{10,26},{12,28},{14,30},{16,0},... | collective-permute-start | bytes 835592 | tf_op jit(solution)/shard_map/ppermute | solution.py:306
  47.9 21.1 %all-to-all-start.1 = ((bf16[4,32,1024]{2,1,0:T(8,128)(2,1)}), bf16[4,32,1024]{2,1,0:T(8,128)(2,1)}, u32[]{:S(2)}, u32[]{:S(2)}) async-start(bf16[4,32,1024]{2,1,0:T(8,128)(2,1)} %reshape.130), calls=%async_computation.1 | async-start | bytes 524288 | tf_op jit(solution)/shard_map/all_to_all | solution.py:329
  61.2 16.1 %collective-permute-start.6 = (bf16[128,544]{1,0:T(8,128)(2,1)S(1)}, bf16[128,544]{1,0:T(8,128)(2,1)S(1)}, u32[]{:S(2)}, u32[]{:S(2)}) collective-permute-start(bf16[128,544]{1,0:T(8,128)(2,1)S(1)} %get-tuple-element.49), channel_id=1, source_target_pairs={{0,4},{2,6},{4,0},{6,2},{8,12},{10,14},{12,8},{14,10},{16,20},{18,... | collective-permute-start | bytes 417800 | tf_op jit(solution)/shard_map/ppermute | solution.py:307
  62.0 16.0 %collective-permute-start.8 = (bf16[128,544]{1,0:T(8,128)(2,1)S(1)}, bf16[128,544]{1,0:T(8,128)(2,1)}, u32[]{:S(2)}, u32[]{:S(2)}) collective-permute-start(bf16[128,544]{1,0:T(8,128)(2,1)S(1)} %get-tuple-element.50), channel_id=1, source_target_pairs={{0,2},{2,0},{4,6},{6,4},{8,10},{10,8},{12,14},{14,12},{16,18},{18,... | collective-permute-start | bytes 417800 | tf_op jit(solution)/shard_map/ppermute | solution.py:307
  69.0 36.5 %all-to-all-start.2 = ((bf16[4,128,1024]{2,1,0:T(8,128)(2,1)}), bf16[4,128,1024]{2,1,0:T(8,128)(2,1)S(1)}, u32[]{:S(2)}, u32[]{:S(2)}) async-start(bf16[4,128,1024]{2,1,0:T(8,128)(2,1)} %reshape.134), calls=%async_computation.2 | async-start | bytes 2097152 | tf_op jit(solution)/shard_map/all_to_all | solution.py:329
  73.9 24.7 %collective-permute-start.11 = (bf16[128,1024]{1,0:T(8,128)(2,1)}, bf16[128,1024]{1,0:T(8,128)(2,1)}, u32[]{:S(2)}, u32[]{:S(2)}) collective-permute-start(bf16[128,1024]{1,0:T(8,128)(2,1)} %bitcast.9), channel_id=1, source_target_pairs={{0,16},{2,18},{4,20},{6,22},{8,24},{10,26},{12,28},{14,30},{16,0},... | collective-permute-start | bytes 786440 | tf_op jit(solution)/shard_map/ppermute | solution.py:306
  77.3 20.3 %collective-permute-start.10 = (bf16[128,1024]{1,0:T(8,128)(2,1)}, bf16[128,1024]{1,0:T(8,128)(2,1)}, u32[]{:S(2)}, u32[]{:S(2)}) collective-permute-start(bf16[128,1024]{1,0:T(8,128)(2,1)} %bitcast.9), channel_id=1, source_target_pairs={{0,24},{2,26},{4,28},{6,30},{8,0},{10,2},{12,4},{14,6},{16,8},{18,... | collective-permute-start | bytes 786440 | tf_op jit(solution)/shard_map/ppermute | solution.py:306
  80.3 19.3 %collective-permute-start.9 = (f32[256,544]{0,1:T(8,128)}, f32[256,544]{0,1:T(8,128)}, u32[]{:S(2)}, u32[]{:S(2)}) collective-permute-start(f32[256,544]{0,1:T(8,128)} %copy.46), channel_id=1, source_target_pairs={{0,1},{1,0},{2,3},{3,2},{4,5},{5,4},{6,7},{7,6},{8,9},{9,8},{10,11... | collective-permute-start | bytes 1671176 | tf_op jit(solution)/shard_map/ppermute | solution.py:320
  82.9 16.7 %collective-permute-start.12 = (bf16[128,1024]{1,0:T(8,128)(2,1)}, bf16[128,1024]{1,0:T(8,128)(2,1)S(1)}, u32[]{:S(2)}, u32[]{:S(2)}) collective-permute-start(bf16[128,1024]{1,0:T(8,128)(2,1)} %bitcast.9), channel_id=1, source_target_pairs={{0,8},{2,10},{4,12},{6,14},{8,16},{10,18},{12,20},{14,22},{16,24},... | collective-permute-start | bytes 786440 | tf_op jit(solution)/shard_map/ppermute | solution.py:306
  136.5 13.1 %collective-permute-start.14 = (f32[17,1024]{1,0:T(8,128)S(1)}, f32[17,1024]{1,0:T(8,128)S(1)}, u32[]{:S(2)}, u32[]{:S(2)}) collective-permute-start(f32[17,1024]{1,0:T(8,128)S(1)} %pad_maximum_fusion.6), channel_id=1, source_target_pairs={{0,16},{2,18},{4,20},{6,22},{8,24},{10,26},{12,28},{14,30},{1,17},... | collective-permute-start | bytes 208904 | tf_op jit(solution)/shard_map/ppermute | solution.py:306
  144.4 12.8 %collective-permute-start.16 = (f32[17,1024]{1,0:T(8,128)S(1)}, f32[17,1024]{1,0:T(8,128)S(1)}, u32[]{:S(2)}, u32[]{:S(2)}) collective-permute-start(f32[17,1024]{1,0:T(8,128)S(1)} %concatenate.63), channel_id=1, source_target_pairs={{8,0},{10,2},{12,4},{14,6},{16,8},{18,10},{20,12},{22,14},{24,16},... | collective-permute-start | bytes 208904 | tf_op jit(solution)/shard_map/ppermute | solution.py:306
  224.3 23.6 %collective-permute-start.27 = (bf16[128,1024]{1,0:T(8,128)(2,1)S(1)}, bf16[128,1024]{1,0:T(8,128)(2,1)}, u32[]{:S(2)}, u32[]{:S(2)}) collective-permute-start(bf16[128,1024]{1,0:T(8,128)(2,1)S(1)} %convolution_convert_fusion.1), channel_id=1, source_target_pairs={{0,8},{2,10},{4,12},{6,14},{8,16},{10,18},{12,20},{14,22},{16,24},... | collective-permute-start | bytes 786440 | tf_op jit(solution)/shard_map/ppermute | solution.py:307
  226.4 22.9 %collective-permute-start.28 = (bf16[128,1024]{1,0:T(8,128)(2,1)}, bf16[128,1024]{1,0:T(8,128)(2,1)}, u32[]{:S(2)}, u32[]{:S(2)}) collective-permute-start(bf16[128,1024]{1,0:T(8,128)(2,1)} %convolution_convert_fusion), channel_id=1, source_target_pairs={{0,24},{2,26},{4,28},{6,30},{8,0},{10,2},{12,4},{14,6},{16,8},{18,... | collective-permute-start | bytes 786440 | tf_op jit(solution)/shard_map/ppermute | solution.py:307
  230.0 25.4 %collective-permute-start.20 = (bf16[128,544]{1,0:T(8,128)(2,1)S(1)}, bf16[128,544]{1,0:T(8,128)(2,1)S(1)}, u32[]{:S(2)}, u32[]{:S(2)}) collective-permute-start(bf16[128,544]{1,0:T(8,128)(2,1)S(1)} %get-tuple-element.45), channel_id=1, source_target_pairs={{0,2},{2,0},{4,6},{6,4},{8,10},{10,8},{12,14},{14,12},{16,18},{18,... | collective-permute-start | bytes 417800 | tf_op jit(solution)/shard_map/ppermute | solution.py:307
  230.6 24.8 %collective-permute-start.22 = (bf16[128,544]{1,0:T(8,128)(2,1)S(1)}, bf16[128,544]{1,0:T(8,128)(2,1)S(1)}, u32[]{:S(2)}, u32[]{:S(2)}) collective-permute-start(bf16[128,544]{1,0:T(8,128)(2,1)S(1)} %get-tuple-element.46), channel_id=1, source_target_pairs={{0,4},{2,6},{4,0},{6,2},{8,12},{10,14},{12,8},{14,10},{16,20},{18,... | collective-permute-start | bytes 417800 | tf_op jit(solution)/shard_map/ppermute | solution.py:307
  259.9 16.4 %all-to-all-start.4 = ((bf16[4,128,1024]{2,1,0:T(8,128)(2,1)}), bf16[4,128,1024]{2,1,0:T(8,128)(2,1)}, u32[]{:S(2)}, u32[]{:S(2)}) async-start(bf16[4,128,1024]{2,1,0:T(8,128)(2,1)} %bitcast.23), calls=%async_computation.4 | async-start | bytes 2097152 | tf_op jit(solution)/shard_map/all_to_all | solution.py:329
  267.4 17.0 %collective-permute-start.24 = (bf16[256,544]{0,1:T(8,128)(2,1)}, bf16[256,544]{0,1:T(8,128)(2,1)}, u32[]{:S(2)}, u32[]{:S(2)}) collective-permute-start(bf16[256,544]{0,1:T(8,128)(2,1)} %copy.55), channel_id=1, source_target_pairs={{0,1},{1,0},{2,3},{3,2},{4,5},{5,4},{6,7},{7,6},{8,9},{9,8},{10,11... | collective-permute-start | bytes 835592 | tf_op jit(solution)/shard_map/ppermute | solution.py:320
  292.3 15.9 %collective-permute-start.29 = (f32[23,256]{1,0:T(8,128)S(1)}, f32[23,256]{1,0:T(8,128)S(1)}, u32[]{:S(2)}, u32[]{:S(2)}) collective-permute-start(f32[23,256]{1,0:T(8,128)S(1)} %bitcast.109), channel_id=1, source_target_pairs={{0,8},{2,10},{4,12},{6,14},{8,16},{10,18},{12,20},{14,22},{16,24},... | collective-permute-start | bytes 70664 | tf_op jit(solution)/shard_map/ppermute | solution.py:306
  294.4 13.9 %collective-permute-start.30 = (f32[23,256]{1,0:T(8,128)S(1)}, f32[23,256]{1,0:T(8,128)S(1)}, u32[]{:S(2)}, u32[]{:S(2)}) collective-permute-start(f32[23,256]{1,0:T(8,128)S(1)} %bitcast.108), channel_id=1, source_target_pairs={{0,16},{2,18},{4,20},{6,22},{8,24},{10,26},{12,28},{14,30},{16,0},... | collective-permute-start | bytes 70664 | tf_op jit(solution)/shard_map/ppermute | solution.py:306
  295.4 12.9 %collective-permute-start.31 = (f32[23,256]{1,0:T(8,128)S(1)}, f32[23,256]{1,0:T(8,128)S(1)}, u32[]{:S(2)}, u32[]{:S(2)}) collective-permute-start(f32[23,256]{1,0:T(8,128)S(1)} %bitcast.107), channel_id=1, source_target_pairs={{0,24},{2,26},{4,28},{6,30},{8,0},{10,2},{12,4},{14,6},{16,8},{18,... | collective-permute-start | bytes 70664 | tf_op jit(solution)/shard_map/ppermute | solution.py:306
  299.2 15.4 %all-to-all-start.3 = ((bf16[4,128,1024]{2,1,0:T(8,128)(2,1)}), bf16[4,128,1024]{2,1,0:T(8,128)(2,1)S(1)}, u32[]{:S(2)}, u32[]{:S(2)}) async-start(bf16[4,128,1024]{2,1,0:T(8,128)(2,1)} %bitcast.21), calls=%async_computation.3 | async-start | bytes 2097152 | tf_op jit(solution)/shard_map/all_to_all | solution.py:329
  (49 other events, 431.1 us)

commit v2 on v1

--- a/solution.py
+++ b/solution.py
@@ -14,9 +14,13 @@
 GROUP = 8
 UNROLL = 4
 BLOCK = 32
+COLUMNS = 256
+LAST = 16
 LOG2E = 1.4426950408889634
 LN2 = 0.6931471805599453
 VMEM_LIMIT = 58 * 1024 * 1024
+VMEM_MIDDLE = 36 * 1024 * 1024
+VMEM_SMALL = 24 * 1024 * 1024
 F32 = jnp.float32
 BF16 = jnp.bfloat16
 
@@ -48,15 +52,48 @@
     )
 
 
-def local_kernel(b, c, low, dtw, dtb, act, g, alog, step_out, sig_out, ends_out, a2, us, gs):
+def join_halves(core, mine, other, out):
+    half = mine.shape[1]
+    for which, (first, second) in enumerate(((mine, other), (other, mine))):
+
+        @pl.when(core[0] == which)
+        def _():
+            out[:, :half] = first[...].astype(out.dtype)
+            out[:, half:] = second[...].astype(out.dtype)
+
+
+def spread_rows(bc, out):
+    values = bc[...].T
+    high = values.astype(BF16)
+    rest = values - high.astype(F32)
+    middle = rest.astype(BF16)
+    lowest = (rest - middle.astype(F32)).astype(BF16)
+    parts = jnp.concatenate([high, middle, lowest], axis=1)
+    count = bc.shape[0]
+    column = lax.broadcasted_iota(jnp.int32, (3 * count, LANES), 0) % count
+    for n in range(count):
+        pick_n = jnp.where(column == n, 1.0, 0.0).astype(BF16)
+        out[n] = jnp.dot(parts, pick_n, preferred_element_type=F32)
+
+
+def local_kernel(
+    core, mine, other, dtw, dtb, act, g, alog, step_out, sig_out, state_out, adjoint_out,
+    a2, us, gs, spread, low, bc,
+):
     tokens, width = act.shape
+    rank = dtw.shape[0]
+    join_halves(core, mine.at[:rank], other.at[:rank], low)
+    join_halves(core, mine.at[rank:], other.at[rank:], bc)
+    spread_rows(bc, spread)
     rows = width // LANES
     block = min(tokens, BLOCK)
     a2[...] = (-LOG2E * jnp.exp(alog[...])).reshape(STATE, rows, LANES)
 
     for column in range(0, width, 256):
         columns = slice(column, column + 256)
-        sig_out[:, columns] = jnp.dot(low[...], dtw[:, columns], preferred_element_type=F32)
+        sig_out[:, columns] = lax.dot_general(
+            low[...], dtw[:, columns], (((0,), (0,)), ((), ())), preferred_element_type=F32
+        )
 
     def prepare(i, total):
         at = pl.ds(pl.multiple_of(i * block, block), block)
@@ -69,9 +106,9 @@
         gs[at] = g[at, :].astype(F32).reshape(block, rows, LANES)
         return total + jnp.sum(step, axis=0, keepdims=True)
 
-    ends_out[2 * STATE : 2 * STATE + 1, :] = lax.fori_loop(
-        0, tokens // block, prepare, jnp.zeros((1, width), F32)
-    )
+    total = lax.fori_loop(0, tokens // block, prepare, jnp.zeros((1, width), F32))
+    state_out[STATE : STATE + 1, :] = total
+    adjoint_out[STATE : STATE + 1, :] = total
     zeros = jnp.zeros((8, LANES), F32)
     ones = jnp.ones((8, LANES), F32)
     for r in range(0, rows, 8):
@@ -85,9 +122,9 @@
                 for k in range(GROUP):
                     n = base + k
                     d = jnp.exp2(s * a2[n, part, :])
-                    h[k] = d * h[k] + b[t, n : n + 1, :] * u
+                    h[k] = d * h[k] + spread[n, pl.ds(t, 1), :] * u
                     p[k] = d * p[k]
-                    lam[k] = lam[k] + (c[t, n : n + 1, :] * g_now) * p[k]
+                    lam[k] = lam[k] + (spread[STATE + n, pl.ds(t, 1), :] * g_now) * p[k]
                 return tuple(h), tuple(p), tuple(lam)
 
             h, _, lam = lax.fori_loop(
@@ -97,17 +134,20 @@
             columns = slice(r * LANES, (r + 8) * LANES)
             for k in range(GROUP):
                 n = base + k
-                ends_out[n : n + 1, columns] = h[k].reshape(1, 8 * LANES)
-                ends_out[STATE + n : STATE + n + 1, columns] = lam[k].reshape(1, 8 * LANES)
+                state_out[n : n + 1, columns] = h[k].reshape(1, 8 * LANES)
+                adjoint_out[n : n + 1, columns] = lam[k].reshape(1, 8 * LANES)
 
 
 def full_kernel(
-    b, c, step, sig, act, g, alog, carries, skip,
-    mixed_out, pre_out, act_out, rate_out, vec_out, bc_out,
-    a2, acts, gs, hist, mixed, s1, s2, gb, gc,
+    core, mine, other, dtw, step, sig, act, g, alog, carries, skip,
+    mixed_out, pre_out, act_out, rate_out, vec_out, mine_out, other_out,
+    a2, acts, gs, hist, mixed, s1, s2, gb, gc, spread, both_rows, bc,
 ):
     tokens, rows, _ = step.shape
     width = rows * LANES
+    rank = dtw.shape[0]
+    join_halves(core, mine, other, bc)
+    spread_rows(bc, spread)
     block = min(tokens, BLOCK)
     dense, flat = (block, rows, LANES), (block, width)
     a2[...] = (-LOG2E * jnp.exp(alog[...])).reshape(STATE, rows, LANES)
@@ -134,9 +174,9 @@
             for k in range(GROUP):
                 n = base + k
                 d = jnp.exp2(s * a2[n])
-                h[k] = d * h[k] + b[t, n : n + 1, :] * u
+                h[k] = d * h[k] + spread[n, pl.ds(t, 1), :] * u
                 hist[t + 1, k] = h[k]
-                total = total + c[t, n : n + 1, :] * h[k]
+                total = total + spread[STATE + n, pl.ds(t, 1), :] * h[k]
             mixed[t] = total
             gc[t, group, :] = row_sums([g_now * part for part in h])
             return tuple(h)
@@ -158,8 +198,8 @@
             products = []
             for k in range(GROUP):
                 n = base + k
-                lam = c[t, n : n + 1, :] * g_now + m[k]
-                total1 = total1 + b[t, n : n + 1, :] * lam
+                lam = spread[STATE + n, pl.ds(t, 1), :] * g_now + m[k]
+                total1 = total1 + spread[n, pl.ds(t, 1), :] * lam
                 products.append(lam * u)
                 m[k] = jnp.exp2(s * a2[n]) * lam
                 q = m[k] * hist[t, k]
@@ -197,7 +237,7 @@
                 preferred_element_type=F32,
             ).reshape(block, STATE, LANES)
             both = both + jnp.sum(jnp.where(lane == state + offset, sums, 0.0), axis=1)
-        bc_out[at, :] = both
+        both_rows[at, :] = both
         return (
             totals[0] + jnp.sum(grad_pre, axis=0, keepdims=True),
             totals[1] + jnp.sum(g_now * act_now, axis=0),
@@ -208,44 +248,67 @@
     )
     vec_out[0:1, :] = bias
     vec_out[1:2, :] = gain.reshape(1, width)
-
-
-def scan_local(b, c, low, dtw, dtb, act, g, alog):
+    half = tokens // 2
+    for which, out in ((core[0], mine_out), (1 - core[0], other_out)):
+        at = pl.ds(pl.multiple_of(which * half, half), half)
+        out[:rank, :] = lax.dot_general(
+            dtw[...], pre_out[at, :], (((1,), (1,)), ((), ())), preferred_element_type=F32
+        )
+        out[rank:, :] = both_rows[at, :].T[: 2 * STATE]
+
+
+def took(microseconds):
+    return pl.CostEstimate(
+        flops=0, bytes_accessed=int(microseconds * 3.6e6), transcendentals=0
+    )
+
+
+def vmem_specs(count):
+    return [pl.BlockSpec(memory_space=pltpu.VMEM)] * count
+
+
+def scan_local(core, mine, other, dtw, dtb, act, g, alog):
     tokens, channels = act.shape
     dense = (tokens, channels // LANES, LANES)
-    operands = (b, c, low, dtw, dtb, act, g, alog)
+    operands = (core, mine, other, dtw, dtb, act, g, alog)
+    ends = jax.ShapeDtypeStruct((STATE + 1, channels), F32)
     return pl.pallas_call(
         local_kernel,
-        in_specs=[pl.BlockSpec(memory_space=pltpu.VMEM)] * len(operands),
+        in_specs=[pl.BlockSpec(memory_space=pltpu.SMEM)] + vmem_specs(len(operands) - 1),
         out_shape=[
-            jax.ShapeDtypeStruct(dense, F32),
-            jax.ShapeDtypeStruct((tokens, channels), F32),
-            jax.ShapeDtypeStruct((2 * STATE + 1, channels), F32),
+            jax.ShapeDtypeStruct(dense, F32), jax.ShapeDtypeStruct((tokens, channels), F32), ends, ends,
         ],
         scratch_shapes=[
             pltpu.VMEM((STATE,) + dense[1:], F32), pltpu.VMEM(dense, F32), pltpu.VMEM(dense, F32),
+            pltpu.VMEM((2 * STATE, tokens, LANES), F32), pltpu.VMEM((dtw.shape[0], tokens), BF16),
+            pltpu.VMEM((2 * STATE, tokens), F32),
         ],
-        compiler_params=pltpu.CompilerParams(vmem_limit_bytes=VMEM_LIMIT),
+        compiler_params=pltpu.CompilerParams(vmem_limit_bytes=VMEM_MIDDLE),
+        cost_estimate=took(22),
         name="scan_local",
     )(*operands)
 
 
-def scan_full(b, c, step, sig, act, g, alog, carries, skip):
+def scan_full(core, mine, other, dtw, step, sig, act, g, alog, carries, skip):
     tokens, channels = act.shape
     dense = (tokens, channels // LANES, LANES)
     flat = (tokens, channels)
-    operands = (b, c, step, sig, act, g, alog, carries, skip)
+    operands = (
+        core, mine[dtw.shape[0] :], other[dtw.shape[0] :], dtw, step, sig, act, g, alog, carries, skip
+    )
     small = pltpu.VMEM((tokens, STATE, LANES), F32)
+    half = jax.ShapeDtypeStruct((dtw.shape[0] + 2 * STATE, tokens // 2), F32)
     return pl.pallas_call(
         full_kernel,
-        in_specs=[pl.BlockSpec(memory_space=pltpu.VMEM)] * len(operands),
+        in_specs=[pl.BlockSpec(memory_space=pltpu.SMEM)] + vmem_specs(len(operands) - 1),
         out_shape=[
             jax.ShapeDtypeStruct(flat, BF16),
             jax.ShapeDtypeStruct(flat, BF16),
             jax.ShapeDtypeStruct(flat, F32),
             jax.ShapeDtypeStruct((STATE, channels), F32),
             jax.ShapeDtypeStruct((2, channels), F32),
-            jax.ShapeDtypeStruct((tokens, LANES), F32),
+            half,
+            half,
         ],
         scratch_shapes=[
             pltpu.VMEM((STATE,) + dense[1:], F32),
@@ -257,8 +320,12 @@
             pltpu.VMEM(dense, F32),
             small,
             small,
+            pltpu.VMEM((2 * STATE, tokens, LANES), F32),
+            pltpu.VMEM((tokens, LANES), F32),
+            pltpu.VMEM((2 * STATE, tokens), F32),
         ],
         compiler_params=pltpu.CompilerParams(vmem_limit_bytes=VMEM_LIMIT),
+        cost_estimate=took(51),
         name="scan_full",
     )(*operands)
 
@@ -329,24 +396,75 @@
     return lax.all_to_all(x, "ctx", 0, 0, axis_index_groups=plane_groups(), tiled=True)
 
 
-def by_owner(x):
+def pack_kernel(share, *refs):
+    *inputs, out = refs
+    row = 0
+    for x in inputs:
+        rows = slice(row, row + x.shape[0])
+        row += x.shape[0]
+        for q in range(PLANE):
+            for z in range(out.shape[2] // share):
+                source = (z * PLANE + q) * share
+                out[q, rows, z * share : (z + 1) * share] = x[:, source : source + share]
+
+
+def unpack_kernel(share, x, *outs):
+    row = 0
+    for out in outs:
+        rows = slice(row, row + out.shape[0])
+        row += out.shape[0]
+        for q in range(PLANE):
+            for z in range(x.shape[2] // share):
+                target = (z * PLANE + q) * share
+                out[:, target : target + share] = x[q, rows, z * share : (z + 1) * share].astype(
+                    out.dtype
+                )
+
+
+def along_line(x):
+    count = lax.axis_size("ctx")
+    groups = [list(range(i, count, PLANE)) for i in range(PLANE)]
+    return lax.all_to_all(x, "ctx", 0, 0, axis_index_groups=groups, tiled=True)
+
+
+def by_owner(*arrays):
+    channels = arrays[0].shape[1]
+    rows = sum(x.shape[0] for x in arrays)
+    share = channels // lax.axis_size("ctx")
+    return pl.pallas_call(
+        functools.partial(pack_kernel, share),
+        in_specs=vmem_specs(len(arrays)),
+        out_specs=vmem_specs(1)[0],
+        out_shape=jax.ShapeDtypeStruct((PLANE, rows, channels // PLANE), arrays[0].dtype),
+        cost_estimate=took(2),
+        name="pack",
+    )(*arrays)
+
+
+def to_tokens(x, *results):
+    channels = x.shape[2]
+    share = channels * PLANE // lax.axis_size("ctx")
+    return pl.pallas_call(
+        functools.partial(unpack_kernel, share),
+        in_specs=vmem_specs(1),
+        out_specs=vmem_specs(len(results)),
+        out_shape=[
+            jax.ShapeDtypeStruct((rows, PLANE * channels), dtype) for rows, dtype in results
+        ],
+        cost_estimate=took(2),
+        name="unpack",
+    )(x)
+
+
+def rim_before(x):
     count = lax.axis_size("ctx")
     rows, channels = x.shape
-    x = x.reshape(rows, count // PLANE, PLANE, channels // count).transpose(2, 0, 1, 3)
-    return x.reshape(PLANE, rows, channels // PLANE)
-
-
-def to_channels(x):
-    rows, channels = x.shape
-    return in_plane(by_owner(x)).reshape(PLANE * rows, channels // PLANE)
-
-
-def to_tokens(x):
-    count = lax.axis_size("ctx")
-    rows, channels = x.shape
-    x = in_plane(x.reshape(PLANE, rows // PLANE, channels))
-    x = x.reshape(PLANE, rows // PLANE, count // PLANE, PLANE * channels // count)
-    return x.transpose(1, 2, 0, 3).reshape(rows // PLANE, PLANE * channels)
+    x = x.reshape(rows, count // PLANE, PLANE, channels // count)
+    parts = []
+    for q in range(PLANE):
+        route = [(i - 1, i + q) for i in range(PLANE, count, PLANE)]
+        parts.append(send(x[:, :, q].reshape(rows, channels // PLANE), route))
+    return functools.reduce(jnp.add, parts)
 
 
 def own_channels(x):
@@ -357,63 +475,184 @@
     return x.reshape(rows, channels // PLANE)
 
 
-def gather_line(x):
+def line_blocks(x):
+    planes = lax.axis_size("ctx") // PLANE
+    return [send(x, line_route(-k)) if k else x for k in range(planes)]
+
+
+def place_blocks(blocks, axis):
+    planes = len(blocks)
+    mine = lax.axis_index("ctx") // PLANE
+    size = blocks[0].shape[axis]
+    shape = list(blocks[0].shape)
+    shape[axis] = planes * size
+    out = jnp.zeros(shape, blocks[0].dtype)
+    for k, block in enumerate(blocks):
+        at = lax.rem(mine + k, planes) * size
+        out = lax.dynamic_update_slice(out, block, (at, 0) if axis == 0 else (0, at))
+    return out
+
+
+def after(x, *earlier):
+    return lax.optimization_barrier((x,) + earlier)[0]
+
+
+def pick(x, at, axis=0):
+    return lax.dynamic_index_in_dim(x, at, axis, keepdims=False)
+
+
+def sum_plane(mine, other, *earlier):
+    core = lax.axis_index("mp")
+    mine = mine + swap_mp(other)
+    half = after(mine.astype(BF16), *earlier)
+    routes = [[(i, i ^ bits) for i in range(lax.axis_size("ctx"))] for bits in range(1, PLANE)]
+    total = mine
+    for route in routes:
+        total = total + send(half, route).astype(F32)
+    return total, swap_mp(total)
+
+
+def by_halves(mine, other):
+    core = lax.axis_index("mp")
+    return jnp.where(
+        core == 0, jnp.concatenate([mine, other], axis=1), jnp.concatenate([other, mine], axis=1)
+    )
+
+
+def fill_padded(moved, before, padded, columns):
+    rows = padded.shape[0] // PLANE // 8 * 8
+    padded[8 - before.shape[0] : 8, columns] = before[:, columns].astype(F32)
+    for q in range(PLANE):
+        padded[8 + q * rows : 8 + (q + 1) * rows, columns] = moved[q, :rows, columns].astype(F32)
+
+
+def taps(padded, weight, bias, start, rows, columns):
+    first = 8 - (CONV - 1) + start
+    total = bias[:, columns]
+    for k in range(CONV):
+        total = total + weight[k : k + 1, columns] * padded[first + k : first + k + rows, columns]
+    return total
+
+
+def head_kernel(moved, before, weight, bias, act_out, padded):
+    tokens, width = act_out.shape
+    rows = tokens // PLANE
+    for column in range(0, width, COLUMNS):
+        columns = slice(column, column + COLUMNS)
+        fill_padded(moved, before, padded, columns)
+        for start in range(0, tokens, rows):
+            value = taps(padded, weight, bias, start, rows, columns)
+            act_out[start : start + rows, columns] = (value / (1.0 + jnp.exp(-value))).astype(BF16)
+
+
+def conv_head(moved, before, weight, bias, rows):
+    channels = moved.shape[2]
+    operands = (moved, before, weight, bias)
+    return pl.pallas_call(
+        head_kernel,
+        in_specs=vmem_specs(len(operands)),
+        out_shape=jax.ShapeDtypeStruct((PLANE * rows, channels), BF16),
+        out_specs=vmem_specs(1)[0],
+        scratch_shapes=[pltpu.VMEM((PLANE * rows + 8, channels), F32)],
+        compiler_params=pltpu.CompilerParams(vmem_limit_bytes=VMEM_SMALL),
+        cost_estimate=took(4),
+        name="conv_head",
+    )(*operands)
+
+
+def tail_kernel(
+    core, mine, other, rows_proj, grad_act, moved, before, weight, bias, dt_parts,
+    packed_out, sums_out, last_out, grad, padded, grad_proj,
+):
+    tokens, width = grad_act.shape
+    rows = tokens // PLANE
+    rim = CONV - 1
+    join_halves(core, mine, other, grad_proj)
+    dt_rows = packed_out.shape[1] - rows
+    for q in range(PLANE):
+        at = slice(q * dt_rows, (q + 1) * dt_rows)
+        total = dt_parts[0, at, :].astype(F32)
+        for z in range(1, dt_parts.shape[0]):
+            total = total + dt_parts[z, at, :].astype(F32)
+        packed_out[q, rows:, :] = total.astype(BF16)
+    for column in range(0, width, COLUMNS):
+        columns = slice(column, column + COLUMNS)
+        fill_padded(moved, before, padded, columns)
+        grad[:tokens, columns] = lax.dot_general(
+            grad_proj[...], rows_proj[:, columns], (((0,), (0,)), ((), ())),
+            preferred_element_type=F32,
+        )
+        grad[tokens:, columns] = jnp.zeros((8, COLUMNS), F32)
+        sums = [jnp.zeros((8, COLUMNS), F32)] * (CONV + 1)
+        fold = lambda x: functools.reduce(jnp.add, [x[r : r + 8] for r in range(0, x.shape[0], 8)])
+        piece = rows // 4
+        for start in range(0, tokens, piece):
+            at = slice(start, start + piece)
+            shifts = [
+                padded[8 - rim + k + start : 8 - rim + k + start + piece, columns]
+                for k in range(CONV)
+            ]
+            value = bias[:, columns]
+            for k in range(CONV):
+                value = value + weight[k : k + 1, columns] * shifts[k]
+            s = 1.0 / (1.0 + jnp.exp(-value))
+            now = (grad_act[at, columns] + grad[at, columns]) * (s * (1.0 + value * (1.0 - s)))
+            grad[at, columns] = now
+            for k in range(CONV):
+                sums[k] = sums[k] + fold(now * shifts[k])
+            sums[CONV] = sums[CONV] + fold(now)
+        for k in range(CONV + 1):
+            sums_out[k : k + 1, columns] = jnp.sum(sums[k], axis=0, keepdims=True)
+        for start in range(0, tokens, piece):
+            total = jnp.zeros((piece, COLUMNS), F32)
+            for k in range(CONV):
+                first = rim - k + start
+                total = total + weight[k : k + 1, columns] * grad[first : first + piece, columns]
+            to = start % rows
+            packed_out[start // rows, to : to + piece, columns] = total.astype(BF16)
+        last_out[:, columns] = total[piece - LAST :]
+
+
+def conv_tail(core, mine, other, rows_proj, grad_act, moved, before, weight, bias, dt_parts):
+    tokens, channels = grad_act.shape
+    operands = (core, mine, other, rows_proj, grad_act, moved, before, weight, bias, dt_parts)
+    return pl.pallas_call(
+        tail_kernel,
+        in_specs=[pl.BlockSpec(memory_space=pltpu.SMEM)] + vmem_specs(len(operands) - 1),
+        out_shape=[
+            jax.ShapeDtypeStruct(moved.shape, BF16),
+            jax.ShapeDtypeStruct((CONV + 1, channels), F32),
+            jax.ShapeDtypeStruct((LAST, channels), F32),
+        ],
+        scratch_shapes=[
+            pltpu.VMEM((tokens + 8, channels), F32),
+            pltpu.VMEM((tokens + 8, channels), F32),
+            pltpu.VMEM((mine.shape[0], tokens), BF16),
+        ],
+        compiler_params=pltpu.CompilerParams(vmem_limit_bytes=VMEM_SMALL),
+        cost_estimate=took(8),
+        name="conv_tail",
+    )(*operands)
+
+
+def line_carries(state, adjoint, a_log):
     planes = lax.axis_size("ctx") // PLANE
     mine = lax.axis_index("ctx") // PLANE
-    rows = x.shape[0]
-    out = jnp.zeros((planes * rows, x.shape[1]), x.dtype)
-    for k in range(planes):
-        block = send(x, line_route(-k)) if k else x
-        out = lax.dynamic_update_slice(out, block, (lax.rem(mine + k, planes) * rows, 0))
-    return out
-
-
-def pick(x, at, axis=0):
-    return lax.dynamic_index_in_dim(x, at, axis, keepdims=False)
-
-
-def sum_plane(x):
-    core = lax.axis_index("mp")
-    halves = x.reshape(2, x.shape[0] // 2, x.shape[1])
-    mine = pick(halves, core) + swap_mp(pick(halves, 1 - core))
-    middle = mine.shape[0] // 2
-    a, b = mine[:middle], mine[middle:]
-    a, b = a + send(a, flip_route(1), BF16), b + send(b, flip_route(2), BF16)
-    a, b = a + send(a, flip_route(2), BF16), b + send(b, flip_route(1), BF16)
-    mine = jnp.concatenate([a, b], axis=0)
-    other = swap_mp(mine)
-    return jnp.where(
-        core == 0, jnp.concatenate([mine, other], axis=0), jnp.concatenate([other, mine], axis=0)
-    )
-
-
-def line_carries(ends, a_log):
-    count = lax.axis_size("ctx")
     rates = -jnp.exp(a_log)
-    state, adjoint, total = ends[:STATE], ends[STATE : 2 * STATE], ends[2 * STATE :]
-
-    def enter(x, direction):
-        x = jnp.concatenate([x, total], axis=0)
-        carry = jnp.zeros((STATE, x.shape[1]), F32)
-        parts = []
-        for k in range(1, count // PLANE):
-            step = direction * PLANE * k
-            route = [(i, i + step) for i in range(count) if 0 <= i + step < count]
-            parts.append(send(x, route))
-        for part in reversed(parts):
-            carry = jnp.exp(rates * part[STATE:]) * carry + part[:STATE]
-        return carry
-
-    return jnp.concatenate([enter(state, 1), enter(adjoint, -1)], axis=0)
-
-
-def scatter_line(parts):
-    planes = lax.axis_size("ctx") // PLANE
-    mine = lax.axis_index("ctx") // PLANE
-    total = parts(mine)
-    for k in sorted(range(1, planes), key=lambda k: -min(k, planes - k)):
-        total = total + send(parts(lax.rem(mine + k, planes)), line_route(k), BF16)
-    return total
+    parts = {}
+    for k in range(1, planes):
+        parts[k] = send(jnp.where(mine + k < planes, state, adjoint), line_route(k))
+    entering = []
+    for order, valid in (
+        (range(planes - 1, 0, -1), lambda k: mine - k >= 0),
+        (range(1, planes), lambda k: mine - k < 0),
+    ):
+        carry = jnp.zeros((STATE, state.shape[1]), F32)
+        for k in order:
+            new = jnp.exp(rates * parts[k][STATE:]) * carry + parts[k][:STATE]
+            carry = jnp.where(valid(k), new, carry)
+        entering.append(carry)
+    return jnp.concatenate(entering, axis=0)
 
 
 def sum_line(x):
@@ -453,17 +692,6 @@
     )
 
 
-def spread(x):
-    return jnp.broadcast_to(x[:, :, None], x.shape + (LANES,))
-
-
-def split_proj(projected):
-    low = projected[:, :RANK].astype(BF16)
-    b = spread(projected[:, RANK : RANK + STATE])
-    c = spread(projected[:, RANK + STATE :])
-    return low, b, c
-
-
 def matmul(x, y, dims):
     return lax.dot_general(x, y, ((dims[:1], dims[1:]), ((), ())), preferred_element_type=F32)
 
@@ -486,45 +714,68 @@
     proj_weight, dt_weight, dt_bias, a_log, skip_gain,
 ):
     rim = CONV - 1
-    seq = to_channels(seq_in)
-    rows_proj = gather_line(proj_weight)
-    grad_mixed, gate_factor = gate_parts(gate_in, upstream, forget_flags)
-    rows_dt = gather_line(in_plane(by_owner(dt_weight)).reshape(-1, seq.shape[1]))
-    grad_mixed = to_channels(grad_mixed)
+    core = lax.axis_index("mp")
+    planes = lax.axis_size("ctx") // PLANE
+    here = core.astype(jnp.int32).reshape(1)
+    rows, dt_rows = seq_in.shape[0], dt_weight.shape[0]
+    half = PLANE * rows // 2
+    packed = by_owner(seq_in, dt_weight)
+    proj_blocks = line_blocks(after(proj_weight.T, packed))
+    moved = in_plane(packed)
+    before = rim_before(seq_in[rows - rim :])
     weight, bias, step_bias, rates, gain = (
         own_channels(x)
         for x in (conv_weight, conv_bias[None], dt_bias[None], a_log, skip_gain[None])
     )
-    length = seq.shape[0]
-    padded = jnp.concatenate([shifted(seq[length - rim :], "ctx", PLANE), seq], axis=0)
-    pre_act = conv_forward(padded, weight, bias, length)
-    act = jax.nn.silu(pre_act).astype(BF16)
-    low, b, c = split_proj(sum_plane(matmul(act, rows_proj, (1, 0))))
-    step, sig, ends = scan_local(b, c, low, rows_dt, step_bias, act, grad_mixed, rates)
-    carries = line_carries(ends, rates)
-    mixed, grad_pre, grad_act, grad_rate, grad_vecs, grad_bc = scan_full(
-        b, c, step, sig, act, grad_mixed, rates, carries, gain
-    )
-    grad_low = matmul(grad_pre, rows_dt, (1, 1))
-    grad_proj = sum_plane(
-        jnp.concatenate([grad_low, grad_bc[:, : 2 * STATE]], axis=1)
-    ).astype(BF16)
-    planes = lax.axis_size("ctx") // PLANE
-
-    def dt_part(zt):
-        part = lax.dynamic_slice_in_dim(low, zt * (RANK // planes), RANK // planes, axis=1)
-        return matmul(part, grad_pre, (0, 0))
-
-    grad_dtw = to_tokens(scatter_line(dt_part).astype(BF16)).astype(F32)
-    grad_gate = (gate_factor * to_tokens(mixed).astype(F32)).astype(BF16)
-    grad_pre_act = (grad_act + matmul(grad_proj, rows_proj, (1, 1))) * silu_parts(pre_act)[1]
-    grad_padded = jnp.concatenate(
-        [grad_pre_act, shifted(grad_pre_act[:rim], "ctx", -PLANE)], axis=0
-    )
-    grad_seq = to_tokens(conv_backward(grad_padded, weight, length))
-    sums = sum_line(
-        jnp.concatenate([conv_sums(grad_pre_act, padded), grad_vecs, grad_rate], axis=0)
-    )
+    act = conv_head(moved, before, weight, bias, rows)
+    dt_plane = moved[:, rows:].reshape(PLANE * dt_rows, -1)
+    grad_mixed, gate_factor = gate_parts(gate_in, upstream, forget_flags)
+    mixed_packed = by_owner(grad_mixed)
+    grad_mixed = in_plane(after(mixed_packed, moved)).reshape(PLANE * rows, -1)
+
+    proj_blocks = after(tuple(proj_blocks), act, mixed_packed, dt_plane)
+    rows_proj = place_blocks(proj_blocks, 1)
+    dt_blocks = line_blocks(dt_plane)
+    part = lambda at: matmul(rows_proj, lax.dynamic_slice_in_dim(act, at * half, half), (1, 1))
+    mine, other = sum_plane(part(core), part(1 - core))
+    rows_dt = place_blocks(dt_blocks, 0)
+    step, sig, state, adjoint = scan_local(
+        here, mine, other, rows_dt, step_bias, act, grad_mixed, rates
+    )
+    low = by_halves(mine[:RANK].astype(BF16), other[:RANK].astype(BF16))
+    carries = line_carries(state, adjoint, rates)
+    mixed, grad_pre, grad_act, grad_rate, grad_vecs, grad_mine, grad_other = scan_full(
+        here, mine, other, rows_dt, step, sig, act, grad_mixed, rates, carries, gain
+    )
+
+    dtw_sums = matmul(low, grad_pre, (1, 0)).astype(BF16)
+    dtw_moved = along_line(dtw_sums.reshape(planes, RANK // planes, -1))
+    mine, other = sum_plane(grad_mine, grad_other, dtw_sums)
+    mine, other = mine.astype(BF16), other.astype(BF16)
+    first = 16
+    start = jnp.where(core == 0, mine[:, :first], other[:, :first])
+    first_pre = conv_forward(
+        jnp.concatenate([before, moved[0, :first]], axis=0), weight, bias, first
+    )
+    grad_first = grad_act[:first] + matmul(start, rows_proj, (0, 0))
+    following = shifted((grad_first * silu_parts(first_pre)[1])[:rim], "ctx", -PLANE)
+    packed, grad_conv, last = conv_tail(
+        here, mine, other, rows_proj, grad_act, moved, before, weight, bias, dtw_moved
+    )
+    following = after(following, last)
+    late = [
+        sum(weight[k] * following[j - k] for k in range(j + 1)) for j in range(rim)
+    ]
+    late = last + jnp.pad(jnp.stack(late), ((LAST - rim, 0), (0, 0)))
+    grad_gate = in_plane(after(mixed, mine).reshape(PLANE, rows, -1))
+    packed = lax.dynamic_update_slice(
+        after(packed, grad_gate), late.astype(BF16)[None], (PLANE - 1, rows - LAST, 0)
+    )
+    returned = in_plane(packed)
+    sums = sum_line(after(jnp.concatenate([grad_conv, grad_vecs, grad_rate], axis=0), packed))
+    (grad_gate,) = to_tokens(after(grad_gate, packed), (rows, F32))
+    grad_gate = (gate_factor * grad_gate).astype(BF16)
+    grad_seq, grad_dtw = to_tokens(returned, (rows, BF16), (dt_rows, F32))
     return outputs(grad_seq, grad_gate, grad_dtw, sums)
 
 
@@ -539,23 +790,24 @@
     act = jax.nn.silu(pre_act).astype(BF16)
     rows_proj = lax.all_gather(proj_weight, "ctx", axis=0, tiled=True)
     rows_dt = lax.all_gather(dt_weight, "ctx", axis=0, tiled=True)
-    low, b, c = split_proj(lax.psum(matmul(act, rows_proj, (1, 0)), "mp"))
+    projected = lax.psum(matmul(rows_proj, act, (0, 1)), "mp")
+    low = projected[:RANK].astype(BF16)
+    halves = (jnp.zeros((1,), jnp.int32), projected[:, : length // 2], projected[:, length // 2 :])
     grad_mixed, gate_factor = gate_parts(gate_in, upstream, forget_flags)
-    step, sig, ends = scan_local(b, c, low, rows_dt, dt_bias[None], act, grad_mixed, a_log)
-    carries = exchange_carries(ends, a_log)
-    mixed, grad_pre, grad_act, grad_rate, grad_vecs, grad_bc = scan_full(
-        b, c, step, sig, act, grad_mixed, a_log, carries, skip_gain[None]
+    step, sig, state, adjoint = scan_local(
+        *halves, rows_dt, dt_bias[None], act, grad_mixed, a_log
+    )
+    carries = exchange_carries(jnp.concatenate([state[:STATE], adjoint], axis=0), a_log)
+    mixed, grad_pre, grad_act, grad_rate, grad_vecs, first, second = scan_full(
+        *halves, rows_dt, step, sig, act, grad_mixed, a_log, carries, skip_gain[None]
     )
     grad_gate = (gate_factor * mixed.astype(F32)).astype(BF16)
-    grad_low = matmul(grad_pre, rows_dt, (1, 1))
-    grad_proj = lax.psum(
-        jnp.concatenate([grad_low, grad_bc[:, : 2 * STATE]], axis=1), "mp"
-    ).astype(BF16)
-    grad_pre_act = (grad_act + matmul(grad_proj, rows_proj, (1, 1))) * silu_parts(pre_act)[1]
+    grad_proj = lax.psum(jnp.concatenate([first, second], axis=1), "mp").astype(BF16)
+    grad_pre_act = (grad_act + matmul(grad_proj, rows_proj, (0, 1))) * silu_parts(pre_act)[1]
     grad_padded = jnp.concatenate([grad_pre_act, shifted(grad_pre_act[:rim], "ctx", -1)], axis=0)
     grad_seq = conv_backward(grad_padded, conv_weight, length)
     scatter = lambda x, axis: lax.psum_scatter(x, "ctx", scatter_dimension=axis, tiled=True)
-    grad_dtw = scatter(matmul(low, grad_pre, (0, 0)), 0)
+    grad_dtw = scatter(matmul(low, grad_pre, (1, 0)), 0)
     sums = scatter(
         jnp.concatenate([conv_sums(grad_pre_act, padded), grad_vecs, grad_rate], axis=0), 1
     )

time: 323 us -> 253 us (0.78)
  waiting for transfers between devices: 79.8 us -> 40.3 us
  local copies, waits for them, and re-layouts: 65.8 us -> 36 us
  Pallas kernels: 72.1 us -> 89.7 us
  starting transfers between devices: 70 us -> 60 us
  other arithmetic: 19.6 us -> 14.2 us
    ppermute x11 -> x0, waiting for transfers between devices: 24.2 us -> none  [send(): return lax.ppermute(x.astype(dtype), 'ctx', route).astype(x.dtype)]
    pallas_call x2 -> x8, Pallas kernels: 72.1 us -> 89.7 us  [the longest x1 50.9 us: scan_full(): pl.pallas_call(full_kernel, in_specs=[pl.BlockSpec(memory_space=pltpu.SME...]
    reshape x11 -> x2, local copies, waits for them, and re-layouts: 16.2 us -> 0.73 us  [the longest x1 0.68 us: sum_line(): x = x.reshape(x.shape[0], planes, x.shape[1] // planes)]
    all_to_all x6 -> x4, waiting for transfers between devices: 14.9 us -> 1.29 us  [in_plane(): lax.all_to_all(x, 'ctx', 0, 0, axis_index_groups=plane_groups(), tiled=True)]
    all_to_all x6 -> x4, starting transfers between devices: 29.2 us -> 19.1 us  [in_plane(): lax.all_to_all(x, 'ctx', 0, 0, axis_index_groups=plane_groups(), tiled=True)]
    convert_element_type x6 -> x0, local copies, waits for them, and re-layouts: 9.72 us -> none  [the longest x3 8.08 us: plane_body(): grad_gate = (gate_factor * to_tokens(mixed).astype(F32)).astype(BF16)]
    ppermute x11 -> x0, starting transfers between devices: 6.66 us -> none  [send(): return lax.ppermute(x.astype(dtype), 'ctx', route).astype(x.dtype)]
    broadcast_in_dim x4 -> x2, local copies, waits for them, and re-layouts: 6.5 us -> 0.24 us  [place_blocks(): out = jnp.zeros(shape, blocks[0].dtype)]
  transfers between devices with their start and end apart: 38 -> 32, of which waited for: 14 -> 8; matrix products, arithmetic and copies ran while one was open for 16% -> 15% of each run, Pallas kernels for 0% -> 6%
where the time goes in v2:
time: 253 us; the launch traced here: 250 us
  Pallas kernels  89.7 us (35%)
  starting transfers between devices  60 us (24%)
  waiting for transfers between devices  40.3 us (16%)
  local copies, waits for them, and re-layouts  36 us (14%)
  other arithmetic  14.2 us (6%)
  matrix products  7.91 us (3%)
    pallas_call x1, Pallas kernels, scan_full(): pl.pallas_call(full_kernel, in_specs=[pl.BlockSpec(memory_space=pltpu.SME...  50.9 us
    ppermute x22, waiting for transfers between devices, send(): return lax.ppermute(x, 'ctx', route)  33.4 us
    ppermute x22, starting transfers between devices, send(): return lax.ppermute(x, 'ctx', route)  30.5 us
    all_to_all x4, starting transfers between devices, in_plane(): lax.all_to_all(x, 'ctx', 0, 0, axis_index_groups=plane_groups(), tiled=True)  19.1 us
    pallas_call x1, Pallas kernels, scan_local(): pl.pallas_call(local_kernel, in_specs=[pl.BlockSpec(memory_space=pltpu.SM...  19 us
    unnamed x78, local copies, waits for them, and re-layouts  10.7 us
    dot_general x4, matrix products, matmul(): lax.dot_general(x, y, ((dims[:1], dims[1:]), ((), ())), preferred_element...  7.91 us
    pallas_call x1, Pallas kernels, conv_tail(): pl.pallas_call(tail_kernel, in_specs=[pl.BlockSpec(memory_space=pltpu.SME...  7.68 us
  transfers between devices with their start and end apart: 32, of which 8 were waited for; matrix products, arithmetic and copies ran while one was open for 15% of the time, Pallas kernels for 6%

profile of v2, /device:TPU:14, one launch (start us, length us, event | category | flops | bytes accessed | tf_op | source)
XLA Modules:
  0.0 249.6 jit_solution(2788872356540894147)
XLA Ops:
  0.6 2.5 %pack.2 = bf16[4,160,1024]{2,1,0:T(8,128)(2,1)} custom-call(bf16[128,4096]{1,0:T(8,128)(2,1)} %refs_0_.1, bf16[32,4096]{1,0:T(8,128)(2,1)} %refs_1_.1), custom_call_target="tpu_custom_call" | custom-call | bytes 7200000 | tf_op jit(solution)/shard_map/pack/pallas_call | solution.py:434
  3.1 4.3 %all-to-all-start = ((bf16[4,160,1024]{2,1,0:T(8,128)(2,1)}), bf16[4,160,1024]{2,1,0:T(8,128)(2,1)S(1)}, u32[]{:S(2)}, u32[]{:S(2)}) async-start(bf16[4,160,1024]{2,1,0:T(8,128)(2,1)} %pack.2), calls=%async_computation | async-start | bytes 2621440 | tf_op jit(solution)/shard_map/all_to_all | solution.py:396
  15.2 2.6 %collective-permute-start.6 = (bf16[3,1024]{1,0:T(4,128)(2,1)S(1)}, bf16[3,1024]{1,0:T(4,128)(2,1)S(1)}, u32[]{:S(2)}, u32[]{:S(2)}) collective-permute-start(bf16[3,1024]{1,0:T(4,128)(2,1)S(1)} %bitcast.134), channel_id=1, source_target_pairs={{6,14},{14,22},{22,30},{7,15},{15,23},{23,31}} | collective-permute-start | bytes 18440 | tf_op jit(solution)/shard_map/ppermute | solution.py:373
  20.5 12.4 %collective-permute-done.5 = bf16[3,1024]{1,0:T(4,128)(2,1)S(1)} collective-permute-done((bf16[3,1024]{1,0:T(4,128)(2,1)S(1)}, bf16[3,1024]{1,0:T(4,128)(2,1)S(1)}, u32[]{:S(2)}, u32[]{:S(2)}) %collective-permute-start.5) | collective-permute-done | bytes 6176 | tf_op jit(solution)/shard_map/ppermute | solution.py:373
  36.2 2.3 pack.3
  49.3 2.4 fusion.38
  51.8 3.5 %collective-permute-start.8 = (bf16[544,256]{1,0:T(8,128)(2,1)}, bf16[544,256]{1,0:T(8,128)(2,1)}, u32[]{:S(2)}, u32[]{:S(2)}) collective-permute-start(bf16[544,256]{1,0:T(8,128)(2,1)} %get-tuple-element.96), channel_id=1, source_target_pairs={{0,2},{2,0},{4,6},{6,4},{8,10},{10,8},{12,14},{14,12},{16,18},{18,... | collective-permute-start | bytes 835592 | tf_op jit(solution)/shard_map/ppermute | solution.py:373
  58.1 5.1 %all-to-all-start.1 = ((bf16[4,128,1024]{2,1,0:T(8,128)(2,1)}), bf16[4,128,1024]{2,1,0:T(8,128)(2,1)}, u32[]{:S(2)}, u32[]{:S(2)}) async-start(bf16[4,128,1024]{2,1,0:T(8,128)(2,1)} %pack.3), calls=%async_computation.1 | async-start | bytes 2097152 | tf_op jit(solution)/shard_map/all_to_all | solution.py:396
  63.1 4.4 %collective-permute-done.9 = bf16[544,256]{1,0:T(8,128)(2,1)} collective-permute-done((bf16[544,256]{1,0:T(8,128)(2,1)}, bf16[544,256]{1,0:T(8,128)(2,1)}, u32[]{:S(2)}, u32[]{:S(2)}) %collective-permute-start.9) | collective-permute-done | bytes 278560 | tf_op jit(solution)/shard_map/ppermute | solution.py:373
  78.7 4.3 %collective-permute-done.14 = bf16[128,1024]{1,0:T(8,128)(2,1)S(1)} collective-permute-done((bf16[128,1024]{1,0:T(8,128)(2,1)}, bf16[128,1024]{1,0:T(8,128)(2,1)S(1)}, u32[]{:S(2)}, u32[]{:S(2)}) %collective-permute-start.14) | collective-permute-done | bytes 262176 | tf_op jit(solution)/shard_map/ppermute | solution.py:373
  85.9 19.0 %scan_local.1 = (f32[512,8,128]{2,1,0:T(8,128)S(1)}, f32[512,1024]{1,0:T(8,128)S(1)}, f32[17,1024]{1,0:T(8,128)S(1)}, f32[17,1024]{1,0:T(8,128)S(1)}) custom-call(s32[1]{0:T(128)} %bitcast.core, f32[544,256]{1,0:T(8,128)} %convert_add_fusion.1.mine, f32[544,256]{1,0:T(8,128)} %collective-permute-done.11.other, bf16[512,1024]{1,0:T(8,128)(2,1)S(1)} %copy-done.2, ...), custom_call_target="tpu_custom_call" | custom-call | bytes 79200000 | tf_op jit(solution)/shard_map/scan_local/pallas_call | solution.py:275
  119.9 50.9 %scan_full.1 = (bf16[512,1024]{1,0:T(8,128)(2,1)}, bf16[512,1024]{1,0:T(8,128)(2,1)}, f32[512,1024]{1,0:T(8,128)}, f32[16,1024]{1,0:T(8,128)}, f32[2,1024]{1,0:T...) custom-call(s32[1]{0:T(128)} %bitcast.core, f32[32,256]{1,0:T(8,128)} %slice.170.mine, f32[32,256]{1,0:T(8,128)} %slice.171.other, ...), custom_call_target="tpu_custom_call" | custom-call | bytes 183600000 | tf_op jit(solution)/shard_map/scan_full/pallas_call | solution.py:301
  170.8 2.9 %convolution_convert_fusion = bf16[512,1024]{1,0:T(8,128)(2,1)} fusion(bf16[512,1024]{1,0:T(8,128)(2,1)} %get-tuple-element.48, bf16[512,256]{1,0:T(8,128)(2,1)S(1)} %slice.258, bf16[512,256]{1,0:T(8,128)(2,1)S(1)} %slice.259, pred[]{:T(512)S(6)} %eq.10), kind=kOutput, calls=%fused_computation.14 | convolution fusion | flops 539754496 | bytes 2621441 | tf_op jit(solution)/shard_map/dot_general | solution.py:696
  173.7 5.1 %all-to-all-start.2 = ((bf16[4,128,1024]{2,1,0:T(8,128)(2,1)}), bf16[4,128,1024]{2,1,0:T(8,128)(2,1)S(1)}, u32[]{:S(2)}, u32[]{:S(2)}) async-start(bf16[4,128,1024]{2,1,0:T(8,128)(2,1)} %bitcast.111), calls=%async_computation.2 | async-start | bytes 2097152 | tf_op jit(solution)/shard_map/all_to_all | solution.py:427
  183.7 6.9 %collective-permute-done.21 = bf16[544,256]{1,0:T(8,128)(2,1)S(1)} collective-permute-done((bf16[544,256]{1,0:T(8,128)(2,1)S(1)}, bf16[544,256]{1,0:T(8,128)(2,1)S(1)}, u32[]{:S(2)}, u32[]{:S(2)}) %collective-permute-start.21) | collective-permute-done | bytes 278560 | tf_op jit(solution)/shard_map/ppermute | solution.py:373
  190.6 5.2 %collective-permute-done.20 = bf16[544,256]{1,0:T(8,128)(2,1)S(1)} collective-permute-done((bf16[544,256]{1,0:T(8,128)(2,1)S(1)}, bf16[544,256]{1,0:T(8,128)(2,1)S(1)}, u32[]{:S(2)}, u32[]{:S(2)}) %collective-permute-start.20) | collective-permute-done | bytes 278560 | tf_op jit(solution)/shard_map/ppermute | solution.py:373
  198.9 3.3 %all-to-all-done.2.dt_parts = bf16[4,128,1024]{2,1,0:T(8,128)(2,1)S(1)} async-done(((bf16[4,128,1024]{2,1,0:T(8,128)(2,1)}), bf16[4,128,1024]{2,1,0:T(8,128)(2,1)S(1)}, u32[]{:S(2)}, u32[]{:S(2)}) %all-to-all-start.2) | async-done | bytes 1048608 | tf_op jit(solution)/shard_map/all_to_all | solution.py:427
  202.2 5.6 %all-to-all-start.3 = ((bf16[4,128,1024]{2,1,0:T(8,128)(2,1)}), bf16[4,128,1024]{2,1,0:T(8,128)(2,1)}, u32[]{:S(2)}, u32[]{:S(2)}) async-start(bf16[4,128,1024]{2,1,0:T(8,128)(2,1)} %bitcast.110), calls=%async_computation.3 | async-start | bytes 2097152 | tf_op jit(solution)/shard_map/all_to_all | solution.py:396
  209.8 5.2 %collective-permute-start.23 = (f32[3,1024]{1,0:T(4,128)S(1)}, f32[3,1024]{1,0:T(4,128)S(1)}, u32[]{:S(2)}, u32[]{:S(2)}) collective-permute-start(f32[3,1024]{1,0:T(4,128)S(1)} %fusion.28), channel_id=1, source_target_pairs={{8,0},{10,2},{12,4},{14,6},{16,8},{18,10},{20,12},{22,14},{24,16},... | collective-permute-start | bytes 36872 | tf_op jit(solution)/shard_map/ppermute | solution.py:368
  216.7 7.7 %conv_tail.1 = (bf16[4,160,1024]{2,1,0:T(8,128)(2,1)S(1)}, f32[5,1024]{1,0:T(8,128)S(1)}, f32[16,1024]{1,0:T(8,128)S(1)}) custom-call(s32[1]{0:T(128)} %bitcast.core, bf16[544,256]{1,0:T(8,128)(2,1)} %convert_add_fusion.mine, bf16[544,256]{1,0:T(8,128)(2,1)} %collective-permute-done.22.other, ...), custom_call_target="tpu_custom_call" | custom-call | bytes 28800000 | tf_op jit(solution)/shard_map/conv_tail/pallas_call | solution.py:619
  227.6 4.2 %all-to-all-start.4 = ((bf16[4,160,1024]{2,1,0:T(8,128)(2,1)}), bf16[4,160,1024]{2,1,0:T(8,128)(2,1)S(1)}, u32[]{:S(2)}, u32[]{:S(2)}) async-start(bf16[4,160,1024]{2,1,0:T(8,128)(2,1)} %bitcast_dynamic-update-slice_fusion), calls=%async_computation.4 | async-start | bytes 2621440 | tf_op jit(solution)/shard_map/all_to_all | solution.py:396
  235.8 2.7 %unpack.3 = f32[128,4096]{1,0:T(8,128)} custom-call(bf16[4,128,1024]{2,1,0:T(8,128)(2,1)} %all-to-all-done.3.x), custom_call_target="tpu_custom_call" | custom-call | bytes 7200000 | tf_op jit(solution)/shard_map/unpack/pallas_call | solution.py:447
  238.5 3.5 %fusion.9 = bf16[128,4096]{1,0:T(8,128)(2,1)} fusion(f32[128,4096]{1,0:T(8,128)} %unpack.3, bf16[128,4096]{1,0:T(8,128)(2,1)S(1)} %copy-done.16, bf16[128,4096]{1,0:T(8,128)(2,1)S(1)} %copy-done.18, f32[128]{0:T(128)S(1)} %copy-done.27), kind=kLoop, calls=%fused_computation.12 | loop fusion | flops 6815744 | bytes 5243392 | tf_op jit(solution)/shard_map/convert_element_type | solution.py:777
  247.0 2.6 %unpack.2 = (bf16[128,4096]{1,0:T(8,128)(2,1)}, f32[32,4096]{1,0:T(8,128)}) custom-call(bf16[4,160,1024]{2,1,0:T(8,128)(2,1)} %copy-done.14), custom_call_target="tpu_custom_call" | custom-call | bytes 7200000 | tf_op jit(solution)/shard_map/unpack/pallas_call | solution.py:447
  (184 shorter events, 79.4 us)
Async XLA Ops:
  3.1 35.4 %all-to-all-start = ((bf16[4,160,1024]{2,1,0:T(8,128)(2,1)}), bf16[4,160,1024]{2,1,0:T(8,128)(2,1)S(1)}, u32[]{:S(2)}, u32[]{:S(2)}) async-start(bf16[4,160,1024]{2,1,0:T(8,128)(2,1)} %pack.2), calls=%async_computation | async-start | bytes 2621440 | tf_op jit(solution)/shard_map/all_to_all | solution.py:396
  7.5 33.9 %collective-permute-start.2 = (bf16[544,256]{1,0:T(8,128)(2,1)}, bf16[544,256]{1,0:T(8,128)(2,1)}, u32[]{:S(2)}, u32[]{:S(2)}) collective-permute-start(bf16[544,256]{1,0:T(8,128)(2,1)} %bitcast.112), channel_id=1, source_target_pairs={{0,8},{2,10},{4,12},{6,14},{8,16},{10,18},{12,20},{14,22},{16,24},... | collective-permute-start | bytes 835592 | tf_op jit(solution)/shard_map/ppermute | solution.py:373
  9.0 32.3 %collective-permute-start.1 = (bf16[544,256]{1,0:T(8,128)(2,1)}, bf16[544,256]{1,0:T(8,128)(2,1)}, u32[]{:S(2)}, u32[]{:S(2)}) collective-permute-start(bf16[544,256]{1,0:T(8,128)(2,1)} %bitcast.113), channel_id=1, source_target_pairs={{0,16},{2,18},{4,20},{6,22},{8,24},{10,26},{12,28},{14,30},{16,0},... | collective-permute-start | bytes 835592 | tf_op jit(solution)/shard_map/ppermute | solution.py:373
  10.3 31.1 %collective-permute-start = (bf16[544,256]{1,0:T(8,128)(2,1)}, bf16[544,256]{1,0:T(8,128)(2,1)}, u32[]{:S(2)}, u32[]{:S(2)}) collective-permute-start(bf16[544,256]{1,0:T(8,128)(2,1)} %bitcast.114), channel_id=1, source_target_pairs={{0,24},{2,26},{4,28},{6,30},{8,0},{10,2},{12,4},{14,6},{16,8},{18,... | collective-permute-start | bytes 835592 | tf_op jit(solution)/shard_map/ppermute | solution.py:373
  13.1 19.8 %collective-permute-start.5 = (bf16[3,1024]{1,0:T(4,128)(2,1)S(1)}, bf16[3,1024]{1,0:T(4,128)(2,1)S(1)}, u32[]{:S(2)}, u32[]{:S(2)}) collective-permute-start(bf16[3,1024]{1,0:T(4,128)(2,1)S(1)} %bitcast.135), channel_id=1, source_target_pairs={{6,12},{14,20},{22,28},{7,13},{15,21},{23,29}} | collective-permute-start | bytes 18440 | tf_op jit(solution)/shard_map/ppermute | solution.py:373
  15.2 18.9 %collective-permute-start.6 = (bf16[3,1024]{1,0:T(4,128)(2,1)S(1)}, bf16[3,1024]{1,0:T(4,128)(2,1)S(1)}, u32[]{:S(2)}, u32[]{:S(2)}) collective-permute-start(bf16[3,1024]{1,0:T(4,128)(2,1)S(1)} %bitcast.134), channel_id=1, source_target_pairs={{6,14},{14,22},{22,30},{7,15},{15,23},{23,31}} | collective-permute-start | bytes 18440 | tf_op jit(solution)/shard_map/ppermute | solution.py:373
  51.8 11.4 %collective-permute-start.10 = (bf16[544,256]{1,0:T(8,128)(2,1)}, bf16[544,256]{1,0:T(8,128)(2,1)}, u32[]{:S(2)}, u32[]{:S(2)}) collective-permute-start(bf16[544,256]{1,0:T(8,128)(2,1)} %get-tuple-element.96), channel_id=1, source_target_pairs={{0,6},{2,4},{4,2},{6,0},{8,14},{10,12},{12,10},{14,8},{16,22},{18,... | collective-permute-start | bytes 835592 | tf_op jit(solution)/shard_map/ppermute | solution.py:373
  51.8 15.8 %collective-permute-start.9 = (bf16[544,256]{1,0:T(8,128)(2,1)}, bf16[544,256]{1,0:T(8,128)(2,1)}, u32[]{:S(2)}, u32[]{:S(2)}) collective-permute-start(bf16[544,256]{1,0:T(8,128)(2,1)} %get-tuple-element.96), channel_id=1, source_target_pairs={{0,4},{2,6},{4,0},{6,2},{8,12},{10,14},{12,8},{14,10},{16,20},{18,... | collective-permute-start | bytes 835592 | tf_op jit(solution)/shard_map/ppermute | solution.py:373
  51.8 15.8 %collective-permute-start.8 = (bf16[544,256]{1,0:T(8,128)(2,1)}, bf16[544,256]{1,0:T(8,128)(2,1)}, u32[]{:S(2)}, u32[]{:S(2)}) collective-permute-start(bf16[544,256]{1,0:T(8,128)(2,1)} %get-tuple-element.96), channel_id=1, source_target_pairs={{0,2},{2,0},{4,6},{6,4},{8,10},{10,8},{12,14},{14,12},{16,18},{18,... | collective-permute-start | bytes 835592 | tf_op jit(solution)/shard_map/ppermute | solution.py:373
  55.3 22.4 %collective-permute-start.13 = (bf16[128,1024]{1,0:T(8,128)(2,1)}, bf16[128,1024]{1,0:T(8,128)(2,1)}, u32[]{:S(2)}, u32[]{:S(2)}) collective-permute-start(bf16[128,1024]{1,0:T(8,128)(2,1)} %bitcast.106), channel_id=1, source_target_pairs={{0,16},{2,18},{4,20},{6,22},{8,24},{10,26},{12,28},{14,30},{16,0},... | collective-permute-start | bytes 786440 | tf_op jit(solution)/shard_map/ppermute | solution.py:373
  56.0 20.7 %collective-permute-start.12 = (bf16[128,1024]{1,0:T(8,128)(2,1)}, bf16[128,1024]{1,0:T(8,128)(2,1)}, u32[]{:S(2)}, u32[]{:S(2)}) collective-permute-start(bf16[128,1024]{1,0:T(8,128)(2,1)} %bitcast.107), channel_id=1, source_target_pairs={{0,24},{2,26},{4,28},{6,30},{8,0},{10,2},{12,4},{14,6},{16,8},{18,... | collective-permute-start | bytes 786440 | tf_op jit(solution)/shard_map/ppermute | solution.py:373
  58.1 26.0 %all-to-all-start.1 = ((bf16[4,128,1024]{2,1,0:T(8,128)(2,1)}), bf16[4,128,1024]{2,1,0:T(8,128)(2,1)}, u32[]{:S(2)}, u32[]{:S(2)}) async-start(bf16[4,128,1024]{2,1,0:T(8,128)(2,1)} %pack.3), calls=%async_computation.1 | async-start | bytes 2097152 | tf_op jit(solution)/shard_map/all_to_all | solution.py:396
  69.8 14.2 %collective-permute-start.11 = (f32[544,256]{1,0:T(8,128)}, f32[544,256]{1,0:T(8,128)}, u32[]{:S(2)}, u32[]{:S(2)}) collective-permute-start(f32[544,256]{1,0:T(8,128)} %convert_add_fusion.1.mine), channel_id=1, source_target_pairs={{0,1},{1,0},{2,3},{3,2},{4,5},{5,4},{6,7},{7,6},{8,9},{9,8},{10,11... | collective-permute-start | bytes 1671176 | tf_op jit(solution)/shard_map/ppermute | solution.py:387
  74.0 9.0 %collective-permute-start.14 = (bf16[128,1024]{1,0:T(8,128)(2,1)}, bf16[128,1024]{1,0:T(8,128)(2,1)S(1)}, u32[]{:S(2)}, u32[]{:S(2)}) collective-permute-start(bf16[128,1024]{1,0:T(8,128)(2,1)} %bitcast.108), channel_id=1, source_target_pairs={{0,8},{2,10},{4,12},{6,14},{8,16},{10,18},{12,20},{14,22},{16,24},... | collective-permute-start | bytes 786440 | tf_op jit(solution)/shard_map/ppermute | solution.py:373
  107.7 11.4 %collective-permute-start.17 = (f32[17,1024]{1,0:T(8,128)S(1)}, f32[17,1024]{1,0:T(8,128)S(1)}, u32[]{:S(2)}, u32[]{:S(2)}) collective-permute-start(f32[17,1024]{1,0:T(8,128)S(1)} %get-tuple-element.70), channel_id=1, source_target_pairs={{0,24},{2,26},{4,28},{6,30},{8,0},{10,2},{12,4},{14,6},{16,8},{18,... | collective-permute-start | bytes 208904 | tf_op jit(solution)/shard_map/ppermute | solution.py:373
  109.7 9.4 %collective-permute-start.16 = (f32[17,1024]{1,0:T(8,128)S(1)}, f32[17,1024]{1,0:T(8,128)S(1)}, u32[]{:S(2)}, u32[]{:S(2)}) collective-permute-start(f32[17,1024]{1,0:T(8,128)S(1)} %get-tuple-element.71), channel_id=1, source_target_pairs={{0,16},{2,18},{4,20},{6,22},{8,24},{10,26},{12,28},{14,30},{16,0},... | collective-permute-start | bytes 208904 | tf_op jit(solution)/shard_map/ppermute | solution.py:373
  173.7 28.5 %all-to-all-start.2 = ((bf16[4,128,1024]{2,1,0:T(8,128)(2,1)}), bf16[4,128,1024]{2,1,0:T(8,128)(2,1)S(1)}, u32[]{:S(2)}, u32[]{:S(2)}) async-start(bf16[4,128,1024]{2,1,0:T(8,128)(2,1)} %bitcast.111), calls=%async_computation.2 | async-start | bytes 2097152 | tf_op jit(solution)/shard_map/all_to_all | solution.py:427
  180.1 10.5 %collective-permute-start.21 = (bf16[544,256]{1,0:T(8,128)(2,1)S(1)}, bf16[544,256]{1,0:T(8,128)(2,1)S(1)}, u32[]{:S(2)}, u32[]{:S(2)}) collective-permute-start(bf16[544,256]{1,0:T(8,128)(2,1)S(1)} %get-tuple-element.49), channel_id=1, source_target_pairs={{0,6},{2,4},{4,2},{6,0},{8,14},{10,12},{12,10},{14,8},{16,22},{18,... | collective-permute-start | bytes 835592 | tf_op jit(solution)/shard_map/ppermute | solution.py:373
  181.7 14.1 %collective-permute-start.20 = (bf16[544,256]{1,0:T(8,128)(2,1)S(1)}, bf16[544,256]{1,0:T(8,128)(2,1)S(1)}, u32[]{:S(2)}, u32[]{:S(2)}) collective-permute-start(bf16[544,256]{1,0:T(8,128)(2,1)S(1)} %get-tuple-element.49), channel_id=1, source_target_pairs={{0,4},{2,6},{4,0},{6,2},{8,12},{10,14},{12,8},{14,10},{16,20},{18,... | collective-permute-start | bytes 835592 | tf_op jit(solution)/shard_map/ppermute | solution.py:373
  183.3 12.6 %collective-permute-start.19 = (bf16[544,256]{1,0:T(8,128)(2,1)S(1)}, bf16[544,256]{1,0:T(8,128)(2,1)S(1)}, u32[]{:S(2)}, u32[]{:S(2)}) collective-permute-start(bf16[544,256]{1,0:T(8,128)(2,1)S(1)} %get-tuple-element.49), channel_id=1, source_target_pairs={{0,2},{2,0},{4,6},{6,4},{8,10},{10,8},{12,14},{14,12},{16,18},{18,... | collective-permute-start | bytes 835592 | tf_op jit(solution)/shard_map/ppermute | solution.py:373
  196.7 11.1 %collective-permute-start.22 = (bf16[544,256]{1,0:T(8,128)(2,1)}, bf16[544,256]{1,0:T(8,128)(2,1)}, u32[]{:S(2)}, u32[]{:S(2)}) collective-permute-start(bf16[544,256]{1,0:T(8,128)(2,1)} %convert_add_fusion.mine), channel_id=1, source_target_pairs={{0,1},{1,0},{2,3},{3,2},{4,5},{5,4},{6,7},{7,6},{8,9},{9,8},{10,11... | collective-permute-start | bytes 835592 | tf_op jit(solution)/shard_map/ppermute | solution.py:387
  202.2 24.0 %all-to-all-start.3 = ((bf16[4,128,1024]{2,1,0:T(8,128)(2,1)}), bf16[4,128,1024]{2,1,0:T(8,128)(2,1)}, u32[]{:S(2)}, u32[]{:S(2)}) async-start(bf16[4,128,1024]{2,1,0:T(8,128)(2,1)} %bitcast.110), calls=%async_computation.3 | async-start | bytes 2097152 | tf_op jit(solution)/shard_map/all_to_all | solution.py:396
  209.8 16.3 %collective-permute-start.23 = (f32[3,1024]{1,0:T(4,128)S(1)}, f32[3,1024]{1,0:T(4,128)S(1)}, u32[]{:S(2)}, u32[]{:S(2)}) collective-permute-start(f32[3,1024]{1,0:T(4,128)S(1)} %fusion.28), channel_id=1, source_target_pairs={{8,0},{10,2},{12,4},{14,6},{16,8},{18,10},{20,12},{22,14},{24,16},... | collective-permute-start | bytes 36872 | tf_op jit(solution)/shard_map/ppermute | solution.py:368
  227.6 18.2 %all-to-all-start.4 = ((bf16[4,160,1024]{2,1,0:T(8,128)(2,1)}), bf16[4,160,1024]{2,1,0:T(8,128)(2,1)S(1)}, u32[]{:S(2)}, u32[]{:S(2)}) async-start(bf16[4,160,1024]{2,1,0:T(8,128)(2,1)} %bitcast_dynamic-update-slice_fusion), calls=%async_computation.4 | async-start | bytes 2621440 | tf_op jit(solution)/shard_map/all_to_all | solution.py:396
  (37 other events, 330.8 us)

commit v3 on v2

--- a/solution.py
+++ b/solution.py
@@ -12,7 +12,7 @@
 PLANE = 4
 LANES = 128
 GROUP = 8
-UNROLL = 4
+UNROLL = 8
 BLOCK = 32
 COLUMNS = 256
 LAST = 16
@@ -77,8 +77,8 @@
 
 
 def local_kernel(
-    core, mine, other, dtw, dtb, act, g, alog, step_out, sig_out, state_out, adjoint_out,
-    a2, us, gs, spread, low, bc,
+    core, mine, other, dtw, dtb, act, g, alog, step_out, sig_out, state_out, adjoint_out, bc,
+    a2, us, gs, spread, low,
 ):
     tokens, width = act.shape
     rank = dtw.shape[0]
@@ -139,14 +139,13 @@
 
 
 def full_kernel(
-    core, mine, other, dtw, step, sig, act, g, alog, carries, skip,
+    core, bc, dtw, step, sig, act, g, alog, carries, skip,
     mixed_out, pre_out, act_out, rate_out, vec_out, mine_out, other_out,
-    a2, acts, gs, hist, mixed, s1, s2, gb, gc, spread, both_rows, bc,
+    a2, acts, gs, hist, mixed, s1, s2, gb, gc, spread, both_rows,
 ):
     tokens, rows, _ = step.shape
     width = rows * LANES
     rank = dtw.shape[0]
-    join_halves(core, mine, other, bc)
     spread_rows(bc, spread)
     block = min(tokens, BLOCK)
     dense, flat = (block, rows, LANES), (block, width)
@@ -277,11 +276,11 @@
         in_specs=[pl.BlockSpec(memory_space=pltpu.SMEM)] + vmem_specs(len(operands) - 1),
         out_shape=[
             jax.ShapeDtypeStruct(dense, F32), jax.ShapeDtypeStruct((tokens, channels), F32), ends, ends,
+            jax.ShapeDtypeStruct((2 * STATE, tokens), F32),
         ],
         scratch_shapes=[
             pltpu.VMEM((STATE,) + dense[1:], F32), pltpu.VMEM(dense, F32), pltpu.VMEM(dense, F32),
             pltpu.VMEM((2 * STATE, tokens, LANES), F32), pltpu.VMEM((dtw.shape[0], tokens), BF16),
-            pltpu.VMEM((2 * STATE, tokens), F32),
         ],
         compiler_params=pltpu.CompilerParams(vmem_limit_bytes=VMEM_MIDDLE),
         cost_estimate=took(22),
@@ -289,13 +288,11 @@
     )(*operands)
 
 
-def scan_full(core, mine, other, dtw, step, sig, act, g, alog, carries, skip):
+def scan_full(core, bc, dtw, step, sig, act, g, alog, carries, skip):
     tokens, channels = act.shape
     dense = (tokens, channels // LANES, LANES)
     flat = (tokens, channels)
-    operands = (
-        core, mine[dtw.shape[0] :], other[dtw.shape[0] :], dtw, step, sig, act, g, alog, carries, skip
-    )
+    operands = (core, bc, dtw, step, sig, act, g, alog, carries, skip)
     small = pltpu.VMEM((tokens, STATE, LANES), F32)
     half = jax.ShapeDtypeStruct((dtw.shape[0] + 2 * STATE, tokens // 2), F32)
     return pl.pallas_call(
@@ -322,7 +319,6 @@
             small,
             pltpu.VMEM((2 * STATE, tokens, LANES), F32),
             pltpu.VMEM((tokens, LANES), F32),
-            pltpu.VMEM((2 * STATE, tokens), F32),
         ],
         compiler_params=pltpu.CompilerParams(vmem_limit_bytes=VMEM_LIMIT),
         cost_estimate=took(51),
@@ -408,17 +404,22 @@
                 out[q, rows, z * share : (z + 1) * share] = x[:, source : source + share]
 
 
-def unpack_kernel(share, x, *outs):
+def unpack_kernel(share, count, x, *refs):
+    late, outs = refs[:-count], refs[-count:]
     row = 0
-    for out in outs:
+    for at, out in enumerate(outs):
         rows = slice(row, row + out.shape[0])
         row += out.shape[0]
         for q in range(PLANE):
             for z in range(x.shape[2] // share):
+                source = slice(z * share, (z + 1) * share)
                 target = (z * PLANE + q) * share
-                out[:, target : target + share] = x[q, rows, z * share : (z + 1) * share].astype(
-                    out.dtype
-                )
+                target = slice(target, target + share)
+                out[:, target] = x[q, rows, source].astype(out.dtype)
+                if late and at == 0:
+                    last = slice(out.shape[0] - LAST, out.shape[0])
+                    total = x[q, last, source].astype(F32) + late[q][:, source]
+                    out[last, target] = total.astype(out.dtype)
 
 
 def along_line(x):
@@ -441,19 +442,19 @@
     )(*arrays)
 
 
-def to_tokens(x, *results):
+def to_tokens(x, *results, late=()):
     channels = x.shape[2]
     share = channels * PLANE // lax.axis_size("ctx")
     return pl.pallas_call(
-        functools.partial(unpack_kernel, share),
-        in_specs=vmem_specs(1),
+        functools.partial(unpack_kernel, share, len(results)),
+        in_specs=vmem_specs(1 + len(late)),
         out_specs=vmem_specs(len(results)),
         out_shape=[
             jax.ShapeDtypeStruct((rows, PLANE * channels), dtype) for rows, dtype in results
         ],
         cost_estimate=took(2),
         name="unpack",
-    )(x)
+    )(x, *late)
 
 
 def rim_before(x):
@@ -465,6 +466,13 @@
         route = [(i - 1, i + q) for i in range(PLANE, count, PLANE)]
         parts.append(send(x[:, :, q].reshape(rows, channels // PLANE), route))
     return functools.reduce(jnp.add, parts)
+
+
+def late_rows(early):
+    count = lax.axis_size("ctx")
+    return [
+        send(early, [(i + q, i - 1) for i in range(PLANE, count, PLANE)]) for q in range(PLANE)
+    ]
 
 
 def own_channels(x):
@@ -562,7 +570,7 @@
 
 def tail_kernel(
     core, mine, other, rows_proj, grad_act, moved, before, weight, bias, dt_parts,
-    packed_out, sums_out, last_out, grad, padded, grad_proj,
+    packed_out, sums_out, early_out, grad, padded, grad_proj,
 ):
     tokens, width = grad_act.shape
     rows = tokens // PLANE
@@ -610,7 +618,12 @@
                 total = total + weight[k : k + 1, columns] * grad[first : first + piece, columns]
             to = start % rows
             packed_out[start // rows, to : to + piece, columns] = total.astype(BF16)
-        last_out[:, columns] = total[piece - LAST :]
+        early_out[: LAST - rim, columns] = jnp.zeros((LAST - rim, COLUMNS), F32)
+        for j in range(rim):
+            early = jnp.zeros((1, COLUMNS), F32)
+            for k in range(j + 1):
+                early = early + weight[k : k + 1, columns] * grad[j - k : j - k + 1, columns]
+            early_out[LAST - rim + j : LAST - rim + j + 1, columns] = early
 
 
 def conv_tail(core, mine, other, rows_proj, grad_act, moved, before, weight, bias, dt_parts):
@@ -720,7 +733,7 @@
     rows, dt_rows = seq_in.shape[0], dt_weight.shape[0]
     half = PLANE * rows // 2
     packed = by_owner(seq_in, dt_weight)
-    proj_blocks = line_blocks(after(proj_weight.T, packed))
+    proj_blocks = line_blocks(proj_weight.T)
     moved = in_plane(packed)
     before = rim_before(seq_in[rows - rim :])
     weight, bias, step_bias, rates, gain = (
@@ -739,43 +752,30 @@
     part = lambda at: matmul(rows_proj, lax.dynamic_slice_in_dim(act, at * half, half), (1, 1))
     mine, other = sum_plane(part(core), part(1 - core))
     rows_dt = place_blocks(dt_blocks, 0)
-    step, sig, state, adjoint = scan_local(
+    step, sig, state, adjoint, bc = scan_local(
         here, mine, other, rows_dt, step_bias, act, grad_mixed, rates
     )
     low = by_halves(mine[:RANK].astype(BF16), other[:RANK].astype(BF16))
     carries = line_carries(state, adjoint, rates)
     mixed, grad_pre, grad_act, grad_rate, grad_vecs, grad_mine, grad_other = scan_full(
-        here, mine, other, rows_dt, step, sig, act, grad_mixed, rates, carries, gain
+        here, bc, rows_dt, step, sig, act, grad_mixed, rates, carries, gain
     )
 
     dtw_sums = matmul(low, grad_pre, (1, 0)).astype(BF16)
     dtw_moved = along_line(dtw_sums.reshape(planes, RANK // planes, -1))
     mine, other = sum_plane(grad_mine, grad_other, dtw_sums)
     mine, other = mine.astype(BF16), other.astype(BF16)
-    first = 16
-    start = jnp.where(core == 0, mine[:, :first], other[:, :first])
-    first_pre = conv_forward(
-        jnp.concatenate([before, moved[0, :first]], axis=0), weight, bias, first
-    )
-    grad_first = grad_act[:first] + matmul(start, rows_proj, (0, 0))
-    following = shifted((grad_first * silu_parts(first_pre)[1])[:rim], "ctx", -PLANE)
-    packed, grad_conv, last = conv_tail(
+    packed, grad_conv, early = conv_tail(
         here, mine, other, rows_proj, grad_act, moved, before, weight, bias, dtw_moved
     )
-    following = after(following, last)
-    late = [
-        sum(weight[k] * following[j - k] for k in range(j + 1)) for j in range(rim)
-    ]
-    late = last + jnp.pad(jnp.stack(late), ((LAST - rim, 0), (0, 0)))
     grad_gate = in_plane(after(mixed, mine).reshape(PLANE, rows, -1))
-    packed = lax.dynamic_update_slice(
-        after(packed, grad_gate), late.astype(BF16)[None], (PLANE - 1, rows - LAST, 0)
-    )
-    returned = in_plane(packed)
-    sums = sum_line(after(jnp.concatenate([grad_conv, grad_vecs, grad_rate], axis=0), packed))
+    returned = in_plane(after(packed, grad_gate))
     (grad_gate,) = to_tokens(after(grad_gate, packed), (rows, F32))
     grad_gate = (gate_factor * grad_gate).astype(BF16)
-    grad_seq, grad_dtw = to_tokens(returned, (rows, BF16), (dt_rows, F32))
+    late = late_rows(after(early, grad_gate))
+    sums = jnp.concatenate([grad_conv, grad_vecs, grad_rate], axis=0)
+    sums = sum_line(after(sums, grad_gate))
+    grad_seq, grad_dtw = to_tokens(returned, (rows, BF16), (dt_rows, F32), late=late)
     return outputs(grad_seq, grad_gate, grad_dtw, sums)
 
 
@@ -794,12 +794,12 @@
     low = projected[:RANK].astype(BF16)
     halves = (jnp.zeros((1,), jnp.int32), projected[:, : length // 2], projected[:, length // 2 :])
     grad_mixed, gate_factor = gate_parts(gate_in, upstream, forget_flags)
-    step, sig, state, adjoint = scan_local(
+    step, sig, state, adjoint, bc = scan_local(
         *halves, rows_dt, dt_bias[None], act, grad_mixed, a_log
     )
     carries = exchange_carries(jnp.concatenate([state[:STATE], adjoint], axis=0), a_log)
     mixed, grad_pre, grad_act, grad_rate, grad_vecs, first, second = scan_full(
-        *halves, rows_dt, step, sig, act, grad_mixed, a_log, carries, skip_gain[None]
+        halves[0], bc, rows_dt, step, sig, act, grad_mixed, a_log, carries, skip_gain[None]
     )
     grad_gate = (gate_factor * mixed.astype(F32)).astype(BF16)
     grad_proj = lax.psum(jnp.concatenate([first, second], axis=1), "mp").astype(BF16)

time: 253 us -> 248 us (0.980)
  local copies, waits for them, and re-layouts: 36 us -> 30.4 us
  starting transfers between devices: 60 us -> 65.6 us
  waiting for transfers between devices: 40.3 us -> 45.4 us
  Pallas kernels: 89.7 us -> 85.9 us
  other arithmetic: 14.2 us -> 10.5 us
    ppermute x22 -> x26, starting transfers between devices: 30.5 us -> 41 us  [send(): return lax.ppermute(x, 'ctx', route)]
    ppermute x1 -> x0, starting transfers between devices: 5.19 us -> none  [shifted(): return lax.ppermute(block, axis, route)]
    slice x3 -> x0, local copies, waits for them, and re-layouts: 4.19 us -> none  [the longest x1 1.47 us: plane_body(): grad_first = grad_act[:first] + matmul(start, rows_proj, (0, 0))]
    ppermute x4, waiting for transfers between devices: 2.3 us -> 6.36 us  [swap_mp(): return lax.ppermute(x, 'mp', [(0, 1), (1, 0)])]
    pallas_call x1, Pallas kernels: 50.9 us -> 48 us  [scan_full(): pl.pallas_call(full_kernel, in_specs=[pl.BlockSpec(memory_space=pltpu.SME...]
    ppermute x22 -> x26, waiting for transfers between devices: 33.4 us -> 36.2 us  [send(): return lax.ppermute(x, 'ctx', route)]
    dot_general x4 -> x3, matrix products: 7.91 us -> 6.66 us  [matmul(): lax.dot_general(x, y, ((dims[:1], dims[1:]), ((), ())), preferred_element...]
    unnamed x78 -> x79, local copies, waits for them, and re-layouts: 10.7 us -> 11.7 us
  transfers between devices with their start and end apart: 32 -> 35, of which waited for: 8 -> 15; matrix products, arithmetic and copies ran while one was open for 15% -> 10% of each run, Pallas kernels for 6% -> 7%
where the time goes in v3:
time: 248 us; the launch traced here: 246 us
  Pallas kernels  85.9 us (35%)
  starting transfers between devices  65.6 us (26%)
  waiting for transfers between devices  45.4 us (18%)
  local copies, waits for them, and re-layouts  30.4 us (12%)
  other arithmetic  10.5 us (4%)
  matrix products  6.66 us (3%)
    pallas_call x1, Pallas kernels, scan_full(): pl.pallas_call(full_kernel, in_specs=[pl.BlockSpec(memory_space=pltpu.SME...  48 us
    ppermute x26, starting transfers between devices, send(): return lax.ppermute(x, 'ctx', route)  41 us
    ppermute x26, waiting for transfers between devices, send(): return lax.ppermute(x, 'ctx', route)  36.2 us
    all_to_all x4, starting transfers between devices, in_plane(): lax.all_to_all(x, 'ctx', 0, 0, axis_index_groups=plane_groups(), tiled=True)  19.4 us
    pallas_call x1, Pallas kernels, scan_local(): pl.pallas_call(local_kernel, in_specs=[pl.BlockSpec(memory_space=pltpu.SM...  18.1 us
    unnamed x79, local copies, waits for them, and re-layouts  11.7 us
    pallas_call x1, Pallas kernels, conv_tail(): pl.pallas_call(tail_kernel, in_specs=[pl.BlockSpec(memory_space=pltpu.SME...  7.58 us
    dynamic_update_slice x8, local copies, waits for them, and re-layouts, place_blocks(): lax.dynamic_update_slice(out, block, (at, 0) if axis == 0 else (0, at))  7.09 us
  transfers between devices with their start and end apart: 35, of which 15 were waited for; matrix products, arithmetic and copies ran while one was open for 10% of the time, Pallas kernels for 7%

profile of v3, /device:TPU:14, one launch (start us, length us, event | category | flops | bytes accessed | tf_op | source)
XLA Modules:
  0.0 246.0 jit_solution(4546126439965239210)
XLA Ops:
  8.4 2.7 %collective-permute-start.6 = (bf16[3,1024]{1,0:T(4,128)(2,1)S(1)}, bf16[3,1024]{1,0:T(4,128)(2,1)S(1)}, u32[]{:S(2)}, u32[]{:S(2)}) collective-permute-start(bf16[3,1024]{1,0:T(4,128)(2,1)S(1)} %bitcast.86), channel_id=1, source_target_pairs={{6,14},{14,22},{22,30},{7,15},{15,23},{23,31}} | collective-permute-start | bytes 18440 | tf_op jit(solution)/shard_map/ppermute | solution.py:369
  11.2 2.5 %pack.2 = bf16[4,160,1024]{2,1,0:T(8,128)(2,1)} custom-call(bf16[128,4096]{1,0:T(8,128)(2,1)} %refs_0_.1, bf16[32,4096]{1,0:T(8,128)(2,1)} %refs_1_.1), custom_call_target="tpu_custom_call" | custom-call | bytes 7200000 | tf_op jit(solution)/shard_map/pack/pallas_call | solution.py:435
  13.7 4.2 %all-to-all-start = ((bf16[4,160,1024]{2,1,0:T(8,128)(2,1)}), bf16[4,160,1024]{2,1,0:T(8,128)(2,1)S(1)}, u32[]{:S(2)}, u32[]{:S(2)}) async-start(bf16[4,160,1024]{2,1,0:T(8,128)(2,1)} %pack.2), calls=%async_computation | async-start | bytes 2621440 | tf_op jit(solution)/shard_map/all_to_all | solution.py:392
  19.7 6.9 %collective-permute-done.5 = bf16[3,1024]{1,0:T(4,128)(2,1)S(1)} collective-permute-done((bf16[3,1024]{1,0:T(4,128)(2,1)S(1)}, bf16[3,1024]{1,0:T(4,128)(2,1)S(1)}, u32[]{:S(2)}, u32[]{:S(2)}) %collective-permute-start.5) | collective-permute-done | bytes 6176 | tf_op jit(solution)/shard_map/ppermute | solution.py:369
  42.5 2.4 fusion.27
  51.2 5.2 %all-to-all-start.1 = ((bf16[4,128,1024]{2,1,0:T(8,128)(2,1)}), bf16[4,128,1024]{2,1,0:T(8,128)(2,1)}, u32[]{:S(2)}, u32[]{:S(2)}) async-start(bf16[4,128,1024]{2,1,0:T(8,128)(2,1)} %pack.3), calls=%async_computation.1 | async-start | bytes 2097152 | tf_op jit(solution)/shard_map/all_to_all | solution.py:392
  56.4 4.5 %collective-permute-done.9 = bf16[544,256]{1,0:T(8,128)(2,1)} collective-permute-done((bf16[544,256]{1,0:T(8,128)(2,1)}, bf16[544,256]{1,0:T(8,128)(2,1)}, u32[]{:S(2)}, u32[]{:S(2)}) %collective-permute-start.9) | collective-permute-done | bytes 278560 | tf_op jit(solution)/shard_map/ppermute | solution.py:369
  72.4 4.6 %collective-permute-done.14 = bf16[128,1024]{1,0:T(8,128)(2,1)S(1)} collective-permute-done((bf16[128,1024]{1,0:T(8,128)(2,1)}, bf16[128,1024]{1,0:T(8,128)(2,1)S(1)}, u32[]{:S(2)}, u32[]{:S(2)}) %collective-permute-start.14) | collective-permute-done | bytes 262176 | tf_op jit(solution)/shard_map/ppermute | solution.py:369
  79.9 18.1 %scan_local.1 = (f32[512,8,128]{2,1,0:T(8,128)S(1)}, f32[512,1024]{1,0:T(8,128)S(1)}, f32[17,1024]{1,0:T(8,128)S(1)}, f32[17,1024]{1,0:T(8,128)S(1)}, f32[32,512]{1,0:T(8,128)S(1)}) custom-call(s32[1]{0:T(128)} %bitcast.core, f32[544,256]{1,0:T(8,128)} %convert_add_fusion.1.mine, f32[544,256]{1,0:T(8,128)} %collective-permute-done.11.other, ...), custom_call_target="tpu_custom_call" | custom-call | bytes 79200000 | tf_op jit(solution)/shard_map/scan_local/pallas_call | solution.py:274
  100.7 3.2 %collective-permute-start.17 = (f32[17,1024]{1,0:T(8,128)S(1)}, f32[17,1024]{1,0:T(8,128)S(1)}, u32[]{:S(2)}, u32[]{:S(2)}) collective-permute-start(f32[17,1024]{1,0:T(8,128)S(1)} %get-tuple-element.68), channel_id=1, source_target_pairs={{0,24},{2,26},{4,28},{6,30},{8,0},{10,2},{12,4},{14,6},{16,8},{18,... | collective-permute-start | bytes 208904 | tf_op jit(solution)/shard_map/ppermute | solution.py:369
  112.6 48.0 %scan_full.1 = (bf16[512,1024]{1,0:T(8,128)(2,1)}, bf16[512,1024]{1,0:T(8,128)(2,1)}, f32[512,1024]{1,0:T(8,128)}, f32[16,1024]{1,0:T(8,128)}, f32[2,1024]{1,0:T...) custom-call(s32[1]{0:T(128)} %bitcast.core, f32[32,512]{1,0:T(8,128)} %copy-done.11, bf16[512,1024]{1,0:T(8,128)(2,1)} %copy-done.1, ...), custom_call_target="tpu_custom_call" | custom-call | bytes 183600000 | tf_op jit(solution)/shard_map/scan_full/pallas_call | solution.py:298
  160.6 2.9 %convolution_convert_fusion = bf16[512,1024]{1,0:T(8,128)(2,1)} fusion(bf16[512,1024]{1,0:T(8,128)(2,1)} %get-tuple-element.48, bf16[512,256]{1,0:T(8,128)(2,1)S(1)} %slice.110, bf16[512,256]{1,0:T(8,128)(2,1)S(1)} %slice.111, pred[]{:T(512)S(6)} %eq.9), kind=kOutput, calls=%fused_computation.14 | convolution fusion | flops 539754496 | bytes 2621441 | tf_op jit(solution)/shard_map/dot_general | solution.py:709
  163.5 5.2 %all-to-all-start.2 = ((bf16[4,128,1024]{2,1,0:T(8,128)(2,1)}), bf16[4,128,1024]{2,1,0:T(8,128)(2,1)S(1)}, u32[]{:S(2)}, u32[]{:S(2)}) async-start(bf16[4,128,1024]{2,1,0:T(8,128)(2,1)} %bitcast.70), calls=%async_computation.2 | async-start | bytes 2097152 | tf_op jit(solution)/shard_map/all_to_all | solution.py:428
  175.6 7.0 %collective-permute-done.21 = bf16[544,256]{1,0:T(8,128)(2,1)S(1)} collective-permute-done((bf16[544,256]{1,0:T(8,128)(2,1)S(1)}, bf16[544,256]{1,0:T(8,128)(2,1)S(1)}, u32[]{:S(2)}, u32[]{:S(2)}) %collective-permute-start.21) | collective-permute-done | bytes 278560 | tf_op jit(solution)/shard_map/ppermute | solution.py:369
  182.6 5.1 %collective-permute-done.20 = bf16[544,256]{1,0:T(8,128)(2,1)S(1)} collective-permute-done((bf16[544,256]{1,0:T(8,128)(2,1)S(1)}, bf16[544,256]{1,0:T(8,128)(2,1)S(1)}, u32[]{:S(2)}, u32[]{:S(2)}) %collective-permute-start.20) | collective-permute-done | bytes 278560 | tf_op jit(solution)/shard_map/ppermute | solution.py:369
  188.5 2.8 %all-to-all-done.2.dt_parts = bf16[4,128,1024]{2,1,0:T(8,128)(2,1)S(1)} async-done(((bf16[4,128,1024]{2,1,0:T(8,128)(2,1)}), bf16[4,128,1024]{2,1,0:T(8,128)(2,1)S(1)}, u32[]{:S(2)}, u32[]{:S(2)}) %all-to-all-start.2) | async-done | bytes 1048608 | tf_op jit(solution)/shard_map/all_to_all | solution.py:428
  191.3 5.8 %all-to-all-start.3 = ((bf16[4,128,1024]{2,1,0:T(8,128)(2,1)}), bf16[4,128,1024]{2,1,0:T(8,128)(2,1)}, u32[]{:S(2)}, u32[]{:S(2)}) async-start(bf16[4,128,1024]{2,1,0:T(8,128)(2,1)} %bitcast.69), calls=%async_computation.3 | async-start | bytes 2097152 | tf_op jit(solution)/shard_map/all_to_all | solution.py:392
  201.6 7.6 %conv_tail.1 = (bf16[4,160,1024]{2,1,0:T(8,128)(2,1)S(1)}, f32[5,1024]{1,0:T(8,128)S(1)}, f32[16,1024]{1,0:T(8,128)S(1)}) custom-call(s32[1]{0:T(128)} %bitcast.core, bf16[544,256]{1,0:T(8,128)(2,1)S(1)} %copy-done.7, bf16[544,256]{1,0:T(8,128)(2,1)} %collective-permute-done.22.other, bf16[544,1024]{1,0:T(8,128)(2,1)S(1)} %constant_dynamic-update-slice_fusion.4.rows_proj, ...), custom_call_target="tpu_custom_call" | custom-call | bytes 28800000 | tf_op jit(solution)/shard_map/conv_tail/pallas_call | solution.py:632
  210.9 4.2 %all-to-all-start.4 = ((bf16[4,160,1024]{2,1,0:T(8,128)(2,1)}), bf16[4,160,1024]{2,1,0:T(8,128)(2,1)S(1)}, u32[]{:S(2)}, u32[]{:S(2)}) async-start(bf16[4,160,1024]{2,1,0:T(8,128)(2,1)} %copy-done.6), calls=%async_computation.4 | async-start | bytes 2621440 | tf_op jit(solution)/shard_map/all_to_all | solution.py:392
  215.2 2.8 %unpack.2 = f32[128,4096]{1,0:T(8,128)} custom-call(bf16[4,128,1024]{2,1,0:T(8,128)(2,1)} %all-to-all-done.3.x), custom_call_target="tpu_custom_call" | custom-call | bytes 7200000 | tf_op jit(solution)/shard_map/unpack/pallas_call | solution.py:448
  217.9 3.8 %fusion.9 = bf16[128,4096]{1,0:T(8,128)(2,1)} fusion(f32[128,4096]{1,0:T(8,128)} %unpack.2, bf16[128,4096]{1,0:T(8,128)(2,1)S(1)} %copy-done.19, bf16[128,4096]{1,0:T(8,128)(2,1)} %param.13, f32[128]{0:T(128)S(1)} %copy-done.32), kind=kLoop, calls=%fused_computation.12 | loop fusion | flops 6815744 | bytes 5243392 | tf_op jit(solution)/shard_map/convert_element_type | solution.py:774
  223.5 4.2 %collective-permute-start.28 = (f32[23,256]{1,0:T(8,128)S(1)}, f32[23,256]{1,0:T(8,128)S(1)}, u32[]{:S(2)}, u32[]{:S(2)}) collective-permute-start(f32[23,256]{1,0:T(8,128)S(1)} %bitcast.78), channel_id=1, source_target_pairs={{0,16},{2,18},{4,20},{6,22},{8,24},{10,26},{12,28},{14,30},{16,0},... | collective-permute-start | bytes 70664 | tf_op jit(solution)/shard_map/ppermute | solution.py:369
  227.6 3.4 %collective-permute-start.26 = (f32[16,1024]{1,0:T(8,128)S(1)}, f32[16,1024]{1,0:T(8,128)S(1)}, u32[]{:S(2)}, u32[]{:S(2)}) collective-permute-start(f32[16,1024]{1,0:T(8,128)S(1)} %copy-done.16), channel_id=1, source_target_pairs={{14,6},{22,14},{30,22},{15,7},{23,15},{31,23}} | collective-permute-start | bytes 196616 | tf_op jit(solution)/shard_map/ppermute | solution.py:369
  243.3 2.7 %unpack.3 = (bf16[128,4096]{1,0:T(8,128)(2,1)}, f32[32,4096]{1,0:T(8,128)}) custom-call(bf16[4,160,1024]{2,1,0:T(8,128)(2,1)} %copy-done.17, f32[16,1024]{1,0:T(8,128)} %copy-done.25, f32[16,1024]{1,0:T(8,128)} %copy-done.24, f32[16,1024]{1,0:T(8,128)} %copy-done.23, f32[16,1024]{1,0:T(8,128)} %copy-done.22), custom_call_target="tpu_custom_call" | custom-call | bytes 7200000 | tf_op jit(solution)/shard_map/unpack/pallas_call | solution.py:448
  (182 shorter events, 84.9 us)
Async XLA Ops:
  0.6 33.9 %collective-permute-start.2 = (bf16[544,256]{1,0:T(8,128)(2,1)}, bf16[544,256]{1,0:T(8,128)(2,1)}, u32[]{:S(2)}, u32[]{:S(2)}) collective-permute-start(bf16[544,256]{1,0:T(8,128)(2,1)} %bitcast.71), channel_id=1, source_target_pairs={{0,8},{2,10},{4,12},{6,14},{8,16},{10,18},{12,20},{14,22},{16,24},... | collective-permute-start | bytes 835592 | tf_op jit(solution)/shard_map/ppermute | solution.py:369
  2.3 32.3 %collective-permute-start.1 = (bf16[544,256]{1,0:T(8,128)(2,1)}, bf16[544,256]{1,0:T(8,128)(2,1)}, u32[]{:S(2)}, u32[]{:S(2)}) collective-permute-start(bf16[544,256]{1,0:T(8,128)(2,1)} %bitcast.72), channel_id=1, source_target_pairs={{0,16},{2,18},{4,20},{6,22},{8,24},{10,26},{12,28},{14,30},{16,0},... | collective-permute-start | bytes 835592 | tf_op jit(solution)/shard_map/ppermute | solution.py:369
  3.5 31.1 %collective-permute-start = (bf16[544,256]{1,0:T(8,128)(2,1)}, bf16[544,256]{1,0:T(8,128)(2,1)}, u32[]{:S(2)}, u32[]{:S(2)}) collective-permute-start(bf16[544,256]{1,0:T(8,128)(2,1)} %bitcast.73), channel_id=1, source_target_pairs={{0,24},{2,26},{4,28},{6,30},{8,0},{10,2},{12,4},{14,6},{16,8},{18,... | collective-permute-start | bytes 835592 | tf_op jit(solution)/shard_map/ppermute | solution.py:369
  6.3 20.3 %collective-permute-start.5 = (bf16[3,1024]{1,0:T(4,128)(2,1)S(1)}, bf16[3,1024]{1,0:T(4,128)(2,1)S(1)}, u32[]{:S(2)}, u32[]{:S(2)}) collective-permute-start(bf16[3,1024]{1,0:T(4,128)(2,1)S(1)} %bitcast.87), channel_id=1, source_target_pairs={{6,12},{14,20},{22,28},{7,13},{15,21},{23,29}} | collective-permute-start | bytes 18440 | tf_op jit(solution)/shard_map/ppermute | solution.py:369
  8.4 19.4 %collective-permute-start.6 = (bf16[3,1024]{1,0:T(4,128)(2,1)S(1)}, bf16[3,1024]{1,0:T(4,128)(2,1)S(1)}, u32[]{:S(2)}, u32[]{:S(2)}) collective-permute-start(bf16[3,1024]{1,0:T(4,128)(2,1)S(1)} %bitcast.86), channel_id=1, source_target_pairs={{6,14},{14,22},{22,30},{7,15},{15,23},{23,31}} | collective-permute-start | bytes 18440 | tf_op jit(solution)/shard_map/ppermute | solution.py:369
  13.7 18.1 %all-to-all-start = ((bf16[4,160,1024]{2,1,0:T(8,128)(2,1)}), bf16[4,160,1024]{2,1,0:T(8,128)(2,1)S(1)}, u32[]{:S(2)}, u32[]{:S(2)}) async-start(bf16[4,160,1024]{2,1,0:T(8,128)(2,1)} %pack.2), calls=%async_computation | async-start | bytes 2621440 | tf_op jit(solution)/shard_map/all_to_all | solution.py:392
  45.0 11.5 %collective-permute-start.10 = (bf16[544,256]{1,0:T(8,128)(2,1)}, bf16[544,256]{1,0:T(8,128)(2,1)}, u32[]{:S(2)}, u32[]{:S(2)}) collective-permute-start(bf16[544,256]{1,0:T(8,128)(2,1)} %get-tuple-element.82), channel_id=1, source_target_pairs={{0,6},{2,4},{4,2},{6,0},{8,14},{10,12},{12,10},{14,8},{16,22},{18,... | collective-permute-start | bytes 835592 | tf_op jit(solution)/shard_map/ppermute | solution.py:369
  46.2 14.7 %collective-permute-start.9 = (bf16[544,256]{1,0:T(8,128)(2,1)}, bf16[544,256]{1,0:T(8,128)(2,1)}, u32[]{:S(2)}, u32[]{:S(2)}) collective-permute-start(bf16[544,256]{1,0:T(8,128)(2,1)} %get-tuple-element.82), channel_id=1, source_target_pairs={{0,4},{2,6},{4,0},{6,2},{8,12},{10,14},{12,8},{14,10},{16,20},{18,... | collective-permute-start | bytes 835592 | tf_op jit(solution)/shard_map/ppermute | solution.py:369
  47.9 13.6 %collective-permute-start.8 = (bf16[544,256]{1,0:T(8,128)(2,1)}, bf16[544,256]{1,0:T(8,128)(2,1)}, u32[]{:S(2)}, u32[]{:S(2)}) collective-permute-start(bf16[544,256]{1,0:T(8,128)(2,1)} %get-tuple-element.82), channel_id=1, source_target_pairs={{0,2},{2,0},{4,6},{6,4},{8,10},{10,8},{12,14},{14,12},{16,18},{18,... | collective-permute-start | bytes 835592 | tf_op jit(solution)/shard_map/ppermute | solution.py:369
  48.5 22.9 %collective-permute-start.13 = (bf16[128,1024]{1,0:T(8,128)(2,1)}, bf16[128,1024]{1,0:T(8,128)(2,1)}, u32[]{:S(2)}, u32[]{:S(2)}) collective-permute-start(bf16[128,1024]{1,0:T(8,128)(2,1)} %bitcast.65), channel_id=1, source_target_pairs={{0,16},{2,18},{4,20},{6,22},{8,24},{10,26},{12,28},{14,30},{16,0},... | collective-permute-start | bytes 786440 | tf_op jit(solution)/shard_map/ppermute | solution.py:369
  49.7 20.7 %collective-permute-start.12 = (bf16[128,1024]{1,0:T(8,128)(2,1)}, bf16[128,1024]{1,0:T(8,128)(2,1)}, u32[]{:S(2)}, u32[]{:S(2)}) collective-permute-start(bf16[128,1024]{1,0:T(8,128)(2,1)} %bitcast.66), channel_id=1, source_target_pairs={{0,24},{2,26},{4,28},{6,30},{8,0},{10,2},{12,4},{14,6},{16,8},{18,... | collective-permute-start | bytes 786440 | tf_op jit(solution)/shard_map/ppermute | solution.py:369
  51.2 26.7 %all-to-all-start.1 = ((bf16[4,128,1024]{2,1,0:T(8,128)(2,1)}), bf16[4,128,1024]{2,1,0:T(8,128)(2,1)}, u32[]{:S(2)}, u32[]{:S(2)}) async-start(bf16[4,128,1024]{2,1,0:T(8,128)(2,1)} %pack.3), calls=%async_computation.1 | async-start | bytes 2097152 | tf_op jit(solution)/shard_map/all_to_all | solution.py:392
  63.7 14.2 %collective-permute-start.11 = (f32[544,256]{1,0:T(8,128)}, f32[544,256]{1,0:T(8,128)}, u32[]{:S(2)}, u32[]{:S(2)}) collective-permute-start(f32[544,256]{1,0:T(8,128)} %convert_add_fusion.1.mine), channel_id=1, source_target_pairs={{0,1},{1,0},{2,3},{3,2},{4,5},{5,4},{6,7},{7,6},{8,9},{9,8},{10,11... | collective-permute-start | bytes 1671176 | tf_op jit(solution)/shard_map/ppermute | solution.py:383
  68.0 9.0 %collective-permute-start.14 = (bf16[128,1024]{1,0:T(8,128)(2,1)}, bf16[128,1024]{1,0:T(8,128)(2,1)S(1)}, u32[]{:S(2)}, u32[]{:S(2)}) collective-permute-start(bf16[128,1024]{1,0:T(8,128)(2,1)} %bitcast.67), channel_id=1, source_target_pairs={{0,8},{2,10},{4,12},{6,14},{8,16},{10,18},{12,20},{14,22},{16,24},... | collective-permute-start | bytes 786440 | tf_op jit(solution)/shard_map/ppermute | solution.py:369
  100.7 8.4 %collective-permute-start.17 = (f32[17,1024]{1,0:T(8,128)S(1)}, f32[17,1024]{1,0:T(8,128)S(1)}, u32[]{:S(2)}, u32[]{:S(2)}) collective-permute-start(f32[17,1024]{1,0:T(8,128)S(1)} %get-tuple-element.68), channel_id=1, source_target_pairs={{0,24},{2,26},{4,28},{6,30},{8,0},{10,2},{12,4},{14,6},{16,8},{18,... | collective-permute-start | bytes 208904 | tf_op jit(solution)/shard_map/ppermute | solution.py:369
  163.5 27.8 %all-to-all-start.2 = ((bf16[4,128,1024]{2,1,0:T(8,128)(2,1)}), bf16[4,128,1024]{2,1,0:T(8,128)(2,1)S(1)}, u32[]{:S(2)}, u32[]{:S(2)}) async-start(bf16[4,128,1024]{2,1,0:T(8,128)(2,1)} %bitcast.70), calls=%async_computation.2 | async-start | bytes 2097152 | tf_op jit(solution)/shard_map/all_to_all | solution.py:428
  172.0 10.5 %collective-permute-start.21 = (bf16[544,256]{1,0:T(8,128)(2,1)S(1)}, bf16[544,256]{1,0:T(8,128)(2,1)S(1)}, u32[]{:S(2)}, u32[]{:S(2)}) collective-permute-start(bf16[544,256]{1,0:T(8,128)(2,1)S(1)} %get-tuple-element.49), channel_id=1, source_target_pairs={{0,6},{2,4},{4,2},{6,0},{8,14},{10,12},{12,10},{14,8},{16,22},{18,... | collective-permute-start | bytes 835592 | tf_op jit(solution)/shard_map/ppermute | solution.py:369
  173.7 14.0 %collective-permute-start.20 = (bf16[544,256]{1,0:T(8,128)(2,1)S(1)}, bf16[544,256]{1,0:T(8,128)(2,1)S(1)}, u32[]{:S(2)}, u32[]{:S(2)}) collective-permute-start(bf16[544,256]{1,0:T(8,128)(2,1)S(1)} %get-tuple-element.49), channel_id=1, source_target_pairs={{0,4},{2,6},{4,0},{6,2},{8,12},{10,14},{12,8},{14,10},{16,20},{18,... | collective-permute-start | bytes 835592 | tf_op jit(solution)/shard_map/ppermute | solution.py:369
  175.2 12.5 %collective-permute-start.19 = (bf16[544,256]{1,0:T(8,128)(2,1)S(1)}, bf16[544,256]{1,0:T(8,128)(2,1)S(1)}, u32[]{:S(2)}, u32[]{:S(2)}) collective-permute-start(bf16[544,256]{1,0:T(8,128)(2,1)S(1)} %get-tuple-element.49), channel_id=1, source_target_pairs={{0,2},{2,0},{4,6},{6,4},{8,10},{10,8},{12,14},{14,12},{16,18},{18,... | collective-permute-start | bytes 835592 | tf_op jit(solution)/shard_map/ppermute | solution.py:369
  191.3 19.6 %all-to-all-start.3 = ((bf16[4,128,1024]{2,1,0:T(8,128)(2,1)}), bf16[4,128,1024]{2,1,0:T(8,128)(2,1)}, u32[]{:S(2)}, u32[]{:S(2)}) async-start(bf16[4,128,1024]{2,1,0:T(8,128)(2,1)} %bitcast.69), calls=%async_computation.3 | async-start | bytes 2097152 | tf_op jit(solution)/shard_map/all_to_all | solution.py:392
  210.9 30.6 %all-to-all-start.4 = ((bf16[4,160,1024]{2,1,0:T(8,128)(2,1)}), bf16[4,160,1024]{2,1,0:T(8,128)(2,1)S(1)}, u32[]{:S(2)}, u32[]{:S(2)}) async-start(bf16[4,160,1024]{2,1,0:T(8,128)(2,1)} %copy-done.6), calls=%async_computation.4 | async-start | bytes 2621440 | tf_op jit(solution)/shard_map/all_to_all | solution.py:392
  221.9 10.4 %collective-permute-start.27 = (f32[23,256]{1,0:T(8,128)S(1)}, f32[23,256]{1,0:T(8,128)S(1)}, u32[]{:S(2)}, u32[]{:S(2)}) collective-permute-start(f32[23,256]{1,0:T(8,128)S(1)} %bitcast.79), channel_id=1, source_target_pairs={{0,8},{2,10},{4,12},{6,14},{8,16},{10,18},{12,20},{14,22},{16,24},... | collective-permute-start | bytes 70664 | tf_op jit(solution)/shard_map/ppermute | solution.py:369
  223.5 10.2 %collective-permute-start.28 = (f32[23,256]{1,0:T(8,128)S(1)}, f32[23,256]{1,0:T(8,128)S(1)}, u32[]{:S(2)}, u32[]{:S(2)}) collective-permute-start(f32[23,256]{1,0:T(8,128)S(1)} %bitcast.78), channel_id=1, source_target_pairs={{0,16},{2,18},{4,20},{6,22},{8,24},{10,26},{12,28},{14,30},{16,0},... | collective-permute-start | bytes 70664 | tf_op jit(solution)/shard_map/ppermute | solution.py:369
  227.6 9.1 %collective-permute-start.26 = (f32[16,1024]{1,0:T(8,128)S(1)}, f32[16,1024]{1,0:T(8,128)S(1)}, u32[]{:S(2)}, u32[]{:S(2)}) collective-permute-start(f32[16,1024]{1,0:T(8,128)S(1)} %copy-done.16), channel_id=1, source_target_pairs={{14,6},{22,14},{30,22},{15,7},{23,15},{31,23}} | collective-permute-start | bytes 196616 | tf_op jit(solution)/shard_map/ppermute | solution.py:369
  (45 other events, 349.4 us)

commit v4 on v3

--- a/solution.py
+++ b/solution.py
@@ -19,7 +19,6 @@
 LOG2E = 1.4426950408889634
 LN2 = 0.6931471805599453
 VMEM_LIMIT = 58 * 1024 * 1024
-VMEM_MIDDLE = 36 * 1024 * 1024
 VMEM_SMALL = 24 * 1024 * 1024
 F32 = jnp.float32
 BF16 = jnp.bfloat16
@@ -77,8 +76,8 @@
 
 
 def local_kernel(
-    core, mine, other, dtw, dtb, act, g, alog, step_out, sig_out, state_out, adjoint_out, bc,
-    a2, us, gs, spread, low,
+    core, mine, other, dtw, dtb, act, g, alog, step_to, sig_to, state_out, adjoint_out, bc,
+    a2, us, gs, spread, low, step_out, sig_out, done,
 ):
     tokens, width = act.shape
     rank = dtw.shape[0]
@@ -107,6 +106,12 @@
         return total + jnp.sum(step, axis=0, keepdims=True)
 
     total = lax.fori_loop(0, tokens // block, prepare, jnp.zeros((1, width), F32))
+    copies = [
+        pltpu.make_async_copy(step_out, step_to, done.at[0]),
+        pltpu.make_async_copy(sig_out, sig_to, done.at[1]),
+    ]
+    for copy in copies:
+        copy.start()
     state_out[STATE : STATE + 1, :] = total
     adjoint_out[STATE : STATE + 1, :] = total
     zeros = jnp.zeros((8, LANES), F32)
@@ -136,6 +141,8 @@
                 n = base + k
                 state_out[n : n + 1, columns] = h[k].reshape(1, 8 * LANES)
                 adjoint_out[n : n + 1, columns] = lam[k].reshape(1, 8 * LANES)
+    for copy in copies:
+        copy.wait()
 
 
 def full_kernel(
@@ -278,11 +285,14 @@
             jax.ShapeDtypeStruct(dense, F32), jax.ShapeDtypeStruct((tokens, channels), F32), ends, ends,
             jax.ShapeDtypeStruct((2 * STATE, tokens), F32),
         ],
+        out_specs=[pl.BlockSpec(memory_space=pl.ANY)] * 2 + vmem_specs(3),
         scratch_shapes=[
             pltpu.VMEM((STATE,) + dense[1:], F32), pltpu.VMEM(dense, F32), pltpu.VMEM(dense, F32),
             pltpu.VMEM((2 * STATE, tokens, LANES), F32), pltpu.VMEM((dtw.shape[0], tokens), BF16),
+            pltpu.VMEM(dense, F32), pltpu.VMEM((tokens, channels), F32),
+            pltpu.SemaphoreType.DMA((2,)),
         ],
-        compiler_params=pltpu.CompilerParams(vmem_limit_bytes=VMEM_MIDDLE),
+        compiler_params=pltpu.CompilerParams(vmem_limit_bytes=VMEM_LIMIT),
         cost_estimate=took(22),
         name="scan_local",
     )(*operands)
@@ -422,6 +432,30 @@
                     out[last, target] = total.astype(out.dtype)
 
 
+def gate_kernel(share, x, gate, up, flags, out):
+    for q in range(PLANE):
+        for z in range(x.shape[2] // share):
+            target = (z * PLANE + q) * share
+            target = slice(target, target + share)
+            value = gate[:, target].astype(F32)
+            s = 1.0 / (1.0 + jnp.exp(-value))
+            factor = -flags[...] * up[:, target].astype(F32) * (s * (1.0 + value * (1.0 - s)))
+            mixed = x[q, :, z * share : (z + 1) * share].astype(F32)
+            out[:, target] = (factor * mixed).astype(BF16)
+
+
+def gate_gradient(x, gate, up, flags):
+    share = x.shape[2] * PLANE // lax.axis_size("ctx")
+    return pl.pallas_call(
+        functools.partial(gate_kernel, share),
+        in_specs=vmem_specs(4),
+        out_specs=vmem_specs(1)[0],
+        out_shape=jax.ShapeDtypeStruct(gate.shape, BF16),
+        cost_estimate=took(4),
+        name="gate_gradient",
+    )(x, gate, up, flags.astype(F32)[:, None])
+
+
 def along_line(x):
     count = lax.axis_size("ctx")
     groups = [list(range(i, count, PLANE)) for i in range(PLANE)]
@@ -509,10 +543,9 @@
     return lax.dynamic_index_in_dim(x, at, axis, keepdims=False)
 
 
-def sum_plane(mine, other, *earlier):
-    core = lax.axis_index("mp")
-    mine = mine + swap_mp(other)
-    half = after(mine.astype(BF16), *earlier)
+def sum_plane(mine, received):
+    mine = mine + received
+    half = mine.astype(BF16)
     routes = [[(i, i ^ bits) for i in range(lax.axis_size("ctx"))] for bits in range(1, PLANE)]
     total = mine
     for route in routes:
@@ -742,7 +775,7 @@
     )
     act = conv_head(moved, before, weight, bias, rows)
     dt_plane = moved[:, rows:].reshape(PLANE * dt_rows, -1)
-    grad_mixed, gate_factor = gate_parts(gate_in, upstream, forget_flags)
+    grad_mixed, _ = gate_parts(gate_in, upstream, forget_flags)
     mixed_packed = by_owner(grad_mixed)
     grad_mixed = in_plane(after(mixed_packed, moved)).reshape(PLANE * rows, -1)
 
@@ -750,7 +783,7 @@
     rows_proj = place_blocks(proj_blocks, 1)
     dt_blocks = line_blocks(dt_plane)
     part = lambda at: matmul(rows_proj, lax.dynamic_slice_in_dim(act, at * half, half), (1, 1))
-    mine, other = sum_plane(part(core), part(1 - core))
+    mine, other = sum_plane(part(core), swap_mp(part(1 - core)))
     rows_dt = place_blocks(dt_blocks, 0)
     step, sig, state, adjoint, bc = scan_local(
         here, mine, other, rows_dt, step_bias, act, grad_mixed, rates
@@ -763,15 +796,14 @@
 
     dtw_sums = matmul(low, grad_pre, (1, 0)).astype(BF16)
     dtw_moved = along_line(dtw_sums.reshape(planes, RANK // planes, -1))
-    mine, other = sum_plane(grad_mine, grad_other, dtw_sums)
+    mine, other = sum_plane(grad_mine, swap_mp(after(grad_other, dtw_sums)))
     mine, other = mine.astype(BF16), other.astype(BF16)
     packed, grad_conv, early = conv_tail(
         here, mine, other, rows_proj, grad_act, moved, before, weight, bias, dtw_moved
     )
     grad_gate = in_plane(after(mixed, mine).reshape(PLANE, rows, -1))
     returned = in_plane(after(packed, grad_gate))
-    (grad_gate,) = to_tokens(after(grad_gate, packed), (rows, F32))
-    grad_gate = (gate_factor * grad_gate).astype(BF16)
+    grad_gate = gate_gradient(after(grad_gate, packed), gate_in, upstream, forget_flags)
     late = late_rows(after(early, grad_gate))
     sums = jnp.concatenate([grad_conv, grad_vecs, grad_rate], axis=0)
     sums = sum_line(after(sums, grad_gate))

time: 248 us -> 243 us (0.980)
  other arithmetic: 10.5 us -> 7.76 us
    unnamed x79 -> x57, local copies, waits for them, and re-layouts: 11.7 us -> 7.67 us
    pallas_call x0 -> x1, Pallas kernels: none -> 3.96 us  [gate_gradient(): pl.pallas_call(functools.partial(gate_kernel, share), in_specs=vmem_specs...]
    convert_element_type x2 -> x1, other arithmetic: 4.96 us -> 1.18 us  [sum_plane(): half = mine.astype(BF16)]
    pallas_call x2 -> x1, Pallas kernels: 5.45 us -> 2.68 us  [to_tokens(): pl.pallas_call(functools.partial(unpack_kernel, share, len(results)), in_...]
where the time goes in v4:
time: 243 us; the launch traced here: 241 us
  Pallas kernels  88.3 us (36%)
  starting transfers between devices  65 us (27%)
  waiting for transfers between devices  43.7 us (18%)
  local copies, waits for them, and re-layouts  28.6 us (12%)
  other arithmetic  7.76 us (3%)
  matrix products  6.68 us (3%)
    pallas_call x1, Pallas kernels, scan_full(): pl.pallas_call(full_kernel, in_specs=[pl.BlockSpec(memory_space=pltpu.SME...  48.2 us
    ppermute x26, starting transfers between devices, send(): return lax.ppermute(x, 'ctx', route)  40.9 us
    ppermute x26, waiting for transfers between devices, send(): return lax.ppermute(x, 'ctx', route)  34.6 us
    pallas_call x1, Pallas kernels, scan_local(): pl.pallas_call(local_kernel, in_specs=[pl.BlockSpec(memory_space=pltpu.SM...  19.8 us
    all_to_all x4, starting transfers between devices, in_plane(): lax.all_to_all(x, 'ctx', 0, 0, axis_index_groups=plane_groups(), tiled=True)  18.9 us
    dynamic_update_slice x8, local copies, waits for them, and re-layouts, place_blocks(): lax.dynamic_update_slice(out, block, (at, 0) if axis == 0 else (0, at))  8.86 us
    unnamed x57, local copies, waits for them, and re-layouts  7.67 us
    pallas_call x1, Pallas kernels, conv_tail(): pl.pallas_call(tail_kernel, in_specs=[pl.BlockSpec(memory_space=pltpu.SME...  6.78 us
  transfers between devices with their start and end apart: 35, of which 15 were waited for; matrix products, arithmetic and copies ran while one was open for 10% of the time, Pallas kernels for 7%

profile of v4, /device:TPU:14, one launch (start us, length us, event | category | flops | bytes accessed | tf_op | source)
XLA Modules:
  0.0 241.2 jit_solution(8843704187733866073)
XLA Ops:
  8.4 2.6 %collective-permute-start.6 = (bf16[3,1024]{1,0:T(4,128)(2,1)S(1)}, bf16[3,1024]{1,0:T(4,128)(2,1)S(1)}, u32[]{:S(2)}, u32[]{:S(2)}) collective-permute-start(bf16[3,1024]{1,0:T(4,128)(2,1)S(1)} %bitcast.90), channel_id=1, source_target_pairs={{6,14},{14,22},{22,30},{7,15},{15,23},{23,31}} | collective-permute-start | bytes 18440 | tf_op jit(solution)/shard_map/ppermute | solution.py:379
  11.0 2.5 %pack.2 = bf16[4,160,1024]{2,1,0:T(8,128)(2,1)} custom-call(bf16[128,4096]{1,0:T(8,128)(2,1)} %refs_0_.1, bf16[32,4096]{1,0:T(8,128)(2,1)} %refs_1_.1), custom_call_target="tpu_custom_call" | custom-call | bytes 7200000 | tf_op jit(solution)/shard_map/pack/pallas_call | solution.py:469
  13.5 4.3 %all-to-all-start = ((bf16[4,160,1024]{2,1,0:T(8,128)(2,1)}), bf16[4,160,1024]{2,1,0:T(8,128)(2,1)S(1)}, u32[]{:S(2)}, u32[]{:S(2)}) async-start(bf16[4,160,1024]{2,1,0:T(8,128)(2,1)} %pack.2), calls=%async_computation | async-start | bytes 2621440 | tf_op jit(solution)/shard_map/all_to_all | solution.py:402
  19.7 6.9 %collective-permute-done.5 = bf16[3,1024]{1,0:T(4,128)(2,1)S(1)} collective-permute-done((bf16[3,1024]{1,0:T(4,128)(2,1)S(1)}, bf16[3,1024]{1,0:T(4,128)(2,1)S(1)}, u32[]{:S(2)}, u32[]{:S(2)}) %collective-permute-start.5) | collective-permute-done | bytes 6176 | tf_op jit(solution)/shard_map/ppermute | solution.py:379
  29.4 2.3 pack.3
  39.2 2.3 collective-permute-done.7
  41.5 2.4 %fusion.22 = (bf16[544,256]{1,0:T(8,128)(2,1)}, f32[544,256]{1,0:T(8,128)}) fusion(f32[544,256]{1,0:T(8,128)} %collective-permute-done.7, bf16[544,1024]{1,0:T(8,128)(2,1)S(1)} %constant_dynamic-update-slice_fusion.4.rows_proj, bf16[512,1024]{1,0:T(8,128)(2,1)S(1)} %conv_head.1.act, s32[]{:T(128)S(6)} %select_n.148), kind=kOutput, calls=%fused_computation.70 | convolution fusion | flops 285491200 | bytes 3031044 | tf_op jit(solution)/shard_map/dot_general | solution.py:742
  50.2 4.5 %all-to-all-start.1 = ((bf16[4,128,1024]{2,1,0:T(8,128)(2,1)}), bf16[4,128,1024]{2,1,0:T(8,128)(2,1)S(1)}, u32[]{:S(2)}, u32[]{:S(2)}) async-start(bf16[4,128,1024]{2,1,0:T(8,128)(2,1)} %pack.3), calls=%async_computation.1 | async-start | bytes 2097152 | tf_op jit(solution)/shard_map/all_to_all | solution.py:402
  54.7 5.2 %collective-permute-done.9 = bf16[544,256]{1,0:T(8,128)(2,1)} collective-permute-done((bf16[544,256]{1,0:T(8,128)(2,1)}, bf16[544,256]{1,0:T(8,128)(2,1)}, u32[]{:S(2)}, u32[]{:S(2)}) %collective-permute-start.9) | collective-permute-done | bytes 278560 | tf_op jit(solution)/shard_map/ppermute | solution.py:379
  77.6 19.8 %scan_local.1 = (f32[512,8,128]{2,1,0:T(8,128)}, f32[512,1024]{1,0:T(8,128)}, f32[17,1024]{1,0:T(8,128)}, f32[17,1024]{1,0:T(8,128)}, f32[32,512]{1,0:T(8,128)}) custom-call(s32[1]{0:T(128)} %bitcast.core, f32[544,256]{1,0:T(8,128)} %convert_add_fusion.1.mine, f32[544,256]{1,0:T(8,128)} %collective-permute-done.11.other, ...), custom_call_target="tpu_custom_call" | custom-call | bytes 79200000 | tf_op jit(solution)/shard_map/scan_local/pallas_call | solution.py:281
  98.4 3.1 %collective-permute-start.17 = (f32[17,1024]{1,0:T(8,128)S(1)}, f32[17,1024]{1,0:T(8,128)S(1)}, u32[]{:S(2)}, u32[]{:S(2)}) collective-permute-start(f32[17,1024]{1,0:T(8,128)S(1)} %get-tuple-element.68), channel_id=1, source_target_pairs={{0,24},{2,26},{4,28},{6,30},{8,0},{10,2},{12,4},{14,6},{16,8},{18,... | collective-permute-start | bytes 208904 | tf_op jit(solution)/shard_map/ppermute | solution.py:379
  110.4 48.2 %scan_full.1 = (bf16[512,1024]{1,0:T(8,128)(2,1)}, bf16[512,1024]{1,0:T(8,128)(2,1)}, f32[512,1024]{1,0:T(8,128)}, f32[16,1024]{1,0:T(8,128)}, f32[2,1024]{1,0:T...) custom-call(s32[1]{0:T(128)} %bitcast.core, f32[32,512]{1,0:T(8,128)} %get-tuple-element.41.bc, ...), custom_call_target="tpu_custom_call" | custom-call | bytes 183600000 | tf_op jit(solution)/shard_map/scan_full/pallas_call | solution.py:308
  158.6 2.9 %convolution_convert_fusion = bf16[512,1024]{1,0:T(8,128)(2,1)} fusion(bf16[512,1024]{1,0:T(8,128)(2,1)} %get-tuple-element.48, bf16[512,256]{1,0:T(8,128)(2,1)S(1)} %slice.110, bf16[512,256]{1,0:T(8,128)(2,1)S(1)} %slice.111, pred[]{:T(512)S(6)} %eq.9), kind=kOutput, calls=%fused_computation.7 | convolution fusion | flops 539754496 | bytes 2621441 | tf_op jit(solution)/shard_map/dot_general | solution.py:742
  161.5 5.2 %all-to-all-start.2 = ((bf16[4,128,1024]{2,1,0:T(8,128)(2,1)}), bf16[4,128,1024]{2,1,0:T(8,128)(2,1)S(1)}, u32[]{:S(2)}, u32[]{:S(2)}) async-start(bf16[4,128,1024]{2,1,0:T(8,128)(2,1)} %bitcast.73), calls=%async_computation.2 | async-start | bytes 2097152 | tf_op jit(solution)/shard_map/all_to_all | solution.py:462
  173.6 7.0 %collective-permute-done.21 = bf16[544,256]{1,0:T(8,128)(2,1)S(1)} collective-permute-done((bf16[544,256]{1,0:T(8,128)(2,1)S(1)}, bf16[544,256]{1,0:T(8,128)(2,1)S(1)}, u32[]{:S(2)}, u32[]{:S(2)}) %collective-permute-start.21) | collective-permute-done | bytes 278560 | tf_op jit(solution)/shard_map/ppermute | solution.py:379
  180.5 5.1 %collective-permute-done.20 = bf16[544,256]{1,0:T(8,128)(2,1)S(1)} collective-permute-done((bf16[544,256]{1,0:T(8,128)(2,1)S(1)}, bf16[544,256]{1,0:T(8,128)(2,1)S(1)}, u32[]{:S(2)}, u32[]{:S(2)}) %collective-permute-start.20) | collective-permute-done | bytes 278560 | tf_op jit(solution)/shard_map/ppermute | solution.py:379
  186.5 2.8 %all-to-all-done.2.dt_parts = bf16[4,128,1024]{2,1,0:T(8,128)(2,1)S(1)} async-done(((bf16[4,128,1024]{2,1,0:T(8,128)(2,1)}), bf16[4,128,1024]{2,1,0:T(8,128)(2,1)S(1)}, u32[]{:S(2)}, u32[]{:S(2)}) %all-to-all-start.2) | async-done | bytes 1048608 | tf_op jit(solution)/shard_map/all_to_all | solution.py:462
  189.3 5.8 %all-to-all-start.3 = ((bf16[4,128,1024]{2,1,0:T(8,128)(2,1)}), bf16[4,128,1024]{2,1,0:T(8,128)(2,1)}, u32[]{:S(2)}, u32[]{:S(2)}) async-start(bf16[4,128,1024]{2,1,0:T(8,128)(2,1)} %bitcast.72), calls=%async_computation.3 | async-start | bytes 2097152 | tf_op jit(solution)/shard_map/all_to_all | solution.py:402
  199.4 6.8 %conv_tail.1 = (bf16[4,160,1024]{2,1,0:T(8,128)(2,1)S(1)}, f32[5,1024]{1,0:T(8,128)S(1)}, f32[16,1024]{1,0:T(8,128)S(1)}) custom-call(s32[1]{0:T(128)} %bitcast.core, bf16[544,256]{1,0:T(8,128)(2,1)S(1)} %copy-done.3, bf16[544,256]{1,0:T(8,128)(2,1)S(1)} %collective-permute-done.22.other, ...), custom_call_target="tpu_custom_call" | custom-call | bytes 28800000 | tf_op jit(solution)/shard_map/conv_tail/pallas_call | solution.py:665
  207.9 4.3 %all-to-all-start.4 = ((bf16[4,160,1024]{2,1,0:T(8,128)(2,1)}), bf16[4,160,1024]{2,1,0:T(8,128)(2,1)S(1)}, u32[]{:S(2)}, u32[]{:S(2)}) async-start(bf16[4,160,1024]{2,1,0:T(8,128)(2,1)} %copy-done.2), calls=%async_computation.4 | async-start | bytes 2621440 | tf_op jit(solution)/shard_map/all_to_all | solution.py:402
  213.0 4.0 %gate_gradient.1 = bf16[128,4096]{1,0:T(8,128)(2,1)} custom-call(bf16[4,128,1024]{2,1,0:T(8,128)(2,1)} %all-to-all-done.3.x, bf16[128,4096]{1,0:T(8,128)(2,1)} %gate.1, bf16[128,4096]{1,0:T(8,128)(2,1)} %up.1, f32[128,1]{1,0:T(8,128)} %copy.32.flags), custom_call_target="tpu_custom_call" | custom-call | bytes 14400000 | tf_op jit(solution)/shard_map/gate_gradient/pallas_call | solution.py:449
  218.7 4.2 %collective-permute-start.28 = (f32[23,256]{1,0:T(8,128)S(1)}, f32[23,256]{1,0:T(8,128)S(1)}, u32[]{:S(2)}, u32[]{:S(2)}) collective-permute-start(f32[23,256]{1,0:T(8,128)S(1)} %bitcast.81), channel_id=1, source_target_pairs={{0,16},{2,18},{4,20},{6,22},{8,24},{10,26},{12,28},{14,30},{16,0},... | collective-permute-start | bytes 70664 | tf_op jit(solution)/shard_map/ppermute | solution.py:379
  222.8 3.4 %collective-permute-start.26 = (f32[16,1024]{1,0:T(8,128)S(1)}, f32[16,1024]{1,0:T(8,128)S(1)}, u32[]{:S(2)}, u32[]{:S(2)}) collective-permute-start(f32[16,1024]{1,0:T(8,128)S(1)} %copy-done.5), channel_id=1, source_target_pairs={{14,6},{22,14},{30,22},{15,7},{23,15},{31,23}} | collective-permute-start | bytes 196616 | tf_op jit(solution)/shard_map/ppermute | solution.py:379
  238.5 2.7 %unpack.1 = (bf16[128,4096]{1,0:T(8,128)(2,1)}, f32[32,4096]{1,0:T(8,128)}) custom-call(bf16[4,160,1024]{2,1,0:T(8,128)(2,1)} %copy-done.7, f32[16,1024]{1,0:T(8,128)} %copy-done.16, f32[16,1024]{1,0:T(8,128)} %copy-done.15, f32[16,1024]{1,0:T(8,128)} %copy-done.14, f32[16,1024]{1,0:T(8,128)} %copy-done.13), custom_call_target="tpu_custom_call" | custom-call | bytes 7200000 | tf_op jit(solution)/shard_map/unpack/pallas_call | solution.py:482
  (161 shorter events, 81.6 us)
Async XLA Ops:
  0.6 33.9 %collective-permute-start.2 = (bf16[544,256]{1,0:T(8,128)(2,1)}, bf16[544,256]{1,0:T(8,128)(2,1)}, u32[]{:S(2)}, u32[]{:S(2)}) collective-permute-start(bf16[544,256]{1,0:T(8,128)(2,1)} %bitcast.74), channel_id=1, source_target_pairs={{0,8},{2,10},{4,12},{6,14},{8,16},{10,18},{12,20},{14,22},{16,24},... | collective-permute-start | bytes 835592 | tf_op jit(solution)/shard_map/ppermute | solution.py:379
  2.3 32.3 %collective-permute-start.1 = (bf16[544,256]{1,0:T(8,128)(2,1)}, bf16[544,256]{1,0:T(8,128)(2,1)}, u32[]{:S(2)}, u32[]{:S(2)}) collective-permute-start(bf16[544,256]{1,0:T(8,128)(2,1)} %bitcast.75), channel_id=1, source_target_pairs={{0,16},{2,18},{4,20},{6,22},{8,24},{10,26},{12,28},{14,30},{16,0},... | collective-permute-start | bytes 835592 | tf_op jit(solution)/shard_map/ppermute | solution.py:379
  3.5 31.1 %collective-permute-start = (bf16[544,256]{1,0:T(8,128)(2,1)}, bf16[544,256]{1,0:T(8,128)(2,1)}, u32[]{:S(2)}, u32[]{:S(2)}) collective-permute-start(bf16[544,256]{1,0:T(8,128)(2,1)} %bitcast.76), channel_id=1, source_target_pairs={{0,24},{2,26},{4,28},{6,30},{8,0},{10,2},{12,4},{14,6},{16,8},{18,... | collective-permute-start | bytes 835592 | tf_op jit(solution)/shard_map/ppermute | solution.py:379
  6.3 20.3 %collective-permute-start.5 = (bf16[3,1024]{1,0:T(4,128)(2,1)S(1)}, bf16[3,1024]{1,0:T(4,128)(2,1)S(1)}, u32[]{:S(2)}, u32[]{:S(2)}) collective-permute-start(bf16[3,1024]{1,0:T(4,128)(2,1)S(1)} %bitcast.91), channel_id=1, source_target_pairs={{6,12},{14,20},{22,28},{7,13},{15,21},{23,29}} | collective-permute-start | bytes 18440 | tf_op jit(solution)/shard_map/ppermute | solution.py:379
  8.4 19.5 %collective-permute-start.6 = (bf16[3,1024]{1,0:T(4,128)(2,1)S(1)}, bf16[3,1024]{1,0:T(4,128)(2,1)S(1)}, u32[]{:S(2)}, u32[]{:S(2)}) collective-permute-start(bf16[3,1024]{1,0:T(4,128)(2,1)S(1)} %bitcast.90), channel_id=1, source_target_pairs={{6,14},{14,22},{22,30},{7,15},{15,23},{23,31}} | collective-permute-start | bytes 18440 | tf_op jit(solution)/shard_map/ppermute | solution.py:379
  13.5 18.3 %all-to-all-start = ((bf16[4,160,1024]{2,1,0:T(8,128)(2,1)}), bf16[4,160,1024]{2,1,0:T(8,128)(2,1)S(1)}, u32[]{:S(2)}, u32[]{:S(2)}) async-start(bf16[4,160,1024]{2,1,0:T(8,128)(2,1)} %pack.2), calls=%async_computation | async-start | bytes 2621440 | tf_op jit(solution)/shard_map/all_to_all | solution.py:402
  44.0 10.8 %collective-permute-start.10 = (bf16[544,256]{1,0:T(8,128)(2,1)}, bf16[544,256]{1,0:T(8,128)(2,1)}, u32[]{:S(2)}, u32[]{:S(2)}) collective-permute-start(bf16[544,256]{1,0:T(8,128)(2,1)} %get-tuple-element.82), channel_id=1, source_target_pairs={{0,6},{2,4},{4,2},{6,0},{8,14},{10,12},{12,10},{14,8},{16,22},{18,... | collective-permute-start | bytes 835592 | tf_op jit(solution)/shard_map/ppermute | solution.py:379
  45.2 14.8 %collective-permute-start.9 = (bf16[544,256]{1,0:T(8,128)(2,1)}, bf16[544,256]{1,0:T(8,128)(2,1)}, u32[]{:S(2)}, u32[]{:S(2)}) collective-permute-start(bf16[544,256]{1,0:T(8,128)(2,1)} %get-tuple-element.82), channel_id=1, source_target_pairs={{0,4},{2,6},{4,0},{6,2},{8,12},{10,14},{12,8},{14,10},{16,20},{18,... | collective-permute-start | bytes 835592 | tf_op jit(solution)/shard_map/ppermute | solution.py:379
  46.9 13.6 %collective-permute-start.8 = (bf16[544,256]{1,0:T(8,128)(2,1)}, bf16[544,256]{1,0:T(8,128)(2,1)}, u32[]{:S(2)}, u32[]{:S(2)}) collective-permute-start(bf16[544,256]{1,0:T(8,128)(2,1)} %get-tuple-element.82), channel_id=1, source_target_pairs={{0,2},{2,0},{4,6},{6,4},{8,10},{10,8},{12,14},{14,12},{16,18},{18,... | collective-permute-start | bytes 835592 | tf_op jit(solution)/shard_map/ppermute | solution.py:379
  47.5 25.2 %collective-permute-start.13 = (bf16[128,1024]{1,0:T(8,128)(2,1)}, bf16[128,1024]{1,0:T(8,128)(2,1)}, u32[]{:S(2)}, u32[]{:S(2)}) collective-permute-start(bf16[128,1024]{1,0:T(8,128)(2,1)} %bitcast.68), channel_id=1, source_target_pairs={{0,16},{2,18},{4,20},{6,22},{8,24},{10,26},{12,28},{14,30},{16,0},... | collective-permute-start | bytes 786440 | tf_op jit(solution)/shard_map/ppermute | solution.py:379
  48.7 22.3 %collective-permute-start.12 = (bf16[128,1024]{1,0:T(8,128)(2,1)}, bf16[128,1024]{1,0:T(8,128)(2,1)}, u32[]{:S(2)}, u32[]{:S(2)}) collective-permute-start(bf16[128,1024]{1,0:T(8,128)(2,1)} %bitcast.69), channel_id=1, source_target_pairs={{0,24},{2,26},{4,28},{6,30},{8,0},{10,2},{12,4},{14,6},{16,8},{18,... | collective-permute-start | bytes 786440 | tf_op jit(solution)/shard_map/ppermute | solution.py:379
  50.2 26.3 %all-to-all-start.1 = ((bf16[4,128,1024]{2,1,0:T(8,128)(2,1)}), bf16[4,128,1024]{2,1,0:T(8,128)(2,1)S(1)}, u32[]{:S(2)}, u32[]{:S(2)}) async-start(bf16[4,128,1024]{2,1,0:T(8,128)(2,1)} %pack.3), calls=%async_computation.1 | async-start | bytes 2097152 | tf_op jit(solution)/shard_map/all_to_all | solution.py:402
  62.7 13.9 %collective-permute-start.11 = (f32[544,256]{1,0:T(8,128)}, f32[544,256]{1,0:T(8,128)}, u32[]{:S(2)}, u32[]{:S(2)}) collective-permute-start(f32[544,256]{1,0:T(8,128)} %convert_add_fusion.1.mine), channel_id=1, source_target_pairs={{0,1},{1,0},{2,3},{3,2},{4,5},{5,4},{6,7},{7,6},{8,9},{9,8},{10,11... | collective-permute-start | bytes 1671176 | tf_op jit(solution)/shard_map/ppermute | solution.py:393
  66.9 8.9 %collective-permute-start.14 = (bf16[128,1024]{1,0:T(8,128)(2,1)}, bf16[128,1024]{1,0:T(8,128)(2,1)S(1)}, u32[]{:S(2)}, u32[]{:S(2)}) collective-permute-start(bf16[128,1024]{1,0:T(8,128)(2,1)} %bitcast.70), channel_id=1, source_target_pairs={{0,8},{2,10},{4,12},{6,14},{8,16},{10,18},{12,20},{14,22},{16,24},... | collective-permute-start | bytes 786440 | tf_op jit(solution)/shard_map/ppermute | solution.py:379
  101.6 8.0 %collective-permute-start.15 = (f32[17,1024]{1,0:T(8,128)S(1)}, f32[17,1024]{1,0:T(8,128)S(1)}, u32[]{:S(2)}, u32[]{:S(2)}) collective-permute-start(f32[17,1024]{1,0:T(8,128)S(1)} %get-tuple-element.70), channel_id=1, source_target_pairs={{0,8},{2,10},{4,12},{6,14},{8,16},{10,18},{12,20},{14,22},{16,24},... | collective-permute-start | bytes 208904 | tf_op jit(solution)/shard_map/ppermute | solution.py:379
  161.5 27.8 %all-to-all-start.2 = ((bf16[4,128,1024]{2,1,0:T(8,128)(2,1)}), bf16[4,128,1024]{2,1,0:T(8,128)(2,1)S(1)}, u32[]{:S(2)}, u32[]{:S(2)}) async-start(bf16[4,128,1024]{2,1,0:T(8,128)(2,1)} %bitcast.73), calls=%async_computation.2 | async-start | bytes 2097152 | tf_op jit(solution)/shard_map/all_to_all | solution.py:462
  170.0 10.5 %collective-permute-start.21 = (bf16[544,256]{1,0:T(8,128)(2,1)S(1)}, bf16[544,256]{1,0:T(8,128)(2,1)S(1)}, u32[]{:S(2)}, u32[]{:S(2)}) collective-permute-start(bf16[544,256]{1,0:T(8,128)(2,1)S(1)} %get-tuple-element.64), channel_id=1, source_target_pairs={{0,6},{2,4},{4,2},{6,0},{8,14},{10,12},{12,10},{14,8},{16,22},{18,... | collective-permute-start | bytes 835592 | tf_op jit(solution)/shard_map/ppermute | solution.py:379
  171.7 14.0 %collective-permute-start.20 = (bf16[544,256]{1,0:T(8,128)(2,1)S(1)}, bf16[544,256]{1,0:T(8,128)(2,1)S(1)}, u32[]{:S(2)}, u32[]{:S(2)}) collective-permute-start(bf16[544,256]{1,0:T(8,128)(2,1)S(1)} %get-tuple-element.64), channel_id=1, source_target_pairs={{0,4},{2,6},{4,0},{6,2},{8,12},{10,14},{12,8},{14,10},{16,20},{18,... | collective-permute-start | bytes 835592 | tf_op jit(solution)/shard_map/ppermute | solution.py:379
  173.1 12.5 %collective-permute-start.19 = (bf16[544,256]{1,0:T(8,128)(2,1)S(1)}, bf16[544,256]{1,0:T(8,128)(2,1)S(1)}, u32[]{:S(2)}, u32[]{:S(2)}) collective-permute-start(bf16[544,256]{1,0:T(8,128)(2,1)S(1)} %get-tuple-element.64), channel_id=1, source_target_pairs={{0,2},{2,0},{4,6},{6,4},{8,10},{10,8},{12,14},{14,12},{16,18},{18,... | collective-permute-start | bytes 835592 | tf_op jit(solution)/shard_map/ppermute | solution.py:379
  189.3 18.6 %all-to-all-start.3 = ((bf16[4,128,1024]{2,1,0:T(8,128)(2,1)}), bf16[4,128,1024]{2,1,0:T(8,128)(2,1)}, u32[]{:S(2)}, u32[]{:S(2)}) async-start(bf16[4,128,1024]{2,1,0:T(8,128)(2,1)} %bitcast.72), calls=%async_computation.3 | async-start | bytes 2097152 | tf_op jit(solution)/shard_map/all_to_all | solution.py:402
  207.9 28.9 %all-to-all-start.4 = ((bf16[4,160,1024]{2,1,0:T(8,128)(2,1)}), bf16[4,160,1024]{2,1,0:T(8,128)(2,1)S(1)}, u32[]{:S(2)}, u32[]{:S(2)}) async-start(bf16[4,160,1024]{2,1,0:T(8,128)(2,1)} %copy-done.2), calls=%async_computation.4 | async-start | bytes 2621440 | tf_op jit(solution)/shard_map/all_to_all | solution.py:402
  217.1 10.4 %collective-permute-start.27 = (f32[23,256]{1,0:T(8,128)S(1)}, f32[23,256]{1,0:T(8,128)S(1)}, u32[]{:S(2)}, u32[]{:S(2)}) collective-permute-start(f32[23,256]{1,0:T(8,128)S(1)} %bitcast.82), channel_id=1, source_target_pairs={{0,8},{2,10},{4,12},{6,14},{8,16},{10,18},{12,20},{14,22},{16,24},... | collective-permute-start | bytes 70664 | tf_op jit(solution)/shard_map/ppermute | solution.py:379
  218.7 10.2 %collective-permute-start.28 = (f32[23,256]{1,0:T(8,128)S(1)}, f32[23,256]{1,0:T(8,128)S(1)}, u32[]{:S(2)}, u32[]{:S(2)}) collective-permute-start(f32[23,256]{1,0:T(8,128)S(1)} %bitcast.81), channel_id=1, source_target_pairs={{0,16},{2,18},{4,20},{6,22},{8,24},{10,26},{12,28},{14,30},{16,0},... | collective-permute-start | bytes 70664 | tf_op jit(solution)/shard_map/ppermute | solution.py:379
  222.8 9.1 %collective-permute-start.26 = (f32[16,1024]{1,0:T(8,128)S(1)}, f32[16,1024]{1,0:T(8,128)S(1)}, u32[]{:S(2)}, u32[]{:S(2)}) collective-permute-start(f32[16,1024]{1,0:T(8,128)S(1)} %copy-done.5), channel_id=1, source_target_pairs={{14,6},{22,14},{30,22},{15,7},{23,15},{31,23}} | collective-permute-start | bytes 196616 | tf_op jit(solution)/shard_map/ppermute | solution.py:379
  (34 other events, 160.5 us)

commit v5 on v4

--- a/solution.py
+++ b/solution.py
@@ -12,7 +12,7 @@
 PLANE = 4
 LANES = 128
 GROUP = 8
-UNROLL = 8
+UNROLL = 16
 BLOCK = 32
 COLUMNS = 256
 LAST = 16
@@ -259,8 +259,8 @@
         at = pl.ds(pl.multiple_of(which * half, half), half)
         out[:rank, :] = lax.dot_general(
             dtw[...], pre_out[at, :], (((1,), (1,)), ((), ())), preferred_element_type=F32
-        )
-        out[rank:, :] = both_rows[at, :].T[: 2 * STATE]
+        ).astype(out.dtype)
+        out[rank:, :] = both_rows[at, :].T[: 2 * STATE].astype(out.dtype)
 
 
 def took(microseconds):
@@ -304,7 +304,7 @@
     flat = (tokens, channels)
     operands = (core, bc, dtw, step, sig, act, g, alog, carries, skip)
     small = pltpu.VMEM((tokens, STATE, LANES), F32)
-    half = jax.ShapeDtypeStruct((dtw.shape[0] + 2 * STATE, tokens // 2), F32)
+    half = (dtw.shape[0] + 2 * STATE, tokens // 2)
     return pl.pallas_call(
         full_kernel,
         in_specs=[pl.BlockSpec(memory_space=pltpu.SMEM)] + vmem_specs(len(operands) - 1),
@@ -314,8 +314,8 @@
             jax.ShapeDtypeStruct(flat, F32),
             jax.ShapeDtypeStruct((STATE, channels), F32),
             jax.ShapeDtypeStruct((2, channels), F32),
-            half,
-            half,
+            jax.ShapeDtypeStruct(half, F32),
+            jax.ShapeDtypeStruct(half, BF16),
         ],
         scratch_shapes=[
             pltpu.VMEM((STATE,) + dense[1:], F32),
@@ -544,7 +544,7 @@
 
 
 def sum_plane(mine, received):
-    mine = mine + received
+    mine = mine + received.astype(F32)
     half = mine.astype(BF16)
     routes = [[(i, i ^ bits) for i in range(lax.axis_size("ctx"))] for bits in range(1, PLANE)]
     total = mine
@@ -783,7 +783,7 @@
     rows_proj = place_blocks(proj_blocks, 1)
     dt_blocks = line_blocks(dt_plane)
     part = lambda at: matmul(rows_proj, lax.dynamic_slice_in_dim(act, at * half, half), (1, 1))
-    mine, other = sum_plane(part(core), swap_mp(part(1 - core)))
+    mine, other = sum_plane(part(core), swap_mp(part(1 - core).astype(BF16)))
     rows_dt = place_blocks(dt_blocks, 0)
     step, sig, state, adjoint, bc = scan_local(
         here, mine, other, rows_dt, step_bias, act, grad_mixed, rates

time: 243 us -> 241 us (level)
  no operation moved by 1% of the time
where the time goes in v5:
time: 241 us; the launch traced here: 239 us
  Pallas kernels  87.7 us (36%)
  starting transfers between devices  65.4 us (27%)
  waiting for transfers between devices  43.2 us (18%)
  local copies, waits for them, and re-layouts  27.5 us (11%)
  other arithmetic  7.74 us (3%)
  matrix products  6.49 us (3%)
    pallas_call x1, Pallas kernels, scan_full(): pl.pallas_call(full_kernel, in_specs=[pl.BlockSpec(memory_space=pltpu.SME...  47.6 us
    ppermute x26, starting transfers between devices, send(): return lax.ppermute(x, 'ctx', route)  41.1 us
    ppermute x26, waiting for transfers between devices, send(): return lax.ppermute(x, 'ctx', route)  34.6 us
    pallas_call x1, Pallas kernels, scan_local(): pl.pallas_call(local_kernel, in_specs=[pl.BlockSpec(memory_space=pltpu.SM...  19.8 us
    all_to_all x4, starting transfers between devices, in_plane(): lax.all_to_all(x, 'ctx', 0, 0, axis_index_groups=plane_groups(), tiled=True)  19 us
    dynamic_update_slice x8, local copies, waits for them, and re-layouts, place_blocks(): lax.dynamic_update_slice(out, block, (at, 0) if axis == 0 else (0, at))  8.86 us
    pallas_call x1, Pallas kernels, conv_tail(): pl.pallas_call(tail_kernel, in_specs=[pl.BlockSpec(memory_space=pltpu.SME...  6.78 us
    unnamed x57, local copies, waits for them, and re-layouts  6.59 us
  transfers between devices with their start and end apart: 35, of which 15 were waited for; matrix products, arithmetic and copies ran while one was open for 10% of the time, Pallas kernels for 7%

profile of v5, /device:TPU:14, one launch (start us, length us, event | category | flops | bytes accessed | tf_op | source)
XLA Modules:
  0.0 239.3 jit_solution(3963895588408250898)
XLA Ops:
  8.4 2.6 %collective-permute-start.6 = (bf16[3,1024]{1,0:T(4,128)(2,1)S(1)}, bf16[3,1024]{1,0:T(4,128)(2,1)S(1)}, u32[]{:S(2)}, u32[]{:S(2)}) collective-permute-start(bf16[3,1024]{1,0:T(4,128)(2,1)S(1)} %bitcast.90), channel_id=1, source_target_pairs={{6,14},{14,22},{22,30},{7,15},{15,23},{23,31}} | collective-permute-start | bytes 18440 | tf_op jit(solution)/shard_map/ppermute | solution.py:379
  11.0 2.5 %pack.2 = bf16[4,160,1024]{2,1,0:T(8,128)(2,1)} custom-call(bf16[128,4096]{1,0:T(8,128)(2,1)} %refs_0_.1, bf16[32,4096]{1,0:T(8,128)(2,1)} %refs_1_.1), custom_call_target="tpu_custom_call" | custom-call | bytes 7200000 | tf_op jit(solution)/shard_map/pack/pallas_call | solution.py:469
  13.5 4.3 %all-to-all-start = ((bf16[4,160,1024]{2,1,0:T(8,128)(2,1)}), bf16[4,160,1024]{2,1,0:T(8,128)(2,1)S(1)}, u32[]{:S(2)}, u32[]{:S(2)}) async-start(bf16[4,160,1024]{2,1,0:T(8,128)(2,1)} %pack.2), calls=%async_computation | async-start | bytes 2621440 | tf_op jit(solution)/shard_map/all_to_all | solution.py:402
  19.7 6.9 %collective-permute-done.5 = bf16[3,1024]{1,0:T(4,128)(2,1)S(1)} collective-permute-done((bf16[3,1024]{1,0:T(4,128)(2,1)S(1)}, bf16[3,1024]{1,0:T(4,128)(2,1)S(1)}, u32[]{:S(2)}, u32[]{:S(2)}) %collective-permute-start.5) | collective-permute-done | bytes 6176 | tf_op jit(solution)/shard_map/ppermute | solution.py:379
  29.4 2.3 pack.3
  41.0 2.3 fusion.21
  49.6 4.5 %all-to-all-start.1 = ((bf16[4,128,1024]{2,1,0:T(8,128)(2,1)}), bf16[4,128,1024]{2,1,0:T(8,128)(2,1)S(1)}, u32[]{:S(2)}, u32[]{:S(2)}) async-start(bf16[4,128,1024]{2,1,0:T(8,128)(2,1)} %pack.3), calls=%async_computation.1 | async-start | bytes 2097152 | tf_op jit(solution)/shard_map/all_to_all | solution.py:402
  54.1 5.2 %collective-permute-done.9 = bf16[544,256]{1,0:T(8,128)(2,1)} collective-permute-done((bf16[544,256]{1,0:T(8,128)(2,1)}, bf16[544,256]{1,0:T(8,128)(2,1)}, u32[]{:S(2)}, u32[]{:S(2)}) %collective-permute-start.9) | collective-permute-done | bytes 278560 | tf_op jit(solution)/shard_map/ppermute | solution.py:379
  59.8 2.2 convert_add_fusion.2.mine
  77.0 19.8 %scan_local.1 = (f32[512,8,128]{2,1,0:T(8,128)}, f32[512,1024]{1,0:T(8,128)}, f32[17,1024]{1,0:T(8,128)}, f32[17,1024]{1,0:T(8,128)}, f32[32,512]{1,0:T(8,128)}) custom-call(s32[1]{0:T(128)} %bitcast.core, f32[544,256]{1,0:T(8,128)} %convert_add_fusion.2.mine, f32[544,256]{1,0:T(8,128)} %collective-permute-done.11.other, ...), custom_call_target="tpu_custom_call" | custom-call | bytes 79200000 | tf_op jit(solution)/shard_map/scan_local/pallas_call | solution.py:281
  97.8 3.2 %collective-permute-start.17 = (f32[17,1024]{1,0:T(8,128)S(1)}, f32[17,1024]{1,0:T(8,128)S(1)}, u32[]{:S(2)}, u32[]{:S(2)}) collective-permute-start(f32[17,1024]{1,0:T(8,128)S(1)} %get-tuple-element.66), channel_id=1, source_target_pairs={{0,24},{2,26},{4,28},{6,30},{8,0},{10,2},{12,4},{14,6},{16,8},{18,... | collective-permute-start | bytes 208904 | tf_op jit(solution)/shard_map/ppermute | solution.py:379
  109.7 47.6 %scan_full.1 = (bf16[512,1024]{1,0:T(8,128)(2,1)}, bf16[512,1024]{1,0:T(8,128)(2,1)}, f32[512,1024]{1,0:T(8,128)}, f32[16,1024]{1,0:T(8,128)}, f32[2,1024]{1,0:T...) custom-call(s32[1]{0:T(128)} %bitcast.core, f32[32,512]{1,0:T(8,128)} %get-tuple-element.41.bc, ...), custom_call_target="tpu_custom_call" | custom-call | bytes 183600000 | tf_op jit(solution)/shard_map/scan_full/pallas_call | solution.py:308
  157.3 2.9 %convolution_convert_fusion = bf16[512,1024]{1,0:T(8,128)(2,1)} fusion(bf16[512,1024]{1,0:T(8,128)(2,1)} %get-tuple-element.48, bf16[512,256]{1,0:T(8,128)(2,1)S(1)} %slice.110, bf16[512,256]{1,0:T(8,128)(2,1)S(1)} %slice.111, pred[]{:T(512)S(6)} %eq.9), kind=kOutput, calls=%fused_computation.7 | convolution fusion | flops 539754496 | bytes 2621441 | tf_op jit(solution)/shard_map/dot_general | solution.py:742
  160.3 5.2 %all-to-all-start.2 = ((bf16[4,128,1024]{2,1,0:T(8,128)(2,1)}), bf16[4,128,1024]{2,1,0:T(8,128)(2,1)S(1)}, u32[]{:S(2)}, u32[]{:S(2)}) async-start(bf16[4,128,1024]{2,1,0:T(8,128)(2,1)} %bitcast.73), calls=%async_computation.2 | async-start | bytes 2097152 | tf_op jit(solution)/shard_map/all_to_all | solution.py:462
  172.0 7.0 %collective-permute-done.21 = bf16[544,256]{1,0:T(8,128)(2,1)S(1)} collective-permute-done((bf16[544,256]{1,0:T(8,128)(2,1)S(1)}, bf16[544,256]{1,0:T(8,128)(2,1)S(1)}, u32[]{:S(2)}, u32[]{:S(2)}) %collective-permute-start.21) | collective-permute-done | bytes 278560 | tf_op jit(solution)/shard_map/ppermute | solution.py:379
  178.9 5.1 %collective-permute-done.20 = bf16[544,256]{1,0:T(8,128)(2,1)S(1)} collective-permute-done((bf16[544,256]{1,0:T(8,128)(2,1)S(1)}, bf16[544,256]{1,0:T(8,128)(2,1)S(1)}, u32[]{:S(2)}, u32[]{:S(2)}) %collective-permute-start.20) | collective-permute-done | bytes 278560 | tf_op jit(solution)/shard_map/ppermute | solution.py:379
  184.9 3.2 %all-to-all-done.2.dt_parts = bf16[4,128,1024]{2,1,0:T(8,128)(2,1)S(1)} async-done(((bf16[4,128,1024]{2,1,0:T(8,128)(2,1)}), bf16[4,128,1024]{2,1,0:T(8,128)(2,1)S(1)}, u32[]{:S(2)}, u32[]{:S(2)}) %all-to-all-start.2) | async-done | bytes 1048608 | tf_op jit(solution)/shard_map/all_to_all | solution.py:462
  188.1 5.8 %all-to-all-start.3 = ((bf16[4,128,1024]{2,1,0:T(8,128)(2,1)}), bf16[4,128,1024]{2,1,0:T(8,128)(2,1)}, u32[]{:S(2)}, u32[]{:S(2)}) async-start(bf16[4,128,1024]{2,1,0:T(8,128)(2,1)} %bitcast.72), calls=%async_computation.3 | async-start | bytes 2097152 | tf_op jit(solution)/shard_map/all_to_all | solution.py:402
  198.2 6.8 %conv_tail.1 = (bf16[4,160,1024]{2,1,0:T(8,128)(2,1)S(1)}, f32[5,1024]{1,0:T(8,128)S(1)}, f32[16,1024]{1,0:T(8,128)S(1)}) custom-call(s32[1]{0:T(128)} %bitcast.core, bf16[544,256]{1,0:T(8,128)(2,1)S(1)} %copy-done.3, bf16[544,256]{1,0:T(8,128)(2,1)S(1)} %collective-permute-done.22.other, ...), custom_call_target="tpu_custom_call" | custom-call | bytes 28800000 | tf_op jit(solution)/shard_map/conv_tail/pallas_call | solution.py:665
  206.7 4.4 %all-to-all-start.4 = ((bf16[4,160,1024]{2,1,0:T(8,128)(2,1)}), bf16[4,160,1024]{2,1,0:T(8,128)(2,1)}, u32[]{:S(2)}, u32[]{:S(2)}) async-start(bf16[4,160,1024]{2,1,0:T(8,128)(2,1)} %copy-done.2), calls=%async_computation.4 | async-start | bytes 2621440 | tf_op jit(solution)/shard_map/all_to_all | solution.py:402
  211.9 4.0 %gate_gradient.1 = bf16[128,4096]{1,0:T(8,128)(2,1)} custom-call(bf16[4,128,1024]{2,1,0:T(8,128)(2,1)} %all-to-all-done.3.x, bf16[128,4096]{1,0:T(8,128)(2,1)} %gate.1, bf16[128,4096]{1,0:T(8,128)(2,1)} %up.1, f32[128,1]{1,0:T(8,128)} %copy.32.flags), custom_call_target="tpu_custom_call" | custom-call | bytes 14400000 | tf_op jit(solution)/shard_map/gate_gradient/pallas_call | solution.py:449
  217.8 4.2 %collective-permute-start.28 = (f32[23,256]{1,0:T(8,128)S(1)}, f32[23,256]{1,0:T(8,128)S(1)}, u32[]{:S(2)}, u32[]{:S(2)}) collective-permute-start(f32[23,256]{1,0:T(8,128)S(1)} %bitcast.81), channel_id=1, source_target_pairs={{0,16},{2,18},{4,20},{6,22},{8,24},{10,26},{12,28},{14,30},{16,0},... | collective-permute-start | bytes 70664 | tf_op jit(solution)/shard_map/ppermute | solution.py:379
  222.0 3.4 %collective-permute-start.26 = (f32[16,1024]{1,0:T(8,128)S(1)}, f32[16,1024]{1,0:T(8,128)S(1)}, u32[]{:S(2)}, u32[]{:S(2)}) collective-permute-start(f32[16,1024]{1,0:T(8,128)S(1)} %copy-done.5), channel_id=1, source_target_pairs={{14,6},{22,14},{30,22},{15,7},{23,15},{31,23}} | collective-permute-start | bytes 196616 | tf_op jit(solution)/shard_map/ppermute | solution.py:379
  236.6 2.7 %unpack.1 = (bf16[128,4096]{1,0:T(8,128)(2,1)}, f32[32,4096]{1,0:T(8,128)}) custom-call(bf16[4,160,1024]{2,1,0:T(8,128)(2,1)} %all-to-all-done.4.x, f32[16,1024]{1,0:T(8,128)} %copy-done.16, f32[16,1024]{1,0:T(8,128)} %copy-done.15, f32[16,1024]{1,0:T(8,128)} %copy-done.14, f32[16,1024]{1,0:T(8,128)} %copy-done.13), custom_call_target="tpu_custom_call" | custom-call | bytes 7200000 | tf_op jit(solution)/shard_map/unpack/pallas_call | solution.py:482
  (161 shorter events, 79.9 us)
Async XLA Ops:
  0.6 33.9 %collective-permute-start.2 = (bf16[544,256]{1,0:T(8,128)(2,1)}, bf16[544,256]{1,0:T(8,128)(2,1)}, u32[]{:S(2)}, u32[]{:S(2)}) collective-permute-start(bf16[544,256]{1,0:T(8,128)(2,1)} %bitcast.74), channel_id=1, source_target_pairs={{0,8},{2,10},{4,12},{6,14},{8,16},{10,18},{12,20},{14,22},{16,24},... | collective-permute-start | bytes 835592 | tf_op jit(solution)/shard_map/ppermute | solution.py:379
  2.3 32.3 %collective-permute-start.1 = (bf16[544,256]{1,0:T(8,128)(2,1)}, bf16[544,256]{1,0:T(8,128)(2,1)}, u32[]{:S(2)}, u32[]{:S(2)}) collective-permute-start(bf16[544,256]{1,0:T(8,128)(2,1)} %bitcast.75), channel_id=1, source_target_pairs={{0,16},{2,18},{4,20},{6,22},{8,24},{10,26},{12,28},{14,30},{16,0},... | collective-permute-start | bytes 835592 | tf_op jit(solution)/shard_map/ppermute | solution.py:379
  3.5 31.1 %collective-permute-start = (bf16[544,256]{1,0:T(8,128)(2,1)}, bf16[544,256]{1,0:T(8,128)(2,1)}, u32[]{:S(2)}, u32[]{:S(2)}) collective-permute-start(bf16[544,256]{1,0:T(8,128)(2,1)} %bitcast.76), channel_id=1, source_target_pairs={{0,24},{2,26},{4,28},{6,30},{8,0},{10,2},{12,4},{14,6},{16,8},{18,... | collective-permute-start | bytes 835592 | tf_op jit(solution)/shard_map/ppermute | solution.py:379
  6.3 20.3 %collective-permute-start.5 = (bf16[3,1024]{1,0:T(4,128)(2,1)S(1)}, bf16[3,1024]{1,0:T(4,128)(2,1)S(1)}, u32[]{:S(2)}, u32[]{:S(2)}) collective-permute-start(bf16[3,1024]{1,0:T(4,128)(2,1)S(1)} %bitcast.91), channel_id=1, source_target_pairs={{6,12},{14,20},{22,28},{7,13},{15,21},{23,29}} | collective-permute-start | bytes 18440 | tf_op jit(solution)/shard_map/ppermute | solution.py:379
  8.4 19.5 %collective-permute-start.6 = (bf16[3,1024]{1,0:T(4,128)(2,1)S(1)}, bf16[3,1024]{1,0:T(4,128)(2,1)S(1)}, u32[]{:S(2)}, u32[]{:S(2)}) collective-permute-start(bf16[3,1024]{1,0:T(4,128)(2,1)S(1)} %bitcast.90), channel_id=1, source_target_pairs={{6,14},{14,22},{22,30},{7,15},{15,23},{23,31}} | collective-permute-start | bytes 18440 | tf_op jit(solution)/shard_map/ppermute | solution.py:379
  13.5 18.3 %all-to-all-start = ((bf16[4,160,1024]{2,1,0:T(8,128)(2,1)}), bf16[4,160,1024]{2,1,0:T(8,128)(2,1)S(1)}, u32[]{:S(2)}, u32[]{:S(2)}) async-start(bf16[4,160,1024]{2,1,0:T(8,128)(2,1)} %pack.2), calls=%async_computation | async-start | bytes 2621440 | tf_op jit(solution)/shard_map/all_to_all | solution.py:402
  43.4 10.8 %collective-permute-start.10 = (bf16[544,256]{1,0:T(8,128)(2,1)}, bf16[544,256]{1,0:T(8,128)(2,1)}, u32[]{:S(2)}, u32[]{:S(2)}) collective-permute-start(bf16[544,256]{1,0:T(8,128)(2,1)} %get-tuple-element.80), channel_id=1, source_target_pairs={{0,6},{2,4},{4,2},{6,0},{8,14},{10,12},{12,10},{14,8},{16,22},{18,... | collective-permute-start | bytes 835592 | tf_op jit(solution)/shard_map/ppermute | solution.py:379
  44.6 14.8 %collective-permute-start.9 = (bf16[544,256]{1,0:T(8,128)(2,1)}, bf16[544,256]{1,0:T(8,128)(2,1)}, u32[]{:S(2)}, u32[]{:S(2)}) collective-permute-start(bf16[544,256]{1,0:T(8,128)(2,1)} %get-tuple-element.80), channel_id=1, source_target_pairs={{0,4},{2,6},{4,0},{6,2},{8,12},{10,14},{12,8},{14,10},{16,20},{18,... | collective-permute-start | bytes 835592 | tf_op jit(solution)/shard_map/ppermute | solution.py:379
  46.3 13.6 %collective-permute-start.8 = (bf16[544,256]{1,0:T(8,128)(2,1)}, bf16[544,256]{1,0:T(8,128)(2,1)}, u32[]{:S(2)}, u32[]{:S(2)}) collective-permute-start(bf16[544,256]{1,0:T(8,128)(2,1)} %get-tuple-element.80), channel_id=1, source_target_pairs={{0,2},{2,0},{4,6},{6,4},{8,10},{10,8},{12,14},{14,12},{16,18},{18,... | collective-permute-start | bytes 835592 | tf_op jit(solution)/shard_map/ppermute | solution.py:379
  46.9 25.2 %collective-permute-start.13 = (bf16[128,1024]{1,0:T(8,128)(2,1)}, bf16[128,1024]{1,0:T(8,128)(2,1)}, u32[]{:S(2)}, u32[]{:S(2)}) collective-permute-start(bf16[128,1024]{1,0:T(8,128)(2,1)} %bitcast.68), channel_id=1, source_target_pairs={{0,16},{2,18},{4,20},{6,22},{8,24},{10,26},{12,28},{14,30},{16,0},... | collective-permute-start | bytes 786440 | tf_op jit(solution)/shard_map/ppermute | solution.py:379
  48.1 22.3 %collective-permute-start.12 = (bf16[128,1024]{1,0:T(8,128)(2,1)}, bf16[128,1024]{1,0:T(8,128)(2,1)}, u32[]{:S(2)}, u32[]{:S(2)}) collective-permute-start(bf16[128,1024]{1,0:T(8,128)(2,1)} %bitcast.69), channel_id=1, source_target_pairs={{0,24},{2,26},{4,28},{6,30},{8,0},{10,2},{12,4},{14,6},{16,8},{18,... | collective-permute-start | bytes 786440 | tf_op jit(solution)/shard_map/ppermute | solution.py:379
  49.6 26.3 %all-to-all-start.1 = ((bf16[4,128,1024]{2,1,0:T(8,128)(2,1)}), bf16[4,128,1024]{2,1,0:T(8,128)(2,1)S(1)}, u32[]{:S(2)}, u32[]{:S(2)}) async-start(bf16[4,128,1024]{2,1,0:T(8,128)(2,1)} %pack.3), calls=%async_computation.1 | async-start | bytes 2097152 | tf_op jit(solution)/shard_map/all_to_all | solution.py:402
  62.1 13.9 %collective-permute-start.11 = (f32[544,256]{1,0:T(8,128)}, f32[544,256]{1,0:T(8,128)}, u32[]{:S(2)}, u32[]{:S(2)}) collective-permute-start(f32[544,256]{1,0:T(8,128)} %convert_add_fusion.2.mine), channel_id=1, source_target_pairs={{0,1},{1,0},{2,3},{3,2},{4,5},{5,4},{6,7},{7,6},{8,9},{9,8},{10,11... | collective-permute-start | bytes 1671176 | tf_op jit(solution)/shard_map/ppermute | solution.py:393
  66.3 8.9 %collective-permute-start.14 = (bf16[128,1024]{1,0:T(8,128)(2,1)}, bf16[128,1024]{1,0:T(8,128)(2,1)S(1)}, u32[]{:S(2)}, u32[]{:S(2)}) collective-permute-start(bf16[128,1024]{1,0:T(8,128)(2,1)} %bitcast.70), channel_id=1, source_target_pairs={{0,8},{2,10},{4,12},{6,14},{8,16},{10,18},{12,20},{14,22},{16,24},... | collective-permute-start | bytes 786440 | tf_op jit(solution)/shard_map/ppermute | solution.py:379
  101.0 8.0 %collective-permute-start.15 = (f32[17,1024]{1,0:T(8,128)S(1)}, f32[17,1024]{1,0:T(8,128)S(1)}, u32[]{:S(2)}, u32[]{:S(2)}) collective-permute-start(f32[17,1024]{1,0:T(8,128)S(1)} %get-tuple-element.68), channel_id=1, source_target_pairs={{0,8},{2,10},{4,12},{6,14},{8,16},{10,18},{12,20},{14,22},{16,24},... | collective-permute-start | bytes 208904 | tf_op jit(solution)/shard_map/ppermute | solution.py:379
  160.3 27.8 %all-to-all-start.2 = ((bf16[4,128,1024]{2,1,0:T(8,128)(2,1)}), bf16[4,128,1024]{2,1,0:T(8,128)(2,1)S(1)}, u32[]{:S(2)}, u32[]{:S(2)}) async-start(bf16[4,128,1024]{2,1,0:T(8,128)(2,1)} %bitcast.73), calls=%async_computation.2 | async-start | bytes 2097152 | tf_op jit(solution)/shard_map/all_to_all | solution.py:462
  168.4 10.5 %collective-permute-start.21 = (bf16[544,256]{1,0:T(8,128)(2,1)S(1)}, bf16[544,256]{1,0:T(8,128)(2,1)S(1)}, u32[]{:S(2)}, u32[]{:S(2)}) collective-permute-start(bf16[544,256]{1,0:T(8,128)(2,1)S(1)} %fusion.13), channel_id=1, source_target_pairs={{0,6},{2,4},{4,2},{6,0},{8,14},{10,12},{12,10},{14,8},{16,22},{18,... | collective-permute-start | bytes 835592 | tf_op jit(solution)/shard_map/ppermute | solution.py:379
  170.0 14.0 %collective-permute-start.20 = (bf16[544,256]{1,0:T(8,128)(2,1)S(1)}, bf16[544,256]{1,0:T(8,128)(2,1)S(1)}, u32[]{:S(2)}, u32[]{:S(2)}) collective-permute-start(bf16[544,256]{1,0:T(8,128)(2,1)S(1)} %fusion.13), channel_id=1, source_target_pairs={{0,4},{2,6},{4,0},{6,2},{8,12},{10,14},{12,8},{14,10},{16,20},{18,... | collective-permute-start | bytes 835592 | tf_op jit(solution)/shard_map/ppermute | solution.py:379
  171.5 12.5 %collective-permute-start.19 = (bf16[544,256]{1,0:T(8,128)(2,1)S(1)}, bf16[544,256]{1,0:T(8,128)(2,1)S(1)}, u32[]{:S(2)}, u32[]{:S(2)}) collective-permute-start(bf16[544,256]{1,0:T(8,128)(2,1)S(1)} %fusion.13), channel_id=1, source_target_pairs={{0,2},{2,0},{4,6},{6,4},{8,10},{10,8},{12,14},{14,12},{16,18},{18,... | collective-permute-start | bytes 835592 | tf_op jit(solution)/shard_map/ppermute | solution.py:379
  188.1 18.6 %all-to-all-start.3 = ((bf16[4,128,1024]{2,1,0:T(8,128)(2,1)}), bf16[4,128,1024]{2,1,0:T(8,128)(2,1)}, u32[]{:S(2)}, u32[]{:S(2)}) async-start(bf16[4,128,1024]{2,1,0:T(8,128)(2,1)} %bitcast.72), calls=%async_computation.3 | async-start | bytes 2097152 | tf_op jit(solution)/shard_map/all_to_all | solution.py:402
  206.7 29.3 %all-to-all-start.4 = ((bf16[4,160,1024]{2,1,0:T(8,128)(2,1)}), bf16[4,160,1024]{2,1,0:T(8,128)(2,1)}, u32[]{:S(2)}, u32[]{:S(2)}) async-start(bf16[4,160,1024]{2,1,0:T(8,128)(2,1)} %copy-done.2), calls=%async_computation.4 | async-start | bytes 2621440 | tf_op jit(solution)/shard_map/all_to_all | solution.py:402
  216.1 10.6 %collective-permute-start.27 = (f32[23,256]{1,0:T(8,128)S(1)}, f32[23,256]{1,0:T(8,128)S(1)}, u32[]{:S(2)}, u32[]{:S(2)}) collective-permute-start(f32[23,256]{1,0:T(8,128)S(1)} %bitcast.82), channel_id=1, source_target_pairs={{0,8},{2,10},{4,12},{6,14},{8,16},{10,18},{12,20},{14,22},{16,24},... | collective-permute-start | bytes 70664 | tf_op jit(solution)/shard_map/ppermute | solution.py:379
  217.8 10.2 %collective-permute-start.28 = (f32[23,256]{1,0:T(8,128)S(1)}, f32[23,256]{1,0:T(8,128)S(1)}, u32[]{:S(2)}, u32[]{:S(2)}) collective-permute-start(f32[23,256]{1,0:T(8,128)S(1)} %bitcast.81), channel_id=1, source_target_pairs={{0,16},{2,18},{4,20},{6,22},{8,24},{10,26},{12,28},{14,30},{16,0},... | collective-permute-start | bytes 70664 | tf_op jit(solution)/shard_map/ppermute | solution.py:379
  222.0 9.1 %collective-permute-start.26 = (f32[16,1024]{1,0:T(8,128)S(1)}, f32[16,1024]{1,0:T(8,128)S(1)}, u32[]{:S(2)}, u32[]{:S(2)}) collective-permute-start(f32[16,1024]{1,0:T(8,128)S(1)} %copy-done.5), channel_id=1, source_target_pairs={{14,6},{22,14},{30,22},{15,7},{23,15},{31,23}} | collective-permute-start | bytes 196616 | tf_op jit(solution)/shard_map/ppermute | solution.py:379
  (34 other events, 174.2 us)
